TPU v7x, 256 devices: a whole 4x4x8 slice. The times are simulated.
256 devices in a mesh: region: 32 (over z, y), sub: 8 (over x, core).
Axes of the slice: x: 4, y: 4, z: 8, core: 2. Of those that a mesh axis runs over, the one named last changes fastest.
Arguments:
- rhs: float32 [4096, 8, 768], P(('region', 'sub')), may hold values from -6 to 6
- diag_inv: bfloat16 [4096, 8, 8, 768], P(('region', 'sub'))
- coupling: bfloat16 [4096, 4, 8, 8, 768], P(('region', 'sub')), may hold values from -0.59765625 to 0.59765625
- neighbours: int32 [4096, 4], P(('region', 'sub')), may hold values from 0 to 47
- send_tiles: int32 [256, 8], P(('region', 'sub')), may hold values from 0 to 15, as said below
- tile_count: int32 [256], P(('region', 'sub')), may hold values from 1 to 16
- hessian: bfloat16 [4096, 6, 6, 768], P(('region', 'sub')), may hold values from -6 to 6
- shared_vertex: int32 [262144], P(('region', 'sub')), may hold values from 0 to 12287
- owner_region: int32 [262144, 1], P(('region', 'sub')), may hold values from 0 to 31; in each aligned block of 1024 rows (0 to 1023, 1024 to 2047, ...) at most 128 rows name the same one
- owner_slot: int32 [262144], P(('region', 'sub')), may hold values from 0 to 1023
Outputs:
- adjoint: float32 [4096, 8, 768], P(('region', 'sub'))
- metric: float32 [4096, 6, 768], P(('region', 'sub'))
- owned_metric: float32 [6, 262144], P(None, ('region', 'sub'))
Inputs may be any that keep to these rules, and one draw needn't show every extreme that they name: `send_tiles`: within one device the 8 entries are distinct. `owner_region`: among the 1024 entries of one device no partition is named more than 128 times.
All inputs are finite; a program needn't handle non-finite values.
Results may differ from a plain program's by a relative error of at most 0.00055.
Values sent between devices are 32-bit elements; how exact they have to be, the bound alone decides.
No kernel may reach another device: no remote copies, remote signals or barrier semaphores. Data moves between devices by JAX's collectives and lax.ppermute only.
A program may use at most 128 MiB of HBM per device.

v0:
```python
import jax
import jax.numpy as jnp
from jax import lax
from jax.sharding import PartitionSpec as P

NVAR = 6
SWEEPS = 3
OWNED = 1024


def with_halo(shard, sides, width):
    for axis, dim in sides:
        peers, length = (lax.axis_size(axis), shard.shape[dim])
        up = [(i, (i + 1) % peers) for i in range(peers - 1)]
        down = [(j, i) for i, j in up]
        last = lax.slice_in_dim(shard, length - width, length, axis=dim)
        leading = lax.slice_in_dim(shard, 0, width, axis=dim)
        before = lax.ppermute(last, axis, up)
        after = lax.ppermute(leading, axis, down)
        shard = jnp.concatenate([before, shard, after], axis=dim)
    return shard


def solve_blocks(inv, resid, live):
    out = jnp.einsum("tjiv,tjv->tiv", inv, resid, preferred_element_type=jnp.float32)
    rows = (lax.iota(jnp.int32, inv.shape[1]) < NVAR).astype(jnp.float32)
    return out * live[:, None, None] * rows[None, :, None]


def per_device(
    rhs,
    diag_inv,
    coupling,
    neighbours,
    send_tiles,
    tile_count,
    hessian,
    shared_vertex,
    owner_region,
    owner_slot,
):
    tiles = rhs.shape[0]
    live = (lax.iota(jnp.int32, tiles) < tile_count[0]).astype(jnp.float32)
    adjoint = solve_blocks(diag_inv, rhs, live)
    listed = send_tiles[0]
    for sweep in range(SWEEPS):
        sent = adjoint[listed]
        beside_all = with_halo(sent[None, None], (("region", 0), ("sub", 1)), 1)
        extended = jnp.concatenate(
            [adjoint, beside_all[0, 1], beside_all[2, 1], beside_all[1, 0], beside_all[1, 2]],
            axis=0,
        )
        near = extended[neighbours]
        pull = jnp.einsum("tkmjv,tkmv->tjv", coupling, near, preferred_element_type=jnp.float32)
        adjoint = solve_blocks(diag_inv, rhs - pull, live)
    metric = jnp.einsum(
        "tcv,tcsv->tsv", jnp.abs(adjoint[:, :NVAR]), hessian, preferred_element_type=jnp.float32
    )
    flat = metric.transpose(1, 0, 2).reshape(6, tiles * rhs.shape[2])
    values = flat[:, shared_vertex]
    dest = owner_region[:, 0]
    regions = lax.axis_size("region")
    target = dest * OWNED + owner_slot
    dense = jax.ops.segment_sum(values.T, target, num_segments=regions * OWNED)
    dense = dense.reshape(regions, OWNED, 6).transpose(0, 2, 1)
    owned = lax.psum_scatter(dense, "region", scatter_dimension=0, tiled=True)[0]
    return (adjoint, metric, owned)


def solution(mesh):
    placed = (
        P(("region", "sub"), None, None),
        P(("region", "sub"), None, None, None),
        P(("region", "sub"), None, None, None, None),
        P(("region", "sub"), None),
        P(("region", "sub"), None),
        P(("region", "sub")),
        P(("region", "sub"), None, None, None),
        P(("region", "sub")),
        P(("region", "sub"), None),
        P(("region", "sub")),
    )
    return jax.shard_map(
        per_device,
        mesh=mesh,
        in_specs=placed,
        out_specs=(
            P(("region", "sub"), None, None),
            P(("region", "sub"), None, None),
            P(None, ("region", "sub")),
        ),
        check_vma=False,
    )
```

profile of v0, /device:TPU:1, one launch (start us, length us, event | category | flops | bytes accessed | tf_op | source)
XLA Modules:
  0.0 308.5 jit_solution(4352201580217266702)
XLA Ops:
  8.6 1.9 fusion.5
  11.8 4.0 %collective-permute-start = (f32[1,1,8,8,768]{4,3,2,1,0:T(8,128)S(1)}, f32[1,1,8,8,768]{4,3,2,1,0:T(8,128)S(1)}, u32[]{:S(2)}, u32[]{:S(2)}) collective-permute-start(f32[1,1,8,8,768]{4,3,2,1,0:T(8,128)S(1)} %bitcast.124), channel_id=1, source_target_pairs={{0,8},{8,16},{16,24},{24,32},{32,40},{40,48},{48,56},{56,64},{64,7... | collective-permute-start | bytes 589832 | tf_op jit(solution)/shard_map/ppermute | solution.py:18
  15.8 1.3 collective-permute-start.1
  17.1 2.2 collective-permute-done
  19.4 3.8 %collective-permute-done.1 = f32[1,1,8,8,768]{4,3,2,1,0:T(8,128)S(1)} collective-permute-done((f32[1,1,8,8,768]{4,3,2,1,0:T(8,128)S(1)}, f32[1,1,8,8,768]{4,3,2,1,0:T(8,128)S(1)}, u32[]{:S(2)}, u32[]{:S(2)}) %collective-permute-start.1) | collective-permute-done | bytes 196640 | tf_op jit(solution)/shard_map/ppermute | solution.py:19
  23.2 4.9 %collective-permute-start.2 = (f32[3,1,8,8,768]{4,3,2,1,0:T(8,128)S(1)}, f32[3,1,8,8,768]{4,3,2,1,0:T(8,128)S(1)}, u32[]{:S(2)}, u32[]{:S(2)}) collective-permute-start(f32[3,1,8,8,768]{4,3,2,1,0:T(8,128)S(1)} %pad_maximum_fusion), channel_id=1, source_target_pairs={{0,1},{1,2},{2,3},{3,4},{4,5},{5,6},{6,7},{8,9},{9,10},{10,11},{11... | collective-permute-start | bytes 1769480 | tf_op jit(solution)/shard_map/ppermute | solution.py:18
  28.3 1.9 collective-permute-start.3
  30.3 4.6 %collective-permute-done.2 = f32[3,1,8,8,768]{4,3,2,1,0:T(8,128)S(1)} collective-permute-done((f32[3,1,8,8,768]{4,3,2,1,0:T(8,128)S(1)}, f32[3,1,8,8,768]{4,3,2,1,0:T(8,128)S(1)}, u32[]{:S(2)}, u32[]{:S(2)}) %collective-permute-start.2) | collective-permute-done | bytes 589856 | tf_op jit(solution)/shard_map/ppermute | solution.py:18
  34.9 4.6 %collective-permute-done.3 = f32[3,1,8,8,768]{4,3,2,1,0:T(8,128)S(1)} collective-permute-done((f32[3,1,8,8,768]{4,3,2,1,0:T(8,128)S(1)}, f32[3,1,8,8,768]{4,3,2,1,0:T(8,128)S(1)}, u32[]{:S(2)}, u32[]{:S(2)}) %collective-permute-start.3) | collective-permute-done | bytes 589856 | tf_op jit(solution)/shard_map/ppermute | solution.py:19
  40.3 4.4 %fusion = f32[16,768,8]{1,2,0:T(8,128)S(1)} fusion(f32[16,768,4,8]{1,3,2,0:T(8,128)S(1)} %bitcast.116, bf16[16,4,8,8,768]{4,3,2,1,0:T(8,128)(2,1)} %param.12), kind=kLoop, calls=%fused_computation.11 | loop fusion | flops 9338880 | bytes 8257536 | tf_op jit(solution)/shard_map/tkmjv,tkmv->tjv/dot_general | solution.py:54
  46.5 3.2 %collective-permute-start.4 = (f32[1,1,8,8,768]{4,3,2,1,0:T(8,128)S(1)}, f32[1,1,8,8,768]{4,3,2,1,0:T(8,128)S(1)}, u32[]{:S(2)}, u32[]{:S(2)}) collective-permute-start(f32[1,1,8,8,768]{4,3,2,1,0:T(8,128)S(1)} %bitcast.127), channel_id=1, source_target_pairs={{0,8},{8,16},{16,24},{24,32},{32,40},{40,48},{48,56},{56,64},{64,7... | collective-permute-start | bytes 589832 | tf_op jit(solution)/shard_map/ppermute | solution.py:18
  49.7 1.3 collective-permute-start.5
  52.3 3.8 %collective-permute-done.5 = f32[1,1,8,8,768]{4,3,2,1,0:T(8,128)S(1)} collective-permute-done((f32[1,1,8,8,768]{4,3,2,1,0:T(8,128)S(1)}, f32[1,1,8,8,768]{4,3,2,1,0:T(8,128)S(1)}, u32[]{:S(2)}, u32[]{:S(2)}) %collective-permute-start.5) | collective-permute-done | bytes 196640 | tf_op jit(solution)/shard_map/ppermute | solution.py:19
  56.2 4.8 %collective-permute-start.6 = (f32[3,1,8,8,768]{4,3,2,1,0:T(8,128)S(1)}, f32[3,1,8,8,768]{4,3,2,1,0:T(8,128)S(1)}, u32[]{:S(2)}, u32[]{:S(2)}) collective-permute-start(f32[3,1,8,8,768]{4,3,2,1,0:T(8,128)S(1)} %pad_maximum_fusion.1), channel_id=1, source_target_pairs={{0,1},{1,2},{2,3},{3,4},{4,5},{5,6},{6,7},{8,9},{9,10},{10,11},{11... | collective-permute-start | bytes 1769480 | tf_op jit(solution)/shard_map/ppermute | solution.py:18
  61.0 1.9 collective-permute-start.7
  64.3 3.5 %collective-permute-done.6 = f32[3,1,8,8,768]{4,3,2,1,0:T(8,128)S(1)} collective-permute-done((f32[3,1,8,8,768]{4,3,2,1,0:T(8,128)S(1)}, f32[3,1,8,8,768]{4,3,2,1,0:T(8,128)S(1)}, u32[]{:S(2)}, u32[]{:S(2)}) %collective-permute-start.6) | collective-permute-done | bytes 589856 | tf_op jit(solution)/shard_map/ppermute | solution.py:18
  68.5 3.7 %collective-permute-done.7 = f32[3,1,8,8,768]{4,3,2,1,0:T(8,128)S(1)} collective-permute-done((f32[3,1,8,8,768]{4,3,2,1,0:T(8,128)S(1)}, f32[3,1,8,8,768]{4,3,2,1,0:T(8,128)S(1)}, u32[]{:S(2)}, u32[]{:S(2)}) %collective-permute-start.7) | collective-permute-done | bytes 589856 | tf_op jit(solution)/shard_map/ppermute | solution.py:19
  72.9 1.9 gather_fusion.3
  74.8 4.3 %fusion.1 = f32[16,768,8]{1,2,0:T(8,128)S(1)} fusion(f32[16,768,4,8]{1,3,2,0:T(8,128)S(1)} %bitcast.117, bf16[16,4,8,8,768]{4,3,2,1,0:T(8,128)(2,1)} %param.12), kind=kLoop, calls=%fused_computation.12 | loop fusion | flops 9338880 | bytes 8257536 | tf_op jit(solution)/shard_map/tkmjv,tkmv->tjv/dot_general | solution.py:54
  80.9 4.3 %collective-permute-start.8 = (f32[1,1,8,8,768]{4,3,2,1,0:T(8,128)S(1)}, f32[1,1,8,8,768]{4,3,2,1,0:T(8,128)S(1)}, u32[]{:S(2)}, u32[]{:S(2)}) collective-permute-start(f32[1,1,8,8,768]{4,3,2,1,0:T(8,128)S(1)} %bitcast.121), channel_id=1, source_target_pairs={{0,8},{8,16},{16,24},{24,32},{32,40},{40,48},{48,56},{56,64},{64,7... | collective-permute-start | bytes 589832 | tf_op jit(solution)/shard_map/ppermute | solution.py:18
  87.8 4.4 %collective-permute-done.9 = f32[1,1,8,8,768]{4,3,2,1,0:T(8,128)S(1)} collective-permute-done((f32[1,1,8,8,768]{4,3,2,1,0:T(8,128)S(1)}, f32[1,1,8,8,768]{4,3,2,1,0:T(8,128)S(1)}, u32[]{:S(2)}, u32[]{:S(2)}) %collective-permute-start.9) | collective-permute-done | bytes 196640 | tf_op jit(solution)/shard_map/ppermute | solution.py:19
  92.3 4.0 %collective-permute-start.10 = (f32[3,1,8,8,768]{4,3,2,1,0:T(8,128)S(1)}, f32[3,1,8,8,768]{4,3,2,1,0:T(8,128)S(1)}, u32[]{:S(2)}, u32[]{:S(2)}) collective-permute-start(f32[3,1,8,8,768]{4,3,2,1,0:T(8,128)S(1)} %pad_maximum_fusion.2), channel_id=1, source_target_pairs={{0,1},{1,2},{2,3},{3,4},{4,5},{5,6},{6,7},{8,9},{9,10},{10,11},{11... | collective-permute-start | bytes 1769480 | tf_op jit(solution)/shard_map/ppermute | solution.py:18
  96.3 2.1 collective-permute-start.11
  99.8 3.3 %collective-permute-done.10 = f32[3,1,8,8,768]{4,3,2,1,0:T(8,128)S(1)} collective-permute-done((f32[3,1,8,8,768]{4,3,2,1,0:T(8,128)S(1)}, f32[3,1,8,8,768]{4,3,2,1,0:T(8,128)S(1)}, u32[]{:S(2)}, u32[]{:S(2)}) %collective-permute-start.10) | collective-permute-done | bytes 589856 | tf_op jit(solution)/shard_map/ppermute | solution.py:18
  103.7 3.8 %collective-permute-done.11 = f32[3,1,8,8,768]{4,3,2,1,0:T(8,128)S(1)} collective-permute-done((f32[3,1,8,8,768]{4,3,2,1,0:T(8,128)S(1)}, f32[3,1,8,8,768]{4,3,2,1,0:T(8,128)S(1)}, u32[]{:S(2)}, u32[]{:S(2)}) %collective-permute-start.11) | collective-permute-done | bytes 589856 | tf_op jit(solution)/shard_map/ppermute | solution.py:19
  108.2 1.9 gather_fusion.5
  110.1 4.3 %fusion.2 = f32[16,768,8]{1,2,0:T(8,128)S(1)} fusion(f32[16,768,4,8]{1,3,2,0:T(8,128)S(1)} %bitcast.115, bf16[16,4,8,8,768]{4,3,2,1,0:T(8,128)(2,1)} %param.12), kind=kLoop, calls=%fused_computation.13 | loop fusion | flops 9338880 | bytes 8257536 | tf_op jit(solution)/shard_map/tkmjv,tkmv->tjv/dot_general | solution.py:54
  116.3 4.1 %copy.21 = f32[6,16,768]{0,2,1:T(8,128)} copy(f32[6,16,768]{2,1,0:T(8,128)S(1)} %bitcast.119) | data formatting | bytes 589824 | tf_op jit(solution)/shard_map/transpose;tcv,tcsv->tsv/transpose | solution.py:59
  120.4 18.7 %scatter_custom_fusion = f32[32768,6]{1,0:T(8,128)} fusion(s32[1024]{0:T(1024)S(1)} %add.32, f32[]{:T(128)} %constant.2.clone.1, f32[6,12288]{0,1:T(8,128)} %bitcast.113, s32[1024]{0:T(1024)} %get-tuple-element.9), kind=kCustom, calls=%fused_computation.14 | custom fusion | flops 6144 | bytes 786944 | tf_op jit(solution)/shard_map/scatter-add | solution.py:64
  139.0 10.8 %copy.79 = f32[32,1024,6]{1,0,2:T(8,128)} copy(f32[32,1024,6]{2,1,0:T(8,128)} %bitcast.112) | data formatting | bytes 1572864 | tf_op jit(solution)/shard_map/reshape | solution.py:65
  150.5 148.9 %all-reduce.3.cloned.1.call-done = f32[32,6,1024]{2,0,1:T(8,128)} async-done(((f32[32,6,1024]{2,0,1:T(8,128)}), f32[32,6,1024]{2,0,1:T(8,128)}) %all-reduce.3.cloned.1.call-update) | async-done | bytes 786448
  299.4 1.6 constant_dynamic-slice_fusion
  (69 shorter events, 19.1 us)
Async XLA Ops:
  7.2 3.3 %copy-start.5 = (s32[1024]{0:T(1024)S(1)}, s32[1024]{0:T(1024)}, u32[]{:S(2)}) copy-start(s32[1024]{0:T(1024)} %param.17) | copy-start | bytes 12292
  7.2 292.2 %all-reduce.3.cloned.1.call-start = ((), (), s32[]{:S(2)}) async-start(), calls=%async_computation | async-start | bytes 1572864
  10.5 17.6 %copy-start.8 = (s32[16,4]{0,1:T(4,128)S(1)}, s32[16,4]{0,1:T(4,128)}, u32[]{:S(2)}) copy-start(s32[16,4]{0,1:T(4,128)} %param.13) | copy-start | bytes 772
  11.8 7.6 %collective-permute-start = (f32[1,1,8,8,768]{4,3,2,1,0:T(8,128)S(1)}, f32[1,1,8,8,768]{4,3,2,1,0:T(8,128)S(1)}, u32[]{:S(2)}, u32[]{:S(2)}) collective-permute-start(f32[1,1,8,8,768]{4,3,2,1,0:T(8,128)S(1)} %bitcast.124), channel_id=1, source_target_pairs={{0,8},{8,16},{16,24},{24,32},{32,40},{40,48},{48,56},{56,64},{64,7... | collective-permute-start | bytes 589832 | tf_op jit(solution)/shard_map/ppermute | solution.py:18
  15.8 7.3 %collective-permute-start.1 = (f32[1,1,8,8,768]{4,3,2,1,0:T(8,128)S(1)}, f32[1,1,8,8,768]{4,3,2,1,0:T(8,128)S(1)}, u32[]{:S(2)}, u32[]{:S(2)}) collective-permute-start(f32[1,1,8,8,768]{4,3,2,1,0:T(8,128)S(1)} %bitcast.125), channel_id=1, source_target_pairs={{8,0},{16,8},{24,16},{32,24},{40,32},{48,40},{56,48},{64,56},{72,6... | collective-permute-start | bytes 589832 | tf_op jit(solution)/shard_map/ppermute | solution.py:19
  23.2 11.7 %collective-permute-start.2 = (f32[3,1,8,8,768]{4,3,2,1,0:T(8,128)S(1)}, f32[3,1,8,8,768]{4,3,2,1,0:T(8,128)S(1)}, u32[]{:S(2)}, u32[]{:S(2)}) collective-permute-start(f32[3,1,8,8,768]{4,3,2,1,0:T(8,128)S(1)} %pad_maximum_fusion), channel_id=1, source_target_pairs={{0,1},{1,2},{2,3},{3,4},{4,5},{5,6},{6,7},{8,9},{9,10},{10,11},{11... | collective-permute-start | bytes 1769480 | tf_op jit(solution)/shard_map/ppermute | solution.py:18
  28.3 11.2 %collective-permute-start.3 = (f32[3,1,8,8,768]{4,3,2,1,0:T(8,128)S(1)}, f32[3,1,8,8,768]{4,3,2,1,0:T(8,128)S(1)}, u32[]{:S(2)}, u32[]{:S(2)}) collective-permute-start(f32[3,1,8,8,768]{4,3,2,1,0:T(8,128)S(1)} %pad_maximum_fusion), channel_id=1, source_target_pairs={{1,0},{2,1},{3,2},{4,3},{5,4},{6,5},{7,6},{9,8},{10,9},{11,10},{12... | collective-permute-start | bytes 1769480 | tf_op jit(solution)/shard_map/ppermute | solution.py:19
  40.2 4.4 %copy-start.1 = (f32[16,8,768]{2,1,0:T(8,128)S(1)}, f32[16,8,768]{2,1,0:T(8,128)}, u32[]{:S(2)}) copy-start(f32[16,8,768]{2,1,0:T(8,128)} %param.10) | copy-start | bytes 1179652
  40.2 4.5 %copy-start = (bf16[16,8,8,768]{3,2,1,0:T(8,128)(2,1)S(1)}, bf16[16,8,8,768]{3,2,1,0:T(8,128)(2,1)}, u32[]{:S(2)}) copy-start(bf16[16,8,8,768]{3,2,1,0:T(8,128)(2,1)} %param.11) | copy-start | bytes 4718596
  46.5 5.8 %collective-permute-start.4 = (f32[1,1,8,8,768]{4,3,2,1,0:T(8,128)S(1)}, f32[1,1,8,8,768]{4,3,2,1,0:T(8,128)S(1)}, u32[]{:S(2)}, u32[]{:S(2)}) collective-permute-start(f32[1,1,8,8,768]{4,3,2,1,0:T(8,128)S(1)} %bitcast.127), channel_id=1, source_target_pairs={{0,8},{8,16},{16,24},{24,32},{32,40},{40,48},{48,56},{56,64},{64,7... | collective-permute-start | bytes 589832 | tf_op jit(solution)/shard_map/ppermute | solution.py:18
  49.7 6.4 %collective-permute-start.5 = (f32[1,1,8,8,768]{4,3,2,1,0:T(8,128)S(1)}, f32[1,1,8,8,768]{4,3,2,1,0:T(8,128)S(1)}, u32[]{:S(2)}, u32[]{:S(2)}) collective-permute-start(f32[1,1,8,8,768]{4,3,2,1,0:T(8,128)S(1)} %bitcast.128), channel_id=1, source_target_pairs={{8,0},{16,8},{24,16},{32,24},{40,32},{48,40},{56,48},{64,56},{72,6... | collective-permute-start | bytes 589832 | tf_op jit(solution)/shard_map/ppermute | solution.py:19
  56.2 11.6 %collective-permute-start.6 = (f32[3,1,8,8,768]{4,3,2,1,0:T(8,128)S(1)}, f32[3,1,8,8,768]{4,3,2,1,0:T(8,128)S(1)}, u32[]{:S(2)}, u32[]{:S(2)}) collective-permute-start(f32[3,1,8,8,768]{4,3,2,1,0:T(8,128)S(1)} %pad_maximum_fusion.1), channel_id=1, source_target_pairs={{0,1},{1,2},{2,3},{3,4},{4,5},{5,6},{6,7},{8,9},{9,10},{10,11},{11... | collective-permute-start | bytes 1769480 | tf_op jit(solution)/shard_map/ppermute | solution.py:18
  61.0 11.2 %collective-permute-start.7 = (f32[3,1,8,8,768]{4,3,2,1,0:T(8,128)S(1)}, f32[3,1,8,8,768]{4,3,2,1,0:T(8,128)S(1)}, u32[]{:S(2)}, u32[]{:S(2)}) collective-permute-start(f32[3,1,8,8,768]{4,3,2,1,0:T(8,128)S(1)} %pad_maximum_fusion.1), channel_id=1, source_target_pairs={{1,0},{2,1},{3,2},{4,3},{5,4},{6,5},{7,6},{9,8},{10,9},{11,10},{12... | collective-permute-start | bytes 1769480 | tf_op jit(solution)/shard_map/ppermute | solution.py:19
  79.5 16.8 %copy-start.7 = (s32[1024,1]{0,1:T(1,128)S(1)}, s32[1024,1]{0,1:T(1,128)}, u32[]{:S(2)}) copy-start(s32[1024,1]{0,1:T(1,128)} %param.18) | copy-start | bytes 12292
  79.5 16.8 %copy-start.6 = (s32[1024]{0:T(1024)S(1)}, s32[1024]{0:T(1024)}, u32[]{:S(2)}) copy-start(s32[1024]{0:T(1024)} %param.19) | copy-start | bytes 12292
  80.9 6.9 %collective-permute-start.8 = (f32[1,1,8,8,768]{4,3,2,1,0:T(8,128)S(1)}, f32[1,1,8,8,768]{4,3,2,1,0:T(8,128)S(1)}, u32[]{:S(2)}, u32[]{:S(2)}) collective-permute-start(f32[1,1,8,8,768]{4,3,2,1,0:T(8,128)S(1)} %bitcast.121), channel_id=1, source_target_pairs={{0,8},{8,16},{16,24},{24,32},{32,40},{40,48},{48,56},{56,64},{64,7... | collective-permute-start | bytes 589832 | tf_op jit(solution)/shard_map/ppermute | solution.py:18
  85.2 7.0 %collective-permute-start.9 = (f32[1,1,8,8,768]{4,3,2,1,0:T(8,128)S(1)}, f32[1,1,8,8,768]{4,3,2,1,0:T(8,128)S(1)}, u32[]{:S(2)}, u32[]{:S(2)}) collective-permute-start(f32[1,1,8,8,768]{4,3,2,1,0:T(8,128)S(1)} %bitcast.122), channel_id=1, source_target_pairs={{8,0},{16,8},{24,16},{32,24},{40,32},{48,40},{56,48},{64,56},{72,6... | collective-permute-start | bytes 589832 | tf_op jit(solution)/shard_map/ppermute | solution.py:19
  92.3 10.8 %collective-permute-start.10 = (f32[3,1,8,8,768]{4,3,2,1,0:T(8,128)S(1)}, f32[3,1,8,8,768]{4,3,2,1,0:T(8,128)S(1)}, u32[]{:S(2)}, u32[]{:S(2)}) collective-permute-start(f32[3,1,8,8,768]{4,3,2,1,0:T(8,128)S(1)} %pad_maximum_fusion.2), channel_id=1, source_target_pairs={{0,1},{1,2},{2,3},{3,4},{4,5},{5,6},{6,7},{8,9},{9,10},{10,11},{11... | collective-permute-start | bytes 1769480 | tf_op jit(solution)/shard_map/ppermute | solution.py:18
  96.3 11.2 %collective-permute-start.11 = (f32[3,1,8,8,768]{4,3,2,1,0:T(8,128)S(1)}, f32[3,1,8,8,768]{4,3,2,1,0:T(8,128)S(1)}, u32[]{:S(2)}, u32[]{:S(2)}) collective-permute-start(f32[3,1,8,8,768]{4,3,2,1,0:T(8,128)S(1)} %pad_maximum_fusion.2), channel_id=1, source_target_pairs={{1,0},{2,1},{3,2},{4,3},{5,4},{6,5},{7,6},{9,8},{10,9},{11,10},{12... | collective-permute-start | bytes 1769480 | tf_op jit(solution)/shard_map/ppermute | solution.py:19
  114.7 1.3 copy-start.4
  114.9 5.5 %copy-start.2 = (f32[16,8,768]{2,1,0:T(8,128)}, f32[16,8,768]{2,1,0:T(8,128)S(1)}, u32[]{:S(2)}) copy-start(f32[16,8,768]{2,1,0:T(8,128)S(1)} %multiply_bitcast_fusion) | copy-start | bytes 1179652
  116.2 4.1 %copy-start.3 = (f32[16,768,6]{1,0,2:T(8,128)}, f32[16,768,6]{1,0,2:T(8,128)S(1)}, u32[]{:S(2)}) copy-start(f32[16,768,6]{1,0,2:T(8,128)S(1)} %multiply_reduce_fusion) | copy-start | bytes 884740
  139.0 10.9 %copy-start.9 = (u32[256]{0:T(256)S(1)}, u32[256]{0:T(256)}, u32[]{:S(2)}) copy-start(u32[256]{0:T(256)} %constant.33) | copy-start | bytes 3076
Sparse Core Ops, SparseCore 0:
  150.0 149.3 all-reduce.2
where the time goes:
time: 313 us; the launch traced here: 308 us
  waiting for transfers between devices  189 us (60%)
  other arithmetic  38.2 us (12%)
  starting transfers between devices  35 us (11%)
  local copies, waits for them, and re-layouts  30.8 us (10%)
  between operations  15.2 us (5%)
    unnamed x2, waiting for transfers between devices  149 us
    ppermute x6, starting transfers between devices, with_halo(): before = lax.ppermute(last, axis, up)  25.2 us
    ppermute x6, waiting for transfers between devices, with_halo(): after = lax.ppermute(leading, axis, down)  24.1 us
    scatter-add x1, other arithmetic, per_device(): dense = jax.ops.segment_sum(values.T, target, num_segments=regions * OWNED)  18.7 us
    ppermute x6, waiting for transfers between devices, with_halo(): before = lax.ppermute(last, axis, up)  16.2 us
    dot_general x3, other arithmetic, per_device(): jnp.einsum('tkmjv,tkmv->tjv', coupling, near, preferred_element_type=jnp....  12.9 us
    reshape x1, local copies, waits for them, and re-layouts, per_device(): dense = dense.reshape(regions, OWNED, 6).transpose(0, 2, 1)  10.8 us
    ppermute x6, starting transfers between devices, with_halo(): after = lax.ppermute(leading, axis, down)  9.82 us
  transfers between devices with their start and end apart: 13, of which 13 were waited for; matrix products, arithmetic and copies ran while one was open for 2% of the time, Pallas kernels for 0%

commit v1 on v0

v1 whole, which is shorter than its diff:
```python
import functools

import jax
import jax.numpy as jnp
from jax import lax
from jax.experimental import pallas as pl
from jax.experimental.pallas import tpu as pltpu
from jax.sharding import PartitionSpec as P

NVAR = 6
SWEEPS = 3
OWNED = 1024
CAP = 128
LANES = 128

F32 = jnp.float32
BF16 = jnp.bfloat16

VMEM = pl.BlockSpec(memory_space=pltpu.VMEM)
SMEM = pl.BlockSpec(memory_space=pltpu.SMEM)


def solve_tile(t, resid, inv_ref, live):
    total = None
    for j in range(inv_ref.shape[1]):
        term = inv_ref[t, j].astype(F32) * resid[pl.ds(j, 1), :]
        total = term if total is None else total + term
    rows = lax.broadcasted_iota(jnp.int32, total.shape, 0)
    return jnp.where((rows < NVAR) & live, total, 0.0)


def pack_sent(adj_ref, send_ref, sent_ref):
    for s in range(send_ref.shape[1]):
        tile = adj_ref[pl.ds(pl.multiple_of(send_ref[0, s] * 8, 8), 8), :]
        sent_ref[NVAR * s : NVAR * (s + 1), :] = tile[:NVAR]


def first_kernel(send_ref, count_ref, rhs_ref, inv_ref, adj_ref, sent_ref):
    tiles = rhs_ref.shape[0]

    @pl.loop(0, tiles)
    def _(t):
        out = solve_tile(t, rhs_ref.at[t], inv_ref, t < count_ref[0])
        adj_ref[pl.ds(pl.multiple_of(t * 8, 8), 8), :] = out

    pack_sent(adj_ref, send_ref, sent_ref)


def build_extended(old_ref, halo_refs, ext_ref):
    own = old_ref.shape[0]
    ext_ref[:own, :] = old_ref[...]
    odd_region = lax.axis_index("region") % 2
    odd_sub = lax.axis_index("sub") % 2
    places = (1 - odd_region, odd_region, 3 - odd_sub, 2 + odd_sub)
    width = halo_refs[0].shape[0]
    for place, halo in zip(places, halo_refs):
        ext_ref[pl.ds(pl.multiple_of(own + place * width, 8), width), :] = halo[...]


def pull_and_solve(t, near_ref, count_ref, rhs_ref, inv_ref, cpl_ref, ext_ref, resid_ref):
    own = rhs_ref.shape[0]
    acc = rhs_ref[t]
    for k in range(cpl_ref.shape[1]):
        tile = near_ref[t, k]
        base = jnp.where(tile < own, tile * 8, tile * NVAR + own * (8 - NVAR))
        for m in range(NVAR):
            acc = acc - cpl_ref[t, k, m].astype(F32) * ext_ref[pl.ds(base + m, 1), :]
    resid_ref[...] = acc
    return solve_tile(t, resid_ref, inv_ref, t < count_ref[0])


def sweep_kernel(
    near_ref, send_ref, count_ref, rhs_ref, inv_ref, cpl_ref, old_ref, h0, h1, h2, h3,
    adj_ref, sent_ref, ext_ref, resid_ref,
):
    build_extended(old_ref, (h0, h1, h2, h3), ext_ref)

    @pl.loop(0, rhs_ref.shape[0])
    def _(t):
        out = pull_and_solve(t, near_ref, count_ref, rhs_ref, inv_ref, cpl_ref, ext_ref, resid_ref)
        adj_ref[pl.ds(pl.multiple_of(t * 8, 8), 8), :] = out

    pack_sent(adj_ref, send_ref, sent_ref)


def last_kernel(
    near_ref, count_ref, rhs_ref, inv_ref, cpl_ref, hess_ref, old_ref, h0, h1, h2, h3,
    vertex_ref, region_ref, slot_ref, rank_hot_ref,
    adj_ref, metric_ref, parcel_ref, ext_ref, resid_ref, abs_ref, table_ref, gathered_ref,
):
    build_extended(old_ref, (h0, h1, h2, h3), ext_ref)
    tiles, width = rhs_ref.shape[0], rhs_ref.shape[2]
    chunks = width // LANES

    @pl.loop(0, tiles)
    def _(t):
        out = pull_and_solve(t, near_ref, count_ref, rhs_ref, inv_ref, cpl_ref, ext_ref, resid_ref)
        adj_ref[t] = out
        abs_ref[...] = jnp.abs(out)
        total = None
        for c in range(NVAR):
            term = hess_ref[t, c].astype(F32) * abs_ref[pl.ds(c, 1), :]
            total = term if total is None else total + term
        metric_ref[t] = total
        for q in range(chunks):
            table_ref[t * chunks + q, :NVAR, :] = total[:, q * LANES : (q + 1) * LANES]

    vertex = vertex_ref[...]
    entries = vertex.shape[1]
    groups = entries // LANES
    row = vertex // LANES
    lane = vertex % LANES
    rows_b = [jnp.broadcast_to(row[:, g * LANES : (g + 1) * LANES], (8, LANES)) for g in range(groups)]
    lanes_b = [jnp.broadcast_to(lane[:, g * LANES : (g + 1) * LANES], (8, LANES)) for g in range(groups)]

    def pick(r, totals):
        block = table_ref[r]
        return tuple(
            jnp.where(rows_b[g] == r, jnp.take_along_axis(block, lanes_b[g], axis=1), totals[g])
            for g in range(groups)
        )

    zero = jnp.zeros((8, LANES), F32)
    totals = lax.fori_loop(0, tiles * chunks, pick, (zero,) * groups, unroll=4)
    for g in range(groups):
        gathered_ref[:, g * LANES : (g + 1) * LANES] = totals[g]
    values = gathered_ref[...]
    which = lax.broadcasted_iota(jnp.int32, values.shape, 0)
    values = jnp.where(which == NVAR, slot_ref[...].astype(F32), jnp.where(which < NVAR, values, 0.0))
    high = values.astype(BF16).astype(F32)
    low = values - high

    regions = parcel_ref.shape[0]
    dest = region_ref[...]
    half = regions // 2

    for part in range(2):
        pieces = []
        for piece in (high, low):
            for d in range(half):
                pieces.append(jnp.where(dest == part * half + d, piece, 0.0))
        left = jnp.concatenate(pieces, axis=0).astype(BF16)
        placed = lax.dot_general(left, rank_hot_ref[...], (((1,), (1,)), ((), ())), preferred_element_type=F32)
        placed = placed[: half * 8] + placed[half * 8 :]
        for d in range(half):
            parcel_ref[part * half + d] = placed[d * 8 : (d + 1) * 8]


def rank_kernel(region_ref, hot_ref, rank_ref):
    entries = region_ref.shape[1]
    regions = 32
    upper = (
        lax.broadcasted_iota(jnp.int32, (LANES, LANES), 0) <= lax.broadcasted_iota(jnp.int32, (LANES, LANES), 1)
    )
    upper = jnp.where(upper, 1.0, 0.0).astype(BF16)
    region_id = lax.broadcasted_iota(jnp.int32, (regions, LANES), 0)
    carry = jnp.zeros((regions, 1), F32)
    for g in range(entries // LANES):
        here = region_id == region_ref[:, g * LANES : (g + 1) * LANES]
        hot = jnp.where(here, 1.0, 0.0)
        count = lax.dot_general(hot.astype(BF16), upper, (((1,), (0,)), ((), ())), preferred_element_type=F32) + carry
        rank_ref[:, g * LANES : (g + 1) * LANES] = jnp.sum(
            jnp.where(here, count - 1.0, 0.0), axis=0, keepdims=True
        )
        carry = count[:, LANES - 1 :]
    rank = rank_ref[...].astype(jnp.int32)
    places = lax.broadcasted_iota(jnp.int32, (CAP, entries), 0)
    hot_ref[...] = jnp.where(places == rank, 1.0, 0.0).astype(BF16)


def owner_kernel(parcel_ref, owned_ref):
    regions = parcel_ref.shape[0]
    highs = OWNED // LANES
    row_high = lax.broadcasted_iota(jnp.int32, (highs * 8, LANES), 0) // 8
    low_id = lax.broadcasted_iota(jnp.int32, (LANES, LANES), 0)
    total = jnp.zeros((2 * highs * 8, LANES), F32)
    for r in range(0, regions, 2):
        lefts, rights = [], []
        for q in (r, r + 1):
            block = parcel_ref[q]
            slot = block[NVAR : NVAR + 1, :].astype(jnp.int32)
            high = block.astype(BF16).astype(F32)
            low = block - high
            mask = row_high == slot // LANES
            tall_h = jnp.where(mask, jnp.concatenate([high] * highs, axis=0), 0.0)
            tall_l = jnp.where(mask, jnp.concatenate([low] * highs, axis=0), 0.0)
            lefts.append(jnp.concatenate([tall_h, tall_l], axis=0).astype(BF16))
            rights.append(jnp.where(low_id == slot % LANES, 1.0, 0.0).astype(BF16))
        left = jnp.concatenate(lefts, axis=1)
        right = jnp.concatenate(rights, axis=1)
        total += lax.dot_general(left, right, (((1,), (1,)), ((), ())), preferred_element_type=F32)
    total = total[: highs * 8] + total[highs * 8 :]
    for h in range(highs):
        owned_ref[:, h * LANES : (h + 1) * LANES] = total[h * 8 : h * 8 + NVAR]


def pairings(regions, subs):
    def swap(length, first):
        return [p for i in range(first, length - 1, 2) for p in ((i, i + 1), (i + 1, i))]

    along_region = [("region", swap(regions, 0)), ("region", swap(regions, 1))]
    along_sub = [("sub", swap(subs, 0)), ("sub", swap(subs, 1))]
    return along_region + along_sub


def exchange(sent):
    ra, rb, sa, sb = pairings(lax.axis_size("region"), lax.axis_size("sub"))
    got_rb = lax.ppermute(sent, *rb)
    got_ra = lax.ppermute(sent, *ra)
    got_sb = lax.ppermute(sent, *sb)
    got_sa = lax.ppermute(sent, *sa)
    return got_ra, got_rb, got_sa, got_sb


def per_device(
    rhs, diag_inv, coupling, neighbours, send_tiles, tile_count, hessian, shared_vertex, owner_region, owner_slot
):
    tiles, block, width = rhs.shape
    sends = send_tiles.shape[1]
    entries = shared_vertex.shape[0]
    regions = lax.axis_size("region")
    params = pltpu.CompilerParams(vmem_limit_bytes=40 * 2**20)
    near = pltpu.with_memory_space_constraint(coupling, pltpu.VMEM)
    coupling = near
    vertex = shared_vertex.reshape(1, entries)
    dest = owner_region.reshape(1, entries)
    slot = owner_slot.reshape(1, entries)

    adj_shape = jax.ShapeDtypeStruct((tiles * 8, width), F32)
    sent_shape = jax.ShapeDtypeStruct((sends * NVAR, width), F32)
    ext = pltpu.VMEM((tiles * 8 + 4 * sends * NVAR, width), F32)
    resid = pltpu.VMEM((8, width), F32)

    adjoint, sent = pl.pallas_call(
        first_kernel,
        out_shape=(adj_shape, sent_shape),
        in_specs=[SMEM, SMEM, VMEM, VMEM],
        out_specs=(VMEM, VMEM),
        compiler_params=params,
    )(send_tiles, tile_count, rhs, diag_inv)
    rank_hot = pl.pallas_call(
        rank_kernel,
        out_shape=jax.ShapeDtypeStruct((CAP, entries), BF16),
        in_specs=[VMEM],
        out_specs=VMEM,
        scratch_shapes=[pltpu.VMEM((1, entries), F32)],
        compiler_params=params,
    )(dest)
    for sweep in range(SWEEPS - 1):
        halos = exchange(sent)
        adjoint, sent = pl.pallas_call(
            sweep_kernel,
            out_shape=(adj_shape, sent_shape),
            in_specs=[SMEM] * 3 + [VMEM] * 8,
            out_specs=(VMEM, VMEM),
            scratch_shapes=[ext, resid],
            compiler_params=params,
        )(neighbours, send_tiles, tile_count, rhs, diag_inv, coupling, adjoint, *halos)
    halos = exchange(sent)
    out, metric, parcels = pl.pallas_call(
        last_kernel,
        out_shape=(
            jax.ShapeDtypeStruct((tiles, block, width), F32),
            jax.ShapeDtypeStruct((tiles, 6, width), F32),
            jax.ShapeDtypeStruct((regions, 8, CAP), F32),
        ),
        in_specs=[SMEM] * 2 + [VMEM] * 13,
        out_specs=(VMEM, VMEM, VMEM),
        scratch_shapes=[
            ext,
            resid,
            pltpu.VMEM((8, width), F32),
            pltpu.VMEM((tiles * width // LANES, 8, LANES), F32),
            pltpu.VMEM((8, entries), F32),
        ],
        compiler_params=params,
    )(neighbours, tile_count, rhs, diag_inv, coupling, hessian, adjoint, *halos, vertex, dest, slot, rank_hot)
    parcels = lax.all_to_all(parcels, "region", 0, 0, tiled=True)
    owned = pl.pallas_call(
        owner_kernel,
        out_shape=jax.ShapeDtypeStruct((6, OWNED), F32),
        in_specs=[VMEM],
        out_specs=VMEM,
        compiler_params=params,
    )(parcels)
    return out, metric, owned


def solution(mesh):
    both = ("region", "sub")
    placed = (
        P(both, None, None),
        P(both, None, None, None),
        P(both, None, None, None, None),
        P(both, None),
        P(both, None),
        P(both),
        P(both, None, None, None),
        P(both),
        P(both, None),
        P(both),
    )
    return jax.shard_map(
        per_device,
        mesh=mesh,
        in_specs=placed,
        out_specs=(P(both, None, None), P(both, None, None), P(None, both)),
        check_vma=False,
    )
```

time: 313 us -> 85.5 us (0.27); the launches traced: 308 us -> 84.6 us
  waiting for transfers between devices: 189 us -> 17.8 us
  other arithmetic: 38.2 us -> 0 us
  local copies, waits for them, and re-layouts: 30.8 us -> 7.03 us
  Pallas kernels: 0 us -> 16.4 us
  between operations: 15.2 us -> 1.5 us
  starting transfers between devices: 35 us -> 41.8 us
    unnamed x2 -> x0, waiting for transfers between devices: 149 us -> none
    ppermute x12, waiting for transfers between devices: 40.3 us -> 9.26 us  [the longest x3 9.24 us: exchange(): got_ra = lax.ppermute(sent, *ra)]
    scatter-add x1 -> x0, other arithmetic: 18.7 us -> none  [per_device(): dense = jax.ops.segment_sum(values.T, target, num_segments=regions * OWNED)]
    pallas_call x0 -> x6, Pallas kernels: none -> 16.4 us  [the longest x1 7.98 us: per_device(): pl.pallas_call(last_kernel, out_shape=(jax.ShapeDtypeStruct((tiles, block...]
    dot_general x8 -> x0, other arithmetic: 16 us -> none  [the longest x3 12.9 us: per_device(): jnp.einsum('tkmjv,tkmv->tjv', coupling, near, preferred_element_type=jnp....]
    all_to_all x0 -> x1, starting transfers between devices: none -> 14 us  [per_device(): parcels = lax.all_to_all(parcels, 'region', 0, 0, tiled=True)]
    reshape x1 -> x0, local copies, waits for them, and re-layouts: 10.8 us -> none  [per_device(): dense = dense.reshape(regions, OWNED, 6).transpose(0, 2, 1)]
    all_to_all x0 -> x1, waiting for transfers between devices: none -> 8.54 us  [per_device(): parcels = lax.all_to_all(parcels, 'region', 0, 0, tiled=True)]
  transfers between devices with their start and end apart: 13 -> 13, of which waited for: 13 -> 4; matrix products, arithmetic and copies ran while one was open for 2% -> 1% of each run, Pallas kernels for 0% -> 1%
where the time goes in v1:
time: 85.5 us; the launch traced here: 84.6 us
  starting transfers between devices  41.8 us (49%)
  waiting for transfers between devices  17.8 us (21%)
  Pallas kernels  16.4 us (19%)
  local copies, waits for them, and re-layouts  7.03 us (8%)
  between operations  1.5 us (2%)
    all_to_all x1, starting transfers between devices, per_device(): parcels = lax.all_to_all(parcels, 'region', 0, 0, tiled=True)  14 us
    ppermute x3, starting transfers between devices, exchange(): got_sb = lax.ppermute(sent, *sb)  12.9 us
    ppermute x3, starting transfers between devices, exchange(): got_ra = lax.ppermute(sent, *ra)  12.6 us
    ppermute x3, waiting for transfers between devices, exchange(): got_ra = lax.ppermute(sent, *ra)  9.24 us
    all_to_all x1, waiting for transfers between devices, per_device(): parcels = lax.all_to_all(parcels, 'region', 0, 0, tiled=True)  8.54 us
    pallas_call x1, Pallas kernels, per_device(): pl.pallas_call(last_kernel, out_shape=(jax.ShapeDtypeStruct((tiles, block...  7.98 us
    unnamed x29, local copies, waits for them, and re-layouts  7.03 us
    pallas_call x2, Pallas kernels, per_device(): pl.pallas_call(sweep_kernel, out_shape=(adj_shape, sent_shape), in_specs=...  5.43 us
  transfers between devices with their start and end apart: 13, of which 4 were waited for; matrix products, arithmetic and copies ran while one was open for 1% of the time, Pallas kernels for 1%

profile of v1, /device:TPU:1, one launch (start us, length us, event | category | flops | bytes accessed | tf_op | source)
XLA Modules:
  0.0 84.6 jit_solution(3670904210511369503)
XLA Ops:
  1.3 1.4 %copy-done.2 = bf16[16,8,8,768]{3,2,1,0:T(8,128)(2,1)S(1)} copy-done((bf16[16,8,8,768]{3,2,1,0:T(8,128)(2,1)S(1)}, bf16[16,8,8,768]{3,2,1,0:T(8,128)(2,1)}, u32[]{:S(2)}) %copy-start.2) | copy-done | bytes 1572888
  2.7 1.0 %copy-done.4 = f32[16,8,768]{2,1,0:T(8,128)S(1)} copy-done((f32[16,8,768]{2,1,0:T(8,128)S(1)}, f32[16,8,768]{2,1,0:T(8,128)}, u32[]{:S(2)}) %copy-start.4) | copy-done | bytes 393240
  3.7 0.7 copy-done.7
  4.4 1.1 %shard_map.121 = (f32[128,768]{1,0:T(8,128)S(1)}, f32[48,768]{1,0:T(8,128)S(1)}) custom-call(s32[1,8]{1,0:T(1,128)S(1)} %copy-done.7, s32[1]{0:T(128)S(6)} %copy.18.count_ref, f32[16,8,768]{2,1,0:T(8,128)S(1)} %copy-done.4, bf16[16,8,8,768]{3,2,1,0:T(8,128)(2,1)S(1)} %copy-done.2), custom_call_target="tpu_custom_call" | custom-call | tf_op jit(solution)/shard_map/pallas_call | solution.py:234
  5.5 4.5 %collective-permute-start.3 = (f32[48,768]{1,0:T(8,128)S(1)}, f32[48,768]{1,0:T(8,128)S(1)}, u32[]{:S(2)}, u32[]{:S(2)}) collective-permute-start(f32[48,768]{1,0:T(8,128)S(1)} %get-tuple-element.13), channel_id=1, source_target_pairs={{1,2},{2,1},{3,4},{4,3},{5,6},{6,5},{9,10},{10,9},{11,12},{12,11},... | collective-permute-start | bytes 442376 | tf_op jit(solution)/shard_map/ppermute | solution.py:210
  10.0 0.1 collective-permute-start.2
  10.1 0.7 collective-permute-start.1
  10.8 3.9 %collective-permute-start = (f32[48,768]{1,0:T(8,128)S(1)}, f32[48,768]{1,0:T(8,128)S(1)}, u32[]{:S(2)}, u32[]{:S(2)}) collective-permute-start(f32[48,768]{1,0:T(8,128)S(1)} %get-tuple-element.13), channel_id=1, source_target_pairs={{0,8},{8,0},{16,24},{24,16},{32,40},{40,32},{48,56},{56,48},{64,72... | collective-permute-start | bytes 442376 | tf_op jit(solution)/shard_map/ppermute | solution.py:209
  14.7 0.1 copy.15.near_ref
  14.8 3.4 %collective-permute-done.h0 = f32[48,768]{1,0:T(8,128)S(1)} collective-permute-done((f32[48,768]{1,0:T(8,128)S(1)}, f32[48,768]{1,0:T(8,128)S(1)}, u32[]{:S(2)}, u32[]{:S(2)}) %collective-permute-start) | collective-permute-done | bytes 147488 | tf_op jit(solution)/shard_map/ppermute | solution.py:209
  18.2 0.0 copy-start
  18.2 2.8 %copy-done = bf16[16,4,8,8,768]{4,3,2,1,0:T(8,128)(2,1)S(1)} copy-done((bf16[16,4,8,8,768]{4,3,2,1,0:T(8,128)(2,1)S(1)}, bf16[16,4,8,8,768]{4,3,2,1,0:T(8,128)(2,1)}, u32[]{:S(2)}) %copy-start) | copy-done | bytes 6291480
  21.0 2.7 %shard_map.122 = (f32[128,768]{1,0:T(8,128)S(1)}, f32[48,768]{1,0:T(8,128)S(1)}) custom-call(s32[16,4]{1,0:T(8,128)S(1)} %copy.15.near_ref, s32[1,8]{1,0:T(1,128)S(1)} %copy-done.8, s32[1]{0:T(128)S(6)} %copy.18.count_ref, f32[16,8,768]{2,1,0:T(8,128)S(1)} %copy-done.5, bf16[16,8,8,768]{3,2,1,0:T(8,128)(2,1)S(1)} %copy-done.3, ...), custom_call_target="tpu_custom_call" | custom-call | tf_op jit(solution)/shard_map/pallas_call | solution.py:251
  23.7 4.3 %collective-permute-start.7 = (f32[48,768]{1,0:T(8,128)S(1)}, f32[48,768]{1,0:T(8,128)S(1)}, u32[]{:S(2)}, u32[]{:S(2)}) collective-permute-start(f32[48,768]{1,0:T(8,128)S(1)} %get-tuple-element.15), channel_id=1, source_target_pairs={{1,2},{2,1},{3,4},{4,3},{5,6},{6,5},{9,10},{10,9},{11,12},{12,11},... | collective-permute-start | bytes 442376 | tf_op jit(solution)/shard_map/ppermute | solution.py:210
  28.1 0.1 collective-permute-start.6
  28.2 0.7 collective-permute-start.5
  28.8 3.6 %collective-permute-start.4 = (f32[48,768]{1,0:T(8,128)S(1)}, f32[48,768]{1,0:T(8,128)S(1)}, u32[]{:S(2)}, u32[]{:S(2)}) collective-permute-start(f32[48,768]{1,0:T(8,128)S(1)} %get-tuple-element.15), channel_id=1, source_target_pairs={{0,8},{8,0},{16,24},{24,16},{32,40},{40,32},{48,56},{56,48},{64,72... | collective-permute-start | bytes 442376 | tf_op jit(solution)/shard_map/ppermute | solution.py:209
  32.5 3.5 %collective-permute-done.4.h0 = f32[48,768]{1,0:T(8,128)S(1)} collective-permute-done((f32[48,768]{1,0:T(8,128)S(1)}, f32[48,768]{1,0:T(8,128)S(1)}, u32[]{:S(2)}, u32[]{:S(2)}) %collective-permute-start.4) | collective-permute-done | bytes 147488 | tf_op jit(solution)/shard_map/ppermute | solution.py:209
  35.9 2.7 %shard_map.123 = (f32[128,768]{1,0:T(8,128)S(1)}, f32[48,768]{1,0:T(8,128)S(1)}) custom-call(s32[16,4]{1,0:T(8,128)S(1)} %copy.15.near_ref, s32[1,8]{1,0:T(1,128)S(1)} %copy-done.8, s32[1]{0:T(128)S(6)} %copy.18.count_ref, f32[16,8,768]{2,1,0:T(8,128)S(1)} %copy-done.5, bf16[16,8,8,768]{3,2,1,0:T(8,128)(2,1)S(1)} %copy-done.3, ...), custom_call_target="tpu_custom_call" | custom-call | tf_op jit(solution)/shard_map/pallas_call | solution.py:251
  38.7 0.0 copy-start.10
  38.7 4.0 %collective-permute-start.11 = (f32[48,768]{1,0:T(8,128)S(1)}, f32[48,768]{1,0:T(8,128)S(1)}, u32[]{:S(2)}, u32[]{:S(2)}) collective-permute-start(f32[48,768]{1,0:T(8,128)S(1)} %get-tuple-element.17), channel_id=1, source_target_pairs={{1,2},{2,1},{3,4},{4,3},{5,6},{6,5},{9,10},{10,9},{11,12},{12,11},... | collective-permute-start | bytes 442376 | tf_op jit(solution)/shard_map/ppermute | solution.py:210
  42.7 0.1 collective-permute-start.10
  42.8 0.7 collective-permute-start.9
  43.5 5.1 %collective-permute-start.8 = (f32[48,768]{1,0:T(8,128)S(1)}, f32[48,768]{1,0:T(8,128)S(1)}, u32[]{:S(2)}, u32[]{:S(2)}) collective-permute-start(f32[48,768]{1,0:T(8,128)S(1)} %get-tuple-element.17), channel_id=1, source_target_pairs={{0,8},{8,0},{16,24},{24,16},{32,40},{40,32},{48,56},{56,48},{64,72... | collective-permute-start | bytes 442376 | tf_op jit(solution)/shard_map/ppermute | solution.py:209
  48.6 0.7 shard_map.124.rank_hot_ref
  49.3 0.3 copy.16.hess_ref
  49.6 2.4 %collective-permute-done.8.h0 = f32[48,768]{1,0:T(8,128)S(1)} collective-permute-done((f32[48,768]{1,0:T(8,128)S(1)}, f32[48,768]{1,0:T(8,128)S(1)}, u32[]{:S(2)}, u32[]{:S(2)}) %collective-permute-start.8) | collective-permute-done | bytes 147488 | tf_op jit(solution)/shard_map/ppermute | solution.py:209
  52.1 8.0 %shard_map.125 = (f32[16,8,768]{2,1,0:T(8,128)}, f32[16,6,768]{2,1,0:T(8,128)S(1)}, f32[32,8,128]{2,1,0:T(8,128)}) custom-call(s32[16,4]{1,0:T(8,128)S(1)} %copy.15.near_ref, s32[1]{0:T(128)S(6)} %copy.18.count_ref, f32[16,8,768]{2,1,0:T(8,128)S(1)} %copy-done.5, bf16[16,8,8,768]{3,2,1,0:T(8,128)(2,1)S(1)} %copy-done.3, ...), custom_call_target="tpu_custom_call" | custom-call | tf_op jit(solution)/shard_map/pallas_call | solution.py:260
  60.0 14.0 %all-to-all-start = ((f32[32,8,128]{2,1,0:T(8,128)}), f32[32,8,128]{2,1,0:T(8,128)S(1)}, u32[]{:S(2)}, u32[]{:S(2)}) async-start(f32[32,8,128]{2,1,0:T(8,128)} %get-tuple-element.20), calls=%async_computation | async-start | bytes 262144 | tf_op jit(solution)/shard_map/all_to_all | solution.py:278
  74.1 0.8 copy.17
  74.9 8.5 %all-to-all-done.parcel_ref = f32[32,8,128]{2,1,0:T(8,128)S(1)} async-done(((f32[32,8,128]{2,1,0:T(8,128)}), f32[32,8,128]{2,1,0:T(8,128)S(1)}, u32[]{:S(2)}, u32[]{:S(2)}) %all-to-all-start) | async-done | bytes 131104 | tf_op jit(solution)/shard_map/all_to_all | solution.py:278
  83.4 1.2 %shard_map.126 = f32[6,1024]{1,0:T(8,128)} custom-call(f32[32,8,128]{2,1,0:T(8,128)S(1)} %all-to-all-done.parcel_ref), custom_call_target="tpu_custom_call" | custom-call | tf_op jit(solution)/shard_map/pallas_call | solution.py:279
  (29 shorter events, 0.1 us)
Async XLA Ops:
  0.6 17.6 %copy-start.8 = (s32[1,8]{1,0:T(1,128)S(1)}, s32[1,8]{1,0:T(1,128)}, u32[]{:S(2)}) copy-start(s32[1,8]{1,0:T(1,128)} %send_ref.5) | copy-start | bytes 100
  1.3 1.4 %copy-start.2 = (bf16[16,8,8,768]{3,2,1,0:T(8,128)(2,1)S(1)}, bf16[16,8,8,768]{3,2,1,0:T(8,128)(2,1)}, u32[]{:S(2)}) copy-start(bf16[16,8,8,768]{3,2,1,0:T(8,128)(2,1)} %inv_ref.7) | copy-start | bytes 4718596
  2.7 1.0 %copy-start.4 = (f32[16,8,768]{2,1,0:T(8,128)S(1)}, f32[16,8,768]{2,1,0:T(8,128)}, u32[]{:S(2)}) copy-start(f32[16,8,768]{2,1,0:T(8,128)} %rhs_ref.7) | copy-start | bytes 1179652
  3.7 0.7 copy-start.7
  4.4 10.4 %copy-start.12 = (s32[16,4]{0,1:T(4,128)S(1)}, s32[16,4]{0,1:T(4,128)}, u32[]{:S(2)}) copy-start(s32[16,4]{0,1:T(4,128)} %param.13) | copy-start | bytes 772
  4.4 13.8 %copy-start.3 = (bf16[16,8,8,768]{3,2,1,0:T(8,128)(2,1)S(1)}, bf16[16,8,8,768]{3,2,1,0:T(8,128)(2,1)}, u32[]{:S(2)}) copy-start(bf16[16,8,8,768]{3,2,1,0:T(8,128)(2,1)} %inv_ref.7) | copy-start | bytes 4718596
  4.4 13.8 %copy-start.5 = (f32[16,8,768]{2,1,0:T(8,128)S(1)}, f32[16,8,768]{2,1,0:T(8,128)}, u32[]{:S(2)}) copy-start(f32[16,8,768]{2,1,0:T(8,128)} %rhs_ref.7) | copy-start | bytes 1179652
  5.5 9.3 %collective-permute-start.3 = (f32[48,768]{1,0:T(8,128)S(1)}, f32[48,768]{1,0:T(8,128)S(1)}, u32[]{:S(2)}, u32[]{:S(2)}) collective-permute-start(f32[48,768]{1,0:T(8,128)S(1)} %get-tuple-element.13), channel_id=1, source_target_pairs={{1,2},{2,1},{3,4},{4,3},{5,6},{6,5},{9,10},{10,9},{11,12},{12,11},... | collective-permute-start | bytes 442376 | tf_op jit(solution)/shard_map/ppermute | solution.py:210
  10.0 4.8 %collective-permute-start.2 = (f32[48,768]{1,0:T(8,128)S(1)}, f32[48,768]{1,0:T(8,128)S(1)}, u32[]{:S(2)}, u32[]{:S(2)}) collective-permute-start(f32[48,768]{1,0:T(8,128)S(1)} %get-tuple-element.13), channel_id=1, source_target_pairs={{0,1},{1,0},{2,3},{3,2},{4,5},{5,4},{6,7},{7,6},{8,9},{9,8},{10,11... | collective-permute-start | bytes 442376 | tf_op jit(solution)/shard_map/ppermute | solution.py:211
  10.1 4.7 %collective-permute-start.1 = (f32[48,768]{1,0:T(8,128)S(1)}, f32[48,768]{1,0:T(8,128)S(1)}, u32[]{:S(2)}, u32[]{:S(2)}) collective-permute-start(f32[48,768]{1,0:T(8,128)S(1)} %get-tuple-element.13), channel_id=1, source_target_pairs={{8,16},{16,8},{24,32},{32,24},{40,48},{48,40},{56,64},{64,56},{72,... | collective-permute-start | bytes 442376 | tf_op jit(solution)/shard_map/ppermute | solution.py:208
  10.8 7.4 %collective-permute-start = (f32[48,768]{1,0:T(8,128)S(1)}, f32[48,768]{1,0:T(8,128)S(1)}, u32[]{:S(2)}, u32[]{:S(2)}) collective-permute-start(f32[48,768]{1,0:T(8,128)S(1)} %get-tuple-element.13), channel_id=1, source_target_pairs={{0,8},{8,0},{16,24},{24,16},{32,40},{40,32},{48,56},{56,48},{64,72... | collective-permute-start | bytes 442376 | tf_op jit(solution)/shard_map/ppermute | solution.py:209
  18.2 2.8 %copy-start = (bf16[16,4,8,8,768]{4,3,2,1,0:T(8,128)(2,1)S(1)}, bf16[16,4,8,8,768]{4,3,2,1,0:T(8,128)(2,1)}, u32[]{:S(2)}) copy-start(bf16[16,4,8,8,768]{4,3,2,1,0:T(8,128)(2,1)} %cpl_ref.5) | copy-start | bytes 18874372
  21.0 14.9 %copy-start.1 = (bf16[16,4,8,8,768]{4,3,2,1,0:T(8,128)(2,1)S(1)}, bf16[16,4,8,8,768]{4,3,2,1,0:T(8,128)(2,1)}, u32[]{:S(2)}) copy-start(bf16[16,4,8,8,768]{4,3,2,1,0:T(8,128)(2,1)} %cpl_ref.5) | copy-start | bytes 18874372
  23.7 8.8 %collective-permute-start.7 = (f32[48,768]{1,0:T(8,128)S(1)}, f32[48,768]{1,0:T(8,128)S(1)}, u32[]{:S(2)}, u32[]{:S(2)}) collective-permute-start(f32[48,768]{1,0:T(8,128)S(1)} %get-tuple-element.15), channel_id=1, source_target_pairs={{1,2},{2,1},{3,4},{4,3},{5,6},{6,5},{9,10},{10,9},{11,12},{12,11},... | collective-permute-start | bytes 442376 | tf_op jit(solution)/shard_map/ppermute | solution.py:210
  28.1 4.4 %collective-permute-start.6 = (f32[48,768]{1,0:T(8,128)S(1)}, f32[48,768]{1,0:T(8,128)S(1)}, u32[]{:S(2)}, u32[]{:S(2)}) collective-permute-start(f32[48,768]{1,0:T(8,128)S(1)} %get-tuple-element.15), channel_id=1, source_target_pairs={{0,1},{1,0},{2,3},{3,2},{4,5},{5,4},{6,7},{7,6},{8,9},{9,8},{10,11... | collective-permute-start | bytes 442376 | tf_op jit(solution)/shard_map/ppermute | solution.py:211
  28.2 4.3 %collective-permute-start.5 = (f32[48,768]{1,0:T(8,128)S(1)}, f32[48,768]{1,0:T(8,128)S(1)}, u32[]{:S(2)}, u32[]{:S(2)}) collective-permute-start(f32[48,768]{1,0:T(8,128)S(1)} %get-tuple-element.15), channel_id=1, source_target_pairs={{8,16},{16,8},{24,32},{32,24},{40,48},{48,40},{56,64},{64,56},{72,... | collective-permute-start | bytes 442376 | tf_op jit(solution)/shard_map/ppermute | solution.py:208
  28.8 7.1 %collective-permute-start.4 = (f32[48,768]{1,0:T(8,128)S(1)}, f32[48,768]{1,0:T(8,128)S(1)}, u32[]{:S(2)}, u32[]{:S(2)}) collective-permute-start(f32[48,768]{1,0:T(8,128)S(1)} %get-tuple-element.15), channel_id=1, source_target_pairs={{0,8},{8,0},{16,24},{24,16},{32,40},{40,32},{48,56},{56,48},{64,72... | collective-permute-start | bytes 442376 | tf_op jit(solution)/shard_map/ppermute | solution.py:209
  35.9 12.6 %copy-start.6 = (s32[1024,1]{0,1:T(1,128)S(1)}, s32[1024,1]{0,1:T(1,128)}, u32[]{:S(2)}) copy-start(s32[1024,1]{0,1:T(1,128)} %param.18) | copy-start | bytes 12292
  35.9 13.4 %copy-start.11 = (bf16[16,6,6,768]{3,0,2,1:T(8,128)(2,1)S(1)}, bf16[16,6,6,768]{3,0,2,1:T(8,128)(2,1)}, u32[]{:S(2)}) copy-start(bf16[16,6,6,768]{3,0,2,1:T(8,128)(2,1)} %param.16) | copy-start | bytes 2654212
  38.7 13.4 %copy-start.9 = (s32[1024]{0:T(1024)S(1)}, s32[1024]{0:T(1024)}, u32[]{:S(2)}) copy-start(s32[1024]{0:T(1024)} %param.17) | copy-start | bytes 12292
  38.7 13.4 %copy-start.10 = (s32[1024]{0:T(1024)S(1)}, s32[1024]{0:T(1024)}, u32[]{:S(2)}) copy-start(s32[1024]{0:T(1024)} %param.19) | copy-start | bytes 12292
  38.7 10.9 %collective-permute-start.11 = (f32[48,768]{1,0:T(8,128)S(1)}, f32[48,768]{1,0:T(8,128)S(1)}, u32[]{:S(2)}, u32[]{:S(2)}) collective-permute-start(f32[48,768]{1,0:T(8,128)S(1)} %get-tuple-element.17), channel_id=1, source_target_pairs={{1,2},{2,1},{3,4},{4,3},{5,6},{6,5},{9,10},{10,9},{11,12},{12,11},... | collective-permute-start | bytes 442376 | tf_op jit(solution)/shard_map/ppermute | solution.py:210
  42.7 6.9 %collective-permute-start.10 = (f32[48,768]{1,0:T(8,128)S(1)}, f32[48,768]{1,0:T(8,128)S(1)}, u32[]{:S(2)}, u32[]{:S(2)}) collective-permute-start(f32[48,768]{1,0:T(8,128)S(1)} %get-tuple-element.17), channel_id=1, source_target_pairs={{0,1},{1,0},{2,3},{3,2},{4,5},{5,4},{6,7},{7,6},{8,9},{9,8},{10,11... | collective-permute-start | bytes 442376 | tf_op jit(solution)/shard_map/ppermute | solution.py:211
  42.8 6.8 %collective-permute-start.9 = (f32[48,768]{1,0:T(8,128)S(1)}, f32[48,768]{1,0:T(8,128)S(1)}, u32[]{:S(2)}, u32[]{:S(2)}) collective-permute-start(f32[48,768]{1,0:T(8,128)S(1)} %get-tuple-element.17), channel_id=1, source_target_pairs={{8,16},{16,8},{24,32},{32,24},{40,48},{48,40},{56,64},{64,56},{72,... | collective-permute-start | bytes 442376 | tf_op jit(solution)/shard_map/ppermute | solution.py:208
  43.5 8.5 %collective-permute-start.8 = (f32[48,768]{1,0:T(8,128)S(1)}, f32[48,768]{1,0:T(8,128)S(1)}, u32[]{:S(2)}, u32[]{:S(2)}) collective-permute-start(f32[48,768]{1,0:T(8,128)S(1)} %get-tuple-element.17), channel_id=1, source_target_pairs={{0,8},{8,0},{16,24},{24,16},{32,40},{40,32},{48,56},{56,48},{64,72... | collective-permute-start | bytes 442376 | tf_op jit(solution)/shard_map/ppermute | solution.py:209
  60.0 23.4 %all-to-all-start = ((f32[32,8,128]{2,1,0:T(8,128)}), f32[32,8,128]{2,1,0:T(8,128)S(1)}, u32[]{:S(2)}, u32[]{:S(2)}) async-start(f32[32,8,128]{2,1,0:T(8,128)} %get-tuple-element.20), calls=%async_computation | async-start | bytes 262144 | tf_op jit(solution)/shard_map/all_to_all | solution.py:278

commit v2 on v1

--- a/solution.py
+++ b/solution.py
@@ -17,7 +17,6 @@
 BF16 = jnp.bfloat16
 
 VMEM = pl.BlockSpec(memory_space=pltpu.VMEM)
-SMEM = pl.BlockSpec(memory_space=pltpu.SMEM)
 
 
 def solve_tile(t, resid, inv_ref, live):
@@ -35,13 +34,41 @@
         sent_ref[NVAR * s : NVAR * (s + 1), :] = tile[:NVAR]
 
 
-def first_kernel(send_ref, count_ref, rhs_ref, inv_ref, adj_ref, sent_ref):
+def fetch(pairs, sems):
+    copies = [pltpu.make_async_copy(src, dst, sems.at[i]) for i, (src, dst) in enumerate(pairs)]
+    for copy in copies:
+        copy.start()
+    return copies
+
+
+def first_kernel(
+    send_hbm, count_ref, rhs_hbm, inv_hbm, adj_ref, sent_ref, rhs_ref, inv_ref, send_ref, sems, table_sems
+):
+    (send_copy,) = fetch(((send_hbm, send_ref),), table_sems)
     tiles = rhs_ref.shape[0]
-
-    @pl.loop(0, tiles)
-    def _(t):
-        out = solve_tile(t, rhs_ref.at[t], inv_ref, t < count_ref[0])
-        adj_ref[pl.ds(pl.multiple_of(t * 8, 8), 8), :] = out
+    parts = sems.shape[0]
+    step = tiles // parts
+    copies = []
+    for p in range(parts):
+        some = pl.ds(p * step, step)
+        copies.append(
+            (
+                pltpu.make_async_copy(rhs_hbm.at[some], rhs_ref.at[some], sems.at[p, 0]),
+                pltpu.make_async_copy(inv_hbm.at[some], inv_ref.at[some], sems.at[p, 1]),
+            )
+        )
+    for pair in copies:
+        for copy in pair:
+            copy.start()
+    send_copy.wait()
+    for p, pair in enumerate(copies):
+        for copy in pair:
+            copy.wait()
+
+        @pl.loop(p * step, (p + 1) * step)
+        def _(t):
+            out = solve_tile(t, rhs_ref.at[t], inv_ref, t < count_ref[0])
+            adj_ref[pl.ds(pl.multiple_of(t * 8, 8), 8), :] = out
 
     pack_sent(adj_ref, send_ref, sent_ref)
 
@@ -51,7 +78,7 @@
     ext_ref[:own, :] = old_ref[...]
     odd_region = lax.axis_index("region") % 2
     odd_sub = lax.axis_index("sub") % 2
-    places = (1 - odd_region, odd_region, 3 - odd_sub, 2 + odd_sub)
+    places = (3 - odd_sub, 1 - odd_region, 2 + odd_sub, odd_region)
     width = halo_refs[0].shape[0]
     for place, halo in zip(places, halo_refs):
         ext_ref[pl.ds(pl.multiple_of(own + place * width, 8), width), :] = halo[...]
@@ -61,7 +88,7 @@
     own = rhs_ref.shape[0]
     acc = rhs_ref[t]
     for k in range(cpl_ref.shape[1]):
-        tile = near_ref[t, k]
+        tile = near_ref[k, t]
         base = jnp.where(tile < own, tile * 8, tile * NVAR + own * (8 - NVAR))
         for m in range(NVAR):
             acc = acc - cpl_ref[t, k, m].astype(F32) * ext_ref[pl.ds(base + m, 1), :]
@@ -70,10 +97,14 @@
 
 
 def sweep_kernel(
-    near_ref, send_ref, count_ref, rhs_ref, inv_ref, cpl_ref, old_ref, h0, h1, h2, h3,
-    adj_ref, sent_ref, ext_ref, resid_ref,
+    near_hbm, send_hbm, count_ref, rhs_ref, inv_ref, cpl_ref, old_ref, h0, h1, h2, h3,
+    adj_ref, sent_ref, ext_ref, resid_ref, near_ref, send_ref, table_sems,
 ):
+    tables = ((near_hbm, near_ref), (send_hbm, send_ref))
+    copies = fetch(tables, table_sems)
     build_extended(old_ref, (h0, h1, h2, h3), ext_ref)
+    for copy in copies:
+        copy.wait()
 
     @pl.loop(0, rhs_ref.shape[0])
     def _(t):
@@ -83,47 +114,86 @@
     pack_sent(adj_ref, send_ref, sent_ref)
 
 
+def sweep_load_kernel(
+    near_hbm, send_hbm, count_ref, rhs_ref, inv_ref, cpl_hbm, old_ref, h0, h1, h2, h3,
+    adj_ref, sent_ref, cpl_ref, ext_ref, resid_ref, near_ref, send_ref, table_sems, sems,
+):
+    tables = fetch(((near_hbm, near_ref), (send_hbm, send_ref)), table_sems)
+    tiles = rhs_ref.shape[0]
+    parts = sems.shape[0]
+    step = tiles // parts
+    copies = [
+        pltpu.make_async_copy(
+            cpl_hbm.at[pl.ds(p * step, step)], cpl_ref.at[pl.ds(p * step, step)], sems.at[p]
+        )
+        for p in range(parts)
+    ]
+    for copy in copies:
+        copy.start()
+    build_extended(old_ref, (h0, h1, h2, h3), ext_ref)
+    for copy in tables:
+        copy.wait()
+    for p, copy in enumerate(copies):
+        copy.wait()
+
+        @pl.loop(p * step, (p + 1) * step)
+        def _(t):
+            out = pull_and_solve(t, near_ref, count_ref, rhs_ref, inv_ref, cpl_ref, ext_ref, resid_ref)
+            adj_ref[pl.ds(pl.multiple_of(t * 8, 8), 8), :] = out
+
+    pack_sent(adj_ref, send_ref, sent_ref)
+
+
 def last_kernel(
-    near_ref, count_ref, rhs_ref, inv_ref, cpl_ref, hess_ref, old_ref, h0, h1, h2, h3,
+    near_hbm, count_ref, rhs_ref, inv_ref, cpl_ref, hess_ref, old_ref, h0, h1, h2, h3,
     vertex_ref, region_ref, slot_ref, rank_hot_ref,
-    adj_ref, metric_ref, parcel_ref, ext_ref, resid_ref, abs_ref, table_ref, gathered_ref,
+    adj_ref, metric_ref, parcel_ref, ext_ref, resid_ref, column_ref, gathered_ref, near_ref, table_sems,
 ):
+    copies = fetch(((near_hbm, near_ref),), table_sems)
     build_extended(old_ref, (h0, h1, h2, h3), ext_ref)
+    for copy in copies:
+        copy.wait()
     tiles, width = rhs_ref.shape[0], rhs_ref.shape[2]
     chunks = width // LANES
 
     @pl.loop(0, tiles)
     def _(t):
         out = pull_and_solve(t, near_ref, count_ref, rhs_ref, inv_ref, cpl_ref, ext_ref, resid_ref)
-        adj_ref[t] = out
-        abs_ref[...] = jnp.abs(out)
-        total = None
+        here = pl.ds(pl.multiple_of(t * 8, 8), 8)
+        adj_ref[here, :] = out
+        for q in range(chunks):
+            column_ref[q, here, :] = jnp.abs(out[:, q * LANES : (q + 1) * LANES])
+
+    for q in range(chunks):
+        cols = slice(q * LANES, (q + 1) * LANES)
+        sums = [None] * 6
         for c in range(NVAR):
-            term = hess_ref[t, c].astype(F32) * abs_ref[pl.ds(c, 1), :]
-            total = term if total is None else total + term
-        metric_ref[t] = total
+            size = column_ref[q, pl.ds(c, tiles, stride=8), :]
+            for s in range(6):
+                term = hess_ref[c, s, :, cols].astype(F32) * size
+                sums[s] = term if sums[s] is None else sums[s] + term
+        for s in range(6):
+            metric_ref[s, :, cols] = sums[s]
+
+    entries = vertex_ref.shape[1]
+    in_tile = lax.broadcasted_iota(jnp.int32, (8, LANES), 0)
+
+    @pl.loop(0, entries // LANES)
+    def _(g):
+        here = pl.ds(pl.multiple_of(g * LANES, LANES), LANES)
+        vertex = vertex_ref[:, here]
+        row = jnp.broadcast_to(vertex // LANES, (8, LANES))
+        lane = jnp.broadcast_to(vertex % LANES, (8, LANES))
+        sums = [jnp.zeros((8, LANES), F32)] * 6
         for q in range(chunks):
-            table_ref[t * chunks + q, :NVAR, :] = total[:, q * LANES : (q + 1) * LANES]
-
-    vertex = vertex_ref[...]
-    entries = vertex.shape[1]
-    groups = entries // LANES
-    row = vertex // LANES
-    lane = vertex % LANES
-    rows_b = [jnp.broadcast_to(row[:, g * LANES : (g + 1) * LANES], (8, LANES)) for g in range(groups)]
-    lanes_b = [jnp.broadcast_to(lane[:, g * LANES : (g + 1) * LANES], (8, LANES)) for g in range(groups)]
-
-    def pick(r, totals):
-        block = table_ref[r]
-        return tuple(
-            jnp.where(rows_b[g] == r, jnp.take_along_axis(block, lanes_b[g], axis=1), totals[g])
-            for g in range(groups)
-        )
-
-    zero = jnp.zeros((8, LANES), F32)
-    totals = lax.fori_loop(0, tiles * chunks, pick, (zero,) * groups, unroll=4)
-    for g in range(groups):
-        gathered_ref[:, g * LANES : (g + 1) * LANES] = totals[g]
+            for h in range(tiles // 8):
+                mine = row == (in_tile + h * 8) * chunks + q
+                for s in range(6):
+                    block = metric_ref[s, h * 8 : (h + 1) * 8, q * LANES : (q + 1) * LANES]
+                    sums[s] = jnp.where(mine, jnp.take_along_axis(block, lane, axis=1), sums[s])
+        for s in range(6):
+            gathered_ref[s : s + 1, here] = jnp.sum(sums[s], axis=0, keepdims=True)
+
     values = gathered_ref[...]
     which = lax.broadcasted_iota(jnp.int32, values.shape, 0)
     values = jnp.where(which == NVAR, slot_ref[...].astype(F32), jnp.where(which < NVAR, values, 0.0))
@@ -209,7 +279,7 @@
     got_ra = lax.ppermute(sent, *ra)
     got_sb = lax.ppermute(sent, *sb)
     got_sa = lax.ppermute(sent, *sa)
-    return got_ra, got_rb, got_sa, got_sb
+    return got_sa, got_ra, got_sb, got_rb
 
 
 def per_device(
@@ -220,8 +290,11 @@
     entries = shared_vertex.shape[0]
     regions = lax.axis_size("region")
     params = pltpu.CompilerParams(vmem_limit_bytes=40 * 2**20)
-    near = pltpu.with_memory_space_constraint(coupling, pltpu.VMEM)
-    coupling = near
+    rhs = pltpu.with_memory_space_constraint(rhs, pltpu.HBM)
+    diag_inv = pltpu.with_memory_space_constraint(diag_inv, pltpu.HBM)
+    coupling = pltpu.with_memory_space_constraint(coupling, pltpu.HBM)
+    neighbours = pltpu.with_memory_space_constraint(neighbours.T, pltpu.HBM)
+    send_tiles = pltpu.with_memory_space_constraint(send_tiles, pltpu.HBM)
     vertex = shared_vertex.reshape(1, entries)
     dest = owner_region.reshape(1, entries)
     slot = owner_slot.reshape(1, entries)
@@ -230,12 +303,22 @@
     sent_shape = jax.ShapeDtypeStruct((sends * NVAR, width), F32)
     ext = pltpu.VMEM((tiles * 8 + 4 * sends * NVAR, width), F32)
     resid = pltpu.VMEM((8, width), F32)
-
-    adjoint, sent = pl.pallas_call(
+    hbm = pl.BlockSpec(memory_space=pltpu.HBM)
+    smem = pl.BlockSpec(memory_space=pltpu.SMEM)
+    near_table = pltpu.SMEM(neighbours.shape, jnp.int32)
+    send_table = pltpu.SMEM(send_tiles.shape, jnp.int32)
+
+    adjoint, sent, rhs, diag_inv = pl.pallas_call(
         first_kernel,
-        out_shape=(adj_shape, sent_shape),
-        in_specs=[SMEM, SMEM, VMEM, VMEM],
-        out_specs=(VMEM, VMEM),
+        out_shape=(
+            adj_shape,
+            sent_shape,
+            jax.ShapeDtypeStruct(rhs.shape, rhs.dtype),
+            jax.ShapeDtypeStruct(diag_inv.shape, diag_inv.dtype),
+        ),
+        in_specs=[hbm, smem, hbm, hbm],
+        out_specs=(VMEM,) * 4,
+        scratch_shapes=[send_table, pltpu.SemaphoreType.DMA((4, 2)), pltpu.SemaphoreType.DMA((1,))],
         compiler_params=params,
     )(send_tiles, tile_count, rhs, diag_inv)
     rank_hot = pl.pallas_call(
@@ -246,35 +329,53 @@
         scratch_shapes=[pltpu.VMEM((1, entries), F32)],
         compiler_params=params,
     )(dest)
-    for sweep in range(SWEEPS - 1):
+    halos = exchange(sent)
+    adjoint, sent, coupling = pl.pallas_call(
+        sweep_load_kernel,
+        out_shape=(adj_shape, sent_shape, jax.ShapeDtypeStruct(coupling.shape, coupling.dtype)),
+        in_specs=[hbm, hbm, smem] + [VMEM] * 2 + [hbm] + [VMEM] * 5,
+        out_specs=(VMEM,) * 3,
+        scratch_shapes=[
+            ext, resid, near_table, send_table,
+            pltpu.SemaphoreType.DMA((2,)), pltpu.SemaphoreType.DMA((8,)),
+        ],
+        compiler_params=params,
+    )(neighbours, send_tiles, tile_count, rhs, diag_inv, coupling, adjoint, *halos)
+    for sweep in range(SWEEPS - 2):
         halos = exchange(sent)
         adjoint, sent = pl.pallas_call(
             sweep_kernel,
             out_shape=(adj_shape, sent_shape),
-            in_specs=[SMEM] * 3 + [VMEM] * 8,
+            in_specs=[hbm, hbm, smem] + [VMEM] * 8,
             out_specs=(VMEM, VMEM),
-            scratch_shapes=[ext, resid],
+            scratch_shapes=[ext, resid, near_table, send_table, pltpu.SemaphoreType.DMA((2,))],
             compiler_params=params,
         )(neighbours, send_tiles, tile_count, rhs, diag_inv, coupling, adjoint, *halos)
     halos = exchange(sent)
     out, metric, parcels = pl.pallas_call(
         last_kernel,
         out_shape=(
-            jax.ShapeDtypeStruct((tiles, block, width), F32),
-            jax.ShapeDtypeStruct((tiles, 6, width), F32),
+            adj_shape,
+            jax.ShapeDtypeStruct((6, tiles, width), F32),
             jax.ShapeDtypeStruct((regions, 8, CAP), F32),
         ),
-        in_specs=[SMEM] * 2 + [VMEM] * 13,
+        in_specs=[hbm, smem] + [VMEM] * 13,
         out_specs=(VMEM, VMEM, VMEM),
         scratch_shapes=[
             ext,
             resid,
-            pltpu.VMEM((8, width), F32),
-            pltpu.VMEM((tiles * width // LANES, 8, LANES), F32),
+            pltpu.VMEM((width // LANES, tiles * 8, LANES), F32),
             pltpu.VMEM((8, entries), F32),
+            near_table,
+            pltpu.SemaphoreType.DMA((1,)),
         ],
         compiler_params=params,
-    )(neighbours, tile_count, rhs, diag_inv, coupling, hessian, adjoint, *halos, vertex, dest, slot, rank_hot)
+    )(
+        neighbours, tile_count, rhs, diag_inv, coupling, hessian.transpose(1, 2, 0, 3), adjoint, *halos,
+        vertex, dest, slot, rank_hot,
+    )
+    out = out.reshape(tiles, block, width)
+    metric = metric.transpose(1, 0, 2)
     parcels = lax.all_to_all(parcels, "region", 0, 0, tiled=True)
     owned = pl.pallas_call(
         owner_kernel,

time: 85.5 us -> 73.7 us (0.86)
  blocking collectives: 0 us -> 22.1 us
  starting transfers between devices: 41.8 us -> 27.5 us
  waiting for transfers between devices: 17.8 us -> 6.84 us
  local copies, waits for them, and re-layouts: 7.03 us -> 0.03 us
  Pallas kernels: 16.4 us -> 14.7 us
    all_to_all x0 -> x1, blocking collectives: none -> 22.1 us  [per_device(): parcels = lax.all_to_all(parcels, 'region', 0, 0, tiled=True)]
    all_to_all x1 -> x0, starting transfers between devices: 14 us -> none  [per_device(): parcels = lax.all_to_all(parcels, 'region', 0, 0, tiled=True)]
    all_to_all x1 -> x0, waiting for transfers between devices: 8.54 us -> none  [per_device(): parcels = lax.all_to_all(parcels, 'region', 0, 0, tiled=True)]
    unnamed x29 -> x8, local copies, waits for them, and re-layouts: 7.03 us -> 0.03 us
    pallas_call x2 -> x1, Pallas kernels: 5.43 us -> 2.71 us  [per_device(): pl.pallas_call(sweep_kernel, out_shape=(adj_shape, sent_shape), in_specs=...]
    ppermute x3, waiting for transfers between devices: 9.24 us -> 6.81 us  [exchange(): got_ra = lax.ppermute(sent, *ra)]
    ppermute x3, starting transfers between devices: 12.9 us -> 11.1 us  [exchange(): got_sb = lax.ppermute(sent, *sb)]
    ppermute x3, starting transfers between devices: 12.6 us -> 14.2 us  [exchange(): got_ra = lax.ppermute(sent, *ra)]
  transfers between devices with their start and end apart: 13 -> 12, of which waited for: 4 -> 3; matrix products, arithmetic and copies ran while one was open for 1% -> 0% of each run, Pallas kernels for 1% -> 1%
where the time goes in v2:
time: 73.7 us; the launch traced here: 72.6 us
  starting transfers between devices  27.5 us (37%)
  blocking collectives  22.1 us (30%)
  Pallas kernels  14.7 us (20%)
  waiting for transfers between devices  6.84 us (9%)
  between operations  1.44 us (2%)
    all_to_all x1, blocking collectives, per_device(): parcels = lax.all_to_all(parcels, 'region', 0, 0, tiled=True)  22.1 us
    ppermute x3, starting transfers between devices, exchange(): got_ra = lax.ppermute(sent, *ra)  14.2 us
    ppermute x3, starting transfers between devices, exchange(): got_sb = lax.ppermute(sent, *sb)  11.1 us
    ppermute x3, waiting for transfers between devices, exchange(): got_ra = lax.ppermute(sent, *ra)  6.81 us
    pallas_call x1, Pallas kernels, per_device(): pl.pallas_call(last_kernel, out_shape=(adj_shape, jax.ShapeDtypeStruct((6...  5.15 us
    pallas_call x1, Pallas kernels, per_device(): pl.pallas_call(sweep_load_kernel, out_shape=(adj_shape, sent_shape, jax.S...  3.21 us
    pallas_call x1, Pallas kernels, per_device(): pl.pallas_call(sweep_kernel, out_shape=(adj_shape, sent_shape), in_specs=...  2.71 us
    ppermute x3, starting transfers between devices, exchange(): got_rb = lax.ppermute(sent, *rb)  2.14 us
  transfers between devices with their start and end apart: 12, of which 3 were waited for; matrix products, arithmetic and copies ran while one was open for 0% of the time, Pallas kernels for 1%

profile of v2, /device:TPU:1, one launch (start us, length us, event | category | flops | bytes accessed | tf_op | source)
XLA Modules:
  0.0 72.6 jit_solution(10243778013080301915)
XLA Ops:
  1.3 1.8 %shard_map.121 = (f32[128,768]{1,0:T(8,128)S(1)}, f32[48,768]{1,0:T(8,128)S(1)}, f32[16,8,768]{2,1,0:T(8,128)S(1)}, bf16[16,8,8,768]{3,2,1,0:T(8,128)(2,1)S(1)}) custom-call(s32[1,8]{1,0:T(1,128)} %send_hbm.5, s32[1]{0:T(128)S(6)} %copy.13.count_ref, f32[16,8,768]{2,1,0:T(8,128)} %rhs_hbm.1, bf16[16,8,8,768]{3,2,1,0:T(8,128)(2,1)} %inv_hbm.1), custom_call_target="tpu_custom_call" | custom-call | tf_op jit(solution)/shard_map/pallas_call | solution.py:311
  3.0 0.7 collective-permute-start.3
  3.7 4.5 %collective-permute-start.2 = (f32[48,768]{1,0:T(8,128)S(1)}, f32[48,768]{1,0:T(8,128)S(1)}, u32[]{:S(2)}, u32[]{:S(2)}) collective-permute-start(f32[48,768]{1,0:T(8,128)S(1)} %get-tuple-element.18), channel_id=1, source_target_pairs={{1,2},{2,1},{3,4},{4,3},{5,6},{6,5},{9,10},{10,9},{11,12},{12,11},... | collective-permute-start | bytes 442376 | tf_op jit(solution)/shard_map/ppermute | solution.py:280
  8.2 4.2 %collective-permute-start.1 = (f32[48,768]{1,0:T(8,128)S(1)}, f32[48,768]{1,0:T(8,128)S(1)}, u32[]{:S(2)}, u32[]{:S(2)}) collective-permute-start(f32[48,768]{1,0:T(8,128)S(1)} %get-tuple-element.18), channel_id=1, source_target_pairs={{0,8},{8,0},{16,24},{24,16},{32,40},{40,32},{48,56},{56,48},{64,72... | collective-permute-start | bytes 442376 | tf_op jit(solution)/shard_map/ppermute | solution.py:279
  12.4 0.0 collective-permute-start
  12.4 0.0 collective-permute-done.3.h3
  12.4 0.0 collective-permute-done.2.h2
  12.4 2.5 %collective-permute-done.1.h1 = f32[48,768]{1,0:T(8,128)S(1)} collective-permute-done((f32[48,768]{1,0:T(8,128)S(1)}, f32[48,768]{1,0:T(8,128)S(1)}, u32[]{:S(2)}, u32[]{:S(2)}) %collective-permute-start.1) | collective-permute-done | bytes 147488 | tf_op jit(solution)/shard_map/ppermute | solution.py:279
  15.0 0.0 collective-permute-done.h0
  15.0 3.2 %shard_map.122 = (f32[128,768]{1,0:T(8,128)S(1)}, f32[48,768]{1,0:T(8,128)S(1)}, bf16[16,4,8,8,768]{4,3,2,1,0:T(8,128)(2,1)S(1)}) custom-call(s32[4,16]{1,0:T(4,128)} %bitcast.12, s32[1,8]{1,0:T(1,128)} %send_hbm.5, s32[1]{0:T(128)S(6)} %copy.13.count_ref, f32[16,8,768]{2,1,0:T(8,128)S(1)} %get-tuple-element.15.rhs_ref, ...), custom_call_target="tpu_custom_call" | custom-call | tf_op jit(solution)/shard_map/pallas_call | solution.py:333
  18.2 0.0 copy-start.1
  18.2 0.0 copy-start
  18.2 0.0 copy-start.2
  18.2 0.0 copy-start.3
  18.2 0.8 %collective-permute-start.7 = (f32[48,768]{1,0:T(8,128)S(1)}, f32[48,768]{1,0:T(8,128)S(1)}, u32[]{:S(2)}, u32[]{:S(2)}) collective-permute-start(f32[48,768]{1,0:T(8,128)S(1)} %get-tuple-element.21), channel_id=1, source_target_pairs={{8,16},{16,8},{24,32},{32,24},{40,48},{48,40},{56,64},{64,56},{72,... | collective-permute-start | bytes 442376 | tf_op jit(solution)/shard_map/ppermute | solution.py:278
  19.0 3.5 %collective-permute-start.6 = (f32[48,768]{1,0:T(8,128)S(1)}, f32[48,768]{1,0:T(8,128)S(1)}, u32[]{:S(2)}, u32[]{:S(2)}) collective-permute-start(f32[48,768]{1,0:T(8,128)S(1)} %get-tuple-element.21), channel_id=1, source_target_pairs={{1,2},{2,1},{3,4},{4,3},{5,6},{6,5},{9,10},{10,9},{11,12},{12,11},... | collective-permute-start | bytes 442376 | tf_op jit(solution)/shard_map/ppermute | solution.py:280
  22.5 3.9 %collective-permute-start.5 = (f32[48,768]{1,0:T(8,128)S(1)}, f32[48,768]{1,0:T(8,128)S(1)}, u32[]{:S(2)}, u32[]{:S(2)}) collective-permute-start(f32[48,768]{1,0:T(8,128)S(1)} %get-tuple-element.21), channel_id=1, source_target_pairs={{0,8},{8,0},{16,24},{24,16},{32,40},{40,32},{48,56},{56,48},{64,72... | collective-permute-start | bytes 442376 | tf_op jit(solution)/shard_map/ppermute | solution.py:279
  26.4 0.0 collective-permute-start.4
  26.4 0.0 collective-permute-done.7.h3
  26.4 0.0 collective-permute-done.6.h2
  26.4 2.5 %collective-permute-done.5.h1 = f32[48,768]{1,0:T(8,128)S(1)} collective-permute-done((f32[48,768]{1,0:T(8,128)S(1)}, f32[48,768]{1,0:T(8,128)S(1)}, u32[]{:S(2)}, u32[]{:S(2)}) %collective-permute-start.5) | collective-permute-done | bytes 147488 | tf_op jit(solution)/shard_map/ppermute | solution.py:279
  29.0 0.0 collective-permute-done.4.h0
  29.0 2.7 %shard_map.123 = (f32[128,768]{1,0:T(8,128)S(1)}, f32[48,768]{1,0:T(8,128)S(1)}) custom-call(s32[4,16]{1,0:T(4,128)} %bitcast.13, s32[1,8]{1,0:T(1,128)} %send_hbm.5, s32[1]{0:T(128)S(6)} %copy.13.count_ref, f32[16,8,768]{2,1,0:T(8,128)S(1)} %get-tuple-element.15.rhs_ref, bf16[16,8,8,768]{3,2,1,0:T(8,128)(2,1)S(1)} %get-tuple-element.16.inv_ref, ...), custom_call_target="tpu_custom_call" | custom-call | tf_op jit(solution)/shard_map/pallas_call | solution.py:346
  31.7 0.7 collective-permute-start.11
  32.4 3.1 %collective-permute-start.10 = (f32[48,768]{1,0:T(8,128)S(1)}, f32[48,768]{1,0:T(8,128)S(1)}, u32[]{:S(2)}, u32[]{:S(2)}) collective-permute-start(f32[48,768]{1,0:T(8,128)S(1)} %get-tuple-element.23), channel_id=1, source_target_pairs={{1,2},{2,1},{3,4},{4,3},{5,6},{6,5},{9,10},{10,9},{11,12},{12,11},... | collective-permute-start | bytes 442376 | tf_op jit(solution)/shard_map/ppermute | solution.py:280
  35.5 6.1 %collective-permute-start.9 = (f32[48,768]{1,0:T(8,128)S(1)}, f32[48,768]{1,0:T(8,128)S(1)}, u32[]{:S(2)}, u32[]{:S(2)}) collective-permute-start(f32[48,768]{1,0:T(8,128)S(1)} %get-tuple-element.23), channel_id=1, source_target_pairs={{0,8},{8,0},{16,24},{24,16},{32,40},{40,32},{48,56},{56,48},{64,72... | collective-permute-start | bytes 442376 | tf_op jit(solution)/shard_map/ppermute | solution.py:279
  41.6 0.7 %shard_map.124.rank_hot_ref = bf16[128,1024]{1,0:T(8,128)(2,1)S(1)} custom-call(s32[1,1024]{1,0:T(1,128)S(1)} %bitcast.8), custom_call_target="tpu_custom_call" | custom-call | tf_op jit(solution)/shard_map/pallas_call | solution.py:324
  42.4 0.0 collective-permute-done.10.h2
  42.4 1.8 %collective-permute-done.9.h1 = f32[48,768]{1,0:T(8,128)S(1)} collective-permute-done((f32[48,768]{1,0:T(8,128)S(1)}, f32[48,768]{1,0:T(8,128)S(1)}, u32[]{:S(2)}, u32[]{:S(2)}) %collective-permute-start.9) | collective-permute-done | bytes 147488 | tf_op jit(solution)/shard_map/ppermute | solution.py:279
  44.2 5.2 %shard_map.125 = (f32[128,768]{1,0:T(8,128)}, f32[6,16,768]{2,1,0:T(8,128)}, f32[32,8,128]{2,1,0:T(8,128)S(1)}) custom-call(s32[4,16]{1,0:T(4,128)} %bitcast.14, s32[1]{0:T(128)S(6)} %copy.13.count_ref, f32[16,8,768]{2,1,0:T(8,128)S(1)} %get-tuple-element.15.rhs_ref, bf16[16,8,8,768]{3,2,1,0:T(8,128)(2,1)S(1)} %get-tuple-element.16.inv_ref, ...), custom_call_target="tpu_custom_call" | custom-call | tf_op jit(solution)/shard_map/pallas_call | solution.py:355
  49.3 22.1 %all_to_all.5.parcel_ref = f32[32,8,128]{2,1,0:T(8,128)S(1)} all-to-all(f32[32,8,128]{2,1,0:T(8,128)S(1)} %get-tuple-element.26), channel_id=1, replica_groups=mesh['region'=32,'sub'=8] {'region'}, dimensions={0} | all-to-all | bytes 262144 | tf_op jit(solution)/shard_map/all_to_all | solution.py:379
  71.4 1.2 %shard_map.126 = f32[6,1024]{1,0:T(8,128)} custom-call(f32[32,8,128]{2,1,0:T(8,128)S(1)} %all_to_all.5.parcel_ref), custom_call_target="tpu_custom_call" | custom-call | tf_op jit(solution)/shard_map/pallas_call | solution.py:380
  (7 shorter events, 0.0 us)
Async XLA Ops:
  3.0 9.4 %collective-permute-start.3 = (f32[48,768]{1,0:T(8,128)S(1)}, f32[48,768]{1,0:T(8,128)S(1)}, u32[]{:S(2)}, u32[]{:S(2)}) collective-permute-start(f32[48,768]{1,0:T(8,128)S(1)} %get-tuple-element.18), channel_id=1, source_target_pairs={{8,16},{16,8},{24,32},{32,24},{40,48},{48,40},{56,64},{64,56},{72,... | collective-permute-start | bytes 442376 | tf_op jit(solution)/shard_map/ppermute | solution.py:278
  3.7 8.7 %collective-permute-start.2 = (f32[48,768]{1,0:T(8,128)S(1)}, f32[48,768]{1,0:T(8,128)S(1)}, u32[]{:S(2)}, u32[]{:S(2)}) collective-permute-start(f32[48,768]{1,0:T(8,128)S(1)} %get-tuple-element.18), channel_id=1, source_target_pairs={{1,2},{2,1},{3,4},{4,3},{5,6},{6,5},{9,10},{10,9},{11,12},{12,11},... | collective-permute-start | bytes 442376 | tf_op jit(solution)/shard_map/ppermute | solution.py:280
  8.2 6.7 %collective-permute-start.1 = (f32[48,768]{1,0:T(8,128)S(1)}, f32[48,768]{1,0:T(8,128)S(1)}, u32[]{:S(2)}, u32[]{:S(2)}) collective-permute-start(f32[48,768]{1,0:T(8,128)S(1)} %get-tuple-element.18), channel_id=1, source_target_pairs={{0,8},{8,0},{16,24},{24,16},{32,40},{40,32},{48,56},{56,48},{64,72... | collective-permute-start | bytes 442376 | tf_op jit(solution)/shard_map/ppermute | solution.py:279
  12.4 2.5 %collective-permute-start = (f32[48,768]{1,0:T(8,128)S(1)}, f32[48,768]{1,0:T(8,128)S(1)}, u32[]{:S(2)}, u32[]{:S(2)}) collective-permute-start(f32[48,768]{1,0:T(8,128)S(1)} %get-tuple-element.18), channel_id=1, source_target_pairs={{0,1},{1,0},{2,3},{3,2},{4,5},{5,4},{6,7},{7,6},{8,9},{9,8},{10,11... | collective-permute-start | bytes 442376 | tf_op jit(solution)/shard_map/ppermute | solution.py:281
  18.2 23.4 %copy-start.1 = (s32[1024,1]{0,1:T(1,128)S(1)}, s32[1024,1]{0,1:T(1,128)}, u32[]{:S(2)}) copy-start(s32[1024,1]{0,1:T(1,128)} %param.18) | copy-start | bytes 12292
  18.2 25.9 %copy-start = (bf16[16,6,6,768]{3,0,2,1:T(8,128)(2,1)S(1)}, bf16[16,6,6,768]{3,0,2,1:T(8,128)(2,1)}, u32[]{:S(2)}) copy-start(bf16[16,6,6,768]{3,0,2,1:T(8,128)(2,1)} %param.16) | copy-start | bytes 2654212
  18.2 25.9 %copy-start.2 = (s32[1024]{0:T(1024)S(1)}, s32[1024]{0:T(1024)}, u32[]{:S(2)}) copy-start(s32[1024]{0:T(1024)} %param.17) | copy-start | bytes 12292
  18.2 25.9 %copy-start.3 = (s32[1024]{0:T(1024)S(1)}, s32[1024]{0:T(1024)}, u32[]{:S(2)}) copy-start(s32[1024]{0:T(1024)} %param.19) | copy-start | bytes 12292
  18.2 8.2 %collective-permute-start.7 = (f32[48,768]{1,0:T(8,128)S(1)}, f32[48,768]{1,0:T(8,128)S(1)}, u32[]{:S(2)}, u32[]{:S(2)}) collective-permute-start(f32[48,768]{1,0:T(8,128)S(1)} %get-tuple-element.21), channel_id=1, source_target_pairs={{8,16},{16,8},{24,32},{32,24},{40,48},{48,40},{56,64},{64,56},{72,... | collective-permute-start | bytes 442376 | tf_op jit(solution)/shard_map/ppermute | solution.py:278
  19.0 7.4 %collective-permute-start.6 = (f32[48,768]{1,0:T(8,128)S(1)}, f32[48,768]{1,0:T(8,128)S(1)}, u32[]{:S(2)}, u32[]{:S(2)}) collective-permute-start(f32[48,768]{1,0:T(8,128)S(1)} %get-tuple-element.21), channel_id=1, source_target_pairs={{1,2},{2,1},{3,4},{4,3},{5,6},{6,5},{9,10},{10,9},{11,12},{12,11},... | collective-permute-start | bytes 442376 | tf_op jit(solution)/shard_map/ppermute | solution.py:280
  22.5 6.4 %collective-permute-start.5 = (f32[48,768]{1,0:T(8,128)S(1)}, f32[48,768]{1,0:T(8,128)S(1)}, u32[]{:S(2)}, u32[]{:S(2)}) collective-permute-start(f32[48,768]{1,0:T(8,128)S(1)} %get-tuple-element.21), channel_id=1, source_target_pairs={{0,8},{8,0},{16,24},{24,16},{32,40},{40,32},{48,56},{56,48},{64,72... | collective-permute-start | bytes 442376 | tf_op jit(solution)/shard_map/ppermute | solution.py:279
  26.4 2.5 %collective-permute-start.4 = (f32[48,768]{1,0:T(8,128)S(1)}, f32[48,768]{1,0:T(8,128)S(1)}, u32[]{:S(2)}, u32[]{:S(2)}) collective-permute-start(f32[48,768]{1,0:T(8,128)S(1)} %get-tuple-element.21), channel_id=1, source_target_pairs={{0,1},{1,0},{2,3},{3,2},{4,5},{5,4},{6,7},{7,6},{8,9},{9,8},{10,11... | collective-permute-start | bytes 442376 | tf_op jit(solution)/shard_map/ppermute | solution.py:281
  31.7 10.7 %collective-permute-start.11 = (f32[48,768]{1,0:T(8,128)S(1)}, f32[48,768]{1,0:T(8,128)S(1)}, u32[]{:S(2)}, u32[]{:S(2)}) collective-permute-start(f32[48,768]{1,0:T(8,128)S(1)} %get-tuple-element.23), channel_id=1, source_target_pairs={{8,16},{16,8},{24,32},{32,24},{40,48},{48,40},{56,64},{64,56},{72,... | collective-permute-start | bytes 442376 | tf_op jit(solution)/shard_map/ppermute | solution.py:278
  32.4 10.0 %collective-permute-start.10 = (f32[48,768]{1,0:T(8,128)S(1)}, f32[48,768]{1,0:T(8,128)S(1)}, u32[]{:S(2)}, u32[]{:S(2)}) collective-permute-start(f32[48,768]{1,0:T(8,128)S(1)} %get-tuple-element.23), channel_id=1, source_target_pairs={{1,2},{2,1},{3,4},{4,3},{5,6},{6,5},{9,10},{10,9},{11,12},{12,11},... | collective-permute-start | bytes 442376 | tf_op jit(solution)/shard_map/ppermute | solution.py:280
  35.5 8.7 %collective-permute-start.9 = (f32[48,768]{1,0:T(8,128)S(1)}, f32[48,768]{1,0:T(8,128)S(1)}, u32[]{:S(2)}, u32[]{:S(2)}) collective-permute-start(f32[48,768]{1,0:T(8,128)S(1)} %get-tuple-element.23), channel_id=1, source_target_pairs={{0,8},{8,0},{16,24},{24,16},{32,40},{40,32},{48,56},{56,48},{64,72... | collective-permute-start | bytes 442376 | tf_op jit(solution)/shard_map/ppermute | solution.py:279
  41.6 2.5 %collective-permute-start.8 = (f32[48,768]{1,0:T(8,128)S(1)}, f32[48,768]{1,0:T(8,128)S(1)}, u32[]{:S(2)}, u32[]{:S(2)}) collective-permute-start(f32[48,768]{1,0:T(8,128)S(1)} %get-tuple-element.23), channel_id=1, source_target_pairs={{0,1},{1,0},{2,3},{3,2},{4,5},{5,4},{6,7},{7,6},{8,9},{9,8},{10,11... | collective-permute-start | bytes 442376 | tf_op jit(solution)/shard_map/ppermute | solution.py:281

commit v3 on v2

--- a/solution.py
+++ b/solution.py
@@ -19,19 +19,31 @@
 VMEM = pl.BlockSpec(memory_space=pltpu.VMEM)
 
 
-def solve_tile(t, resid, inv_ref, live):
-    total = None
-    for j in range(inv_ref.shape[1]):
-        term = inv_ref[t, j].astype(F32) * resid[pl.ds(j, 1), :]
-        total = term if total is None else total + term
-    rows = lax.broadcasted_iota(jnp.int32, total.shape, 0)
-    return jnp.where((rows < NVAR) & live, total, 0.0)
+def lanes_of(q):
+    return slice(q * LANES, (q + 1) * LANES)
+
+
+def rows_of(t):
+    return pl.ds(pl.multiple_of(t * 8, 8), 8)
+
+
+def solve_tile(t, row_of, inv_ref, live):
+    keep = (lax.broadcasted_iota(jnp.int32, (8, LANES), 0) < NVAR) & live
+    blocks = []
+    for q in range(inv_ref.shape[3] // LANES):
+        total = None
+        for j in range(inv_ref.shape[1]):
+            term = inv_ref[t, j, :, lanes_of(q)].astype(F32) * row_of(q, j)
+            total = term if total is None else total + term
+        blocks.append(jnp.where(keep, total, 0.0))
+    return blocks
 
 
 def pack_sent(adj_ref, send_ref, sent_ref):
     for s in range(send_ref.shape[1]):
-        tile = adj_ref[pl.ds(pl.multiple_of(send_ref[0, s] * 8, 8), 8), :]
-        sent_ref[NVAR * s : NVAR * (s + 1), :] = tile[:NVAR]
+        here = rows_of(send_ref[0, s])
+        for q in range(adj_ref.shape[0]):
+            sent_ref[q, NVAR * s : NVAR * (s + 1), :] = adj_ref[q, here, :][:NVAR]
 
 
 def fetch(pairs, sems):
@@ -41,9 +53,7 @@
     return copies
 
 
-def first_kernel(
-    send_hbm, count_ref, rhs_hbm, inv_hbm, adj_ref, sent_ref, rhs_ref, inv_ref, send_ref, sems, table_sems
-):
+def first_kernel(send_hbm, count_ref, rhs_hbm, inv_hbm, adj_ref, sent_ref, rhs_ref, inv_ref, send_ref, sems, table_sems):
     (send_copy,) = fetch(((send_hbm, send_ref),), table_sems)
     tiles = rhs_ref.shape[0]
     parts = sems.shape[0]
@@ -67,87 +77,76 @@
 
         @pl.loop(p * step, (p + 1) * step)
         def _(t):
-            out = solve_tile(t, rhs_ref.at[t], inv_ref, t < count_ref[0])
-            adj_ref[pl.ds(pl.multiple_of(t * 8, 8), 8), :] = out
+            blocks = solve_tile(t, lambda q, j: rhs_ref[t, j : j + 1, lanes_of(q)], inv_ref, t < count_ref[0])
+            for q, block in enumerate(blocks):
+                adj_ref[q, rows_of(t), :] = block
 
     pack_sent(adj_ref, send_ref, sent_ref)
 
 
+def load_kernel(cpl_hbm, cpl_ref, sems):
+    parts = sems.shape[0]
+    step = cpl_ref.shape[0] // parts
+    some = [pl.ds(p * step, step) for p in range(parts)]
+    for copy in fetch([(cpl_hbm.at[s], cpl_ref.at[s]) for s in some], sems):
+        copy.wait()
+
+
 def build_extended(old_ref, halo_refs, ext_ref):
-    own = old_ref.shape[0]
-    ext_ref[:own, :] = old_ref[...]
+    own = old_ref.shape[1]
+    ext_ref[:, :own, :] = old_ref[...]
     odd_region = lax.axis_index("region") % 2
     odd_sub = lax.axis_index("sub") % 2
-    places = (3 - odd_sub, 1 - odd_region, 2 + odd_sub, odd_region)
-    width = halo_refs[0].shape[0]
+    places = (2 + odd_sub, 1 - odd_region, odd_region, 3 - odd_sub)
+    width = halo_refs[0].shape[1]
     for place, halo in zip(places, halo_refs):
-        ext_ref[pl.ds(pl.multiple_of(own + place * width, 8), width), :] = halo[...]
-
-
-def pull_and_solve(t, near_ref, count_ref, rhs_ref, inv_ref, cpl_ref, ext_ref, resid_ref):
+        ext_ref[:, pl.ds(pl.multiple_of(own + place * width, 8), width), :] = halo[...]
+
+
+def sweep_tiles(near_ref, count_ref, rhs_ref, inv_ref, cpl_ref, ext_ref, resid_ref, put):
     own = rhs_ref.shape[0]
-    acc = rhs_ref[t]
-    for k in range(cpl_ref.shape[1]):
-        tile = near_ref[k, t]
-        base = jnp.where(tile < own, tile * 8, tile * NVAR + own * (8 - NVAR))
-        for m in range(NVAR):
-            acc = acc - cpl_ref[t, k, m].astype(F32) * ext_ref[pl.ds(base + m, 1), :]
-    resid_ref[...] = acc
-    return solve_tile(t, resid_ref, inv_ref, t < count_ref[0])
+
+    @pl.loop(0, own)
+    def _(t):
+        bases = []
+        for k in range(cpl_ref.shape[1]):
+            tile = near_ref[k, t]
+            bases.append(jnp.where(tile < own, tile * 8, tile * NVAR + own * (8 - NVAR)))
+        for q in range(resid_ref.shape[0]):
+            sums = [rhs_ref[t, :, lanes_of(q)], None]
+            for k, base in enumerate(bases):
+                for m in range(NVAR):
+                    term = cpl_ref[t, k, m, :, lanes_of(q)].astype(F32) * ext_ref[q, pl.ds(base + m, 1), :]
+                    if k % 2:
+                        sums[1] = term if sums[1] is None else sums[1] + term
+                    else:
+                        sums[0] = sums[0] - term
+            resid_ref[q] = sums[0] - sums[1]
+        put(t, solve_tile(t, lambda q, j: resid_ref[q, j : j + 1, :], inv_ref, t < count_ref[0]))
 
 
 def sweep_kernel(
     near_hbm, send_hbm, count_ref, rhs_ref, inv_ref, cpl_ref, old_ref, h0, h1, h2, h3,
     adj_ref, sent_ref, ext_ref, resid_ref, near_ref, send_ref, table_sems,
 ):
-    tables = ((near_hbm, near_ref), (send_hbm, send_ref))
-    copies = fetch(tables, table_sems)
+    copies = fetch(((near_hbm, near_ref), (send_hbm, send_ref)), table_sems)
     build_extended(old_ref, (h0, h1, h2, h3), ext_ref)
     for copy in copies:
         copy.wait()
 
-    @pl.loop(0, rhs_ref.shape[0])
-    def _(t):
-        out = pull_and_solve(t, near_ref, count_ref, rhs_ref, inv_ref, cpl_ref, ext_ref, resid_ref)
-        adj_ref[pl.ds(pl.multiple_of(t * 8, 8), 8), :] = out
-
-    pack_sent(adj_ref, send_ref, sent_ref)
-
-
-def sweep_load_kernel(
-    near_hbm, send_hbm, count_ref, rhs_ref, inv_ref, cpl_hbm, old_ref, h0, h1, h2, h3,
-    adj_ref, sent_ref, cpl_ref, ext_ref, resid_ref, near_ref, send_ref, table_sems, sems,
-):
-    tables = fetch(((near_hbm, near_ref), (send_hbm, send_ref)), table_sems)
-    tiles = rhs_ref.shape[0]
-    parts = sems.shape[0]
-    step = tiles // parts
-    copies = [
-        pltpu.make_async_copy(
-            cpl_hbm.at[pl.ds(p * step, step)], cpl_ref.at[pl.ds(p * step, step)], sems.at[p]
-        )
-        for p in range(parts)
-    ]
-    for copy in copies:
-        copy.start()
-    build_extended(old_ref, (h0, h1, h2, h3), ext_ref)
-    for copy in tables:
-        copy.wait()
-    for p, copy in enumerate(copies):
-        copy.wait()
-
-        @pl.loop(p * step, (p + 1) * step)
-        def _(t):
-            out = pull_and_solve(t, near_ref, count_ref, rhs_ref, inv_ref, cpl_ref, ext_ref, resid_ref)
-            adj_ref[pl.ds(pl.multiple_of(t * 8, 8), 8), :] = out
-
+    def put(t, blocks):
+        for q, block in enumerate(blocks):
+            adj_ref[q, rows_of(t), :] = block
+
+    sweep_tiles(near_ref, count_ref, rhs_ref, inv_ref, cpl_ref, ext_ref, resid_ref, put)
     pack_sent(adj_ref, send_ref, sent_ref)
 
 
 def last_kernel(
     near_hbm, count_ref, rhs_ref, inv_ref, cpl_ref, hess_ref, old_ref, h0, h1, h2, h3,
     vertex_ref, region_ref, slot_ref, rank_hot_ref,
-    adj_ref, metric_ref, parcel_ref, ext_ref, resid_ref, column_ref, gathered_ref, near_ref, table_sems,
+    adj_hbm, metric_hbm, parcel_ref,
+    ext_ref, resid_ref, adj_ref, metric_ref, column_ref, gathered_ref, near_ref, table_sems, out_sems,
 ):
     copies = fetch(((near_hbm, near_ref),), table_sems)
     build_extended(old_ref, (h0, h1, h2, h3), ext_ref)
@@ -156,24 +155,26 @@
     tiles, width = rhs_ref.shape[0], rhs_ref.shape[2]
     chunks = width // LANES
 
-    @pl.loop(0, tiles)
-    def _(t):
-        out = pull_and_solve(t, near_ref, count_ref, rhs_ref, inv_ref, cpl_ref, ext_ref, resid_ref)
-        here = pl.ds(pl.multiple_of(t * 8, 8), 8)
-        adj_ref[here, :] = out
-        for q in range(chunks):
-            column_ref[q, here, :] = jnp.abs(out[:, q * LANES : (q + 1) * LANES])
+    def put(t, blocks):
+        for q, block in enumerate(blocks):
+            adj_ref[rows_of(t), lanes_of(q)] = block
+            column_ref[q, rows_of(t), :] = jnp.abs(block)
+
+    sweep_tiles(near_ref, count_ref, rhs_ref, inv_ref, cpl_ref, ext_ref, resid_ref, put)
+    adj_out = pltpu.make_async_copy(adj_ref, adj_hbm, out_sems.at[0])
+    adj_out.start()
 
     for q in range(chunks):
-        cols = slice(q * LANES, (q + 1) * LANES)
         sums = [None] * 6
         for c in range(NVAR):
             size = column_ref[q, pl.ds(c, tiles, stride=8), :]
             for s in range(6):
-                term = hess_ref[c, s, :, cols].astype(F32) * size
+                term = hess_ref[c, s, :, lanes_of(q)].astype(F32) * size
                 sums[s] = term if sums[s] is None else sums[s] + term
         for s in range(6):
-            metric_ref[s, :, cols] = sums[s]
+            metric_ref[s, :, lanes_of(q)] = sums[s]
+    metric_out = pltpu.make_async_copy(metric_ref, metric_hbm, out_sems.at[1])
+    metric_out.start()
 
     entries = vertex_ref.shape[1]
     in_tile = lax.broadcasted_iota(jnp.int32, (8, LANES), 0)
@@ -214,6 +215,8 @@
         placed = placed[: half * 8] + placed[half * 8 :]
         for d in range(half):
             parcel_ref[part * half + d] = placed[d * 8 : (d + 1) * 8]
+    adj_out.wait()
+    metric_out.wait()
 
 
 def rank_kernel(region_ref, hot_ref, rank_ref):
@@ -279,7 +282,7 @@
     got_ra = lax.ppermute(sent, *ra)
     got_sb = lax.ppermute(sent, *sb)
     got_sa = lax.ppermute(sent, *sa)
-    return got_sa, got_ra, got_sb, got_rb
+    return got_sb, got_ra, got_rb, got_sa
 
 
 def per_device(
@@ -299,10 +302,11 @@
     dest = owner_region.reshape(1, entries)
     slot = owner_slot.reshape(1, entries)
 
-    adj_shape = jax.ShapeDtypeStruct((tiles * 8, width), F32)
-    sent_shape = jax.ShapeDtypeStruct((sends * NVAR, width), F32)
-    ext = pltpu.VMEM((tiles * 8 + 4 * sends * NVAR, width), F32)
-    resid = pltpu.VMEM((8, width), F32)
+    chunks = width // LANES
+    adj_shape = jax.ShapeDtypeStruct((chunks, tiles * 8, LANES), F32)
+    sent_shape = jax.ShapeDtypeStruct((chunks, sends * NVAR, LANES), F32)
+    ext = pltpu.VMEM((chunks, tiles * 8 + 4 * sends * NVAR, LANES), F32)
+    resid = pltpu.VMEM((chunks, 8, LANES), F32)
     hbm = pl.BlockSpec(memory_space=pltpu.HBM)
     smem = pl.BlockSpec(memory_space=pltpu.SMEM)
     near_table = pltpu.SMEM(neighbours.shape, jnp.int32)
@@ -320,7 +324,18 @@
         out_specs=(VMEM,) * 4,
         scratch_shapes=[send_table, pltpu.SemaphoreType.DMA((4, 2)), pltpu.SemaphoreType.DMA((1,))],
         compiler_params=params,
+        name="first",
     )(send_tiles, tile_count, rhs, diag_inv)
+    coupling = pl.pallas_call(
+        load_kernel,
+        out_shape=jax.ShapeDtypeStruct(coupling.shape, coupling.dtype),
+        in_specs=[hbm],
+        out_specs=VMEM,
+        scratch_shapes=[pltpu.SemaphoreType.DMA((4,))],
+        compiler_params=params,
+        cost_estimate=pl.CostEstimate(flops=0, bytes_accessed=2 * coupling.size * 2, transcendentals=0),
+        name="load",
+    )(coupling)
     rank_hot = pl.pallas_call(
         rank_kernel,
         out_shape=jax.ShapeDtypeStruct((CAP, entries), BF16),
@@ -328,20 +343,9 @@
         out_specs=VMEM,
         scratch_shapes=[pltpu.VMEM((1, entries), F32)],
         compiler_params=params,
+        name="rank",
     )(dest)
-    halos = exchange(sent)
-    adjoint, sent, coupling = pl.pallas_call(
-        sweep_load_kernel,
-        out_shape=(adj_shape, sent_shape, jax.ShapeDtypeStruct(coupling.shape, coupling.dtype)),
-        in_specs=[hbm, hbm, smem] + [VMEM] * 2 + [hbm] + [VMEM] * 5,
-        out_specs=(VMEM,) * 3,
-        scratch_shapes=[
-            ext, resid, near_table, send_table,
-            pltpu.SemaphoreType.DMA((2,)), pltpu.SemaphoreType.DMA((8,)),
-        ],
-        compiler_params=params,
-    )(neighbours, send_tiles, tile_count, rhs, diag_inv, coupling, adjoint, *halos)
-    for sweep in range(SWEEPS - 2):
+    for sweep in range(SWEEPS - 1):
         halos = exchange(sent)
         adjoint, sent = pl.pallas_call(
             sweep_kernel,
@@ -350,26 +354,31 @@
             out_specs=(VMEM, VMEM),
             scratch_shapes=[ext, resid, near_table, send_table, pltpu.SemaphoreType.DMA((2,))],
             compiler_params=params,
+            name="sweep",
         )(neighbours, send_tiles, tile_count, rhs, diag_inv, coupling, adjoint, *halos)
     halos = exchange(sent)
     out, metric, parcels = pl.pallas_call(
         last_kernel,
         out_shape=(
-            adj_shape,
+            jax.ShapeDtypeStruct((tiles * 8, width), F32),
             jax.ShapeDtypeStruct((6, tiles, width), F32),
             jax.ShapeDtypeStruct((regions, 8, CAP), F32),
         ),
         in_specs=[hbm, smem] + [VMEM] * 13,
-        out_specs=(VMEM, VMEM, VMEM),
+        out_specs=(hbm, hbm, VMEM),
         scratch_shapes=[
             ext,
             resid,
-            pltpu.VMEM((width // LANES, tiles * 8, LANES), F32),
+            pltpu.VMEM((tiles * 8, width), F32),
+            pltpu.VMEM((6, tiles, width), F32),
+            pltpu.VMEM((chunks, tiles * 8, LANES), F32),
             pltpu.VMEM((8, entries), F32),
             near_table,
             pltpu.SemaphoreType.DMA((1,)),
+            pltpu.SemaphoreType.DMA((2,)),
         ],
         compiler_params=params,
+        name="last",
     )(
         neighbours, tile_count, rhs, diag_inv, coupling, hessian.transpose(1, 2, 0, 3), adjoint, *halos,
         vertex, dest, slot, rank_hot,
@@ -383,6 +392,7 @@
         in_specs=[VMEM],
         out_specs=VMEM,
         compiler_params=params,
+        name="owner",
     )(parcels)
     return out, metric, owned
 

time: 73.7 us -> 69.3 us (0.940); the launches traced: 72.6 us -> 68.9 us
  blocking collectives: 22.1 us -> 20 us
  waiting for transfers between devices: 6.84 us -> 4.84 us
    ppermute x3, waiting for transfers between devices: 6.81 us -> 0.01 us  [exchange(): got_ra = lax.ppermute(sent, *ra)]
    ppermute x3, waiting for transfers between devices: 0.01 us -> 4.82 us  [exchange(): got_sb = lax.ppermute(sent, *sb)]
    ppermute x3, starting transfers between devices: 14.2 us -> 9.73 us  [exchange(): got_ra = lax.ppermute(sent, *ra)]
    ppermute x3, starting transfers between devices: 0.01 us -> 3.51 us  [exchange(): got_sa = lax.ppermute(sent, *sa)]
    all_to_all x1, blocking collectives: 22.1 us -> 20 us  [per_device(): parcels = lax.all_to_all(parcels, 'region', 0, 0, tiled=True)]
    pallas_call x1 -> x2, Pallas kernels: 2.71 us -> 4.5 us  [per_device(): pl.pallas_call(sweep_kernel, out_shape=(adj_shape, sent_shape), in_specs=...]
    pallas_call x2, Pallas kernels: 8.37 us -> 7.02 us  [the longest x1 4.15 us: per_device(): pl.pallas_call(last_kernel, out_shape=(jax.ShapeDtypeStruct((tiles * 8, w...]
    ppermute x3, starting transfers between devices: 11.1 us -> 12 us  [exchange(): got_sb = lax.ppermute(sent, *sb)]
  transfers between devices with their start and end apart: 12 -> 12, of which waited for: 3 -> 2; matrix products, arithmetic and copies ran while one was open for 0% -> 0% of each run, Pallas kernels for 1% -> 5%
where the time goes in v3:
time: 69.3 us; the launch traced here: 68.9 us
  starting transfers between devices  27.4 us (40%)
  blocking collectives  20 us (29%)
  Pallas kernels  15.1 us (22%)
  waiting for transfers between devices  4.84 us (7%)
  between operations  1.51 us (2%)
    all_to_all x1, blocking collectives, per_device(): parcels = lax.all_to_all(parcels, 'region', 0, 0, tiled=True)  20 us
    ppermute x3, starting transfers between devices, exchange(): got_sb = lax.ppermute(sent, *sb)  12 us
    ppermute x3, starting transfers between devices, exchange(): got_ra = lax.ppermute(sent, *ra)  9.73 us
    ppermute x3, waiting for transfers between devices, exchange(): got_sb = lax.ppermute(sent, *sb)  4.82 us
    pallas_call x2, Pallas kernels, per_device(): pl.pallas_call(sweep_kernel, out_shape=(adj_shape, sent_shape), in_specs=...  4.5 us
    pallas_call x1, Pallas kernels, per_device(): pl.pallas_call(last_kernel, out_shape=(jax.ShapeDtypeStruct((tiles * 8, w...  4.15 us
    ppermute x3, starting transfers between devices, exchange(): got_sa = lax.ppermute(sent, *sa)  3.51 us
    pallas_call x1, Pallas kernels, per_device(): pl.pallas_call(load_kernel, out_shape=jax.ShapeDtypeStruct(coupling.shape...  2.87 us
  transfers between devices with their start and end apart: 12, of which 2 were waited for; matrix products, arithmetic and copies ran while one was open for 0% of the time, Pallas kernels for 5%

profile of v3, /device:TPU:1, one launch (start us, length us, event | category | flops | bytes accessed | tf_op | source)
XLA Modules:
  0.0 68.9 jit_solution(6778419066601920404)
XLA Ops:
  1.3 1.7 %first.1 = (f32[6,128,128]{2,1,0:T(8,128)S(1)}, f32[6,48,128]{2,1,0:T(8,128)S(1)}, f32[16,8,768]{2,1,0:T(8,128)S(1)}, bf16[16,8,8,768]{3,2,1,0:T(8,128)(2,1)S(1)}) custom-call(s32[1,8]{1,0:T(1,128)} %send_hbm.5, s32[1]{0:T(128)S(6)} %copy.13.count_ref, f32[16,8,768]{2,1,0:T(8,128)} %rhs_hbm.1, bf16[16,8,8,768]{3,2,1,0:T(8,128)(2,1)} %inv_hbm.1), custom_call_target="tpu_custom_call" | custom-call | tf_op jit(solution)/shard_map/first/pallas_call | solution.py:315
  3.0 3.3 %collective-permute-start.3 = (f32[6,48,128]{2,1,0:T(8,128)S(1)}, f32[6,48,128]{2,1,0:T(8,128)S(1)}, u32[]{:S(2)}, u32[]{:S(2)}) collective-permute-start(f32[6,48,128]{2,1,0:T(8,128)S(1)} %get-tuple-element.17), channel_id=1, source_target_pairs={{0,1},{1,0},{2,3},{3,2},{4,5},{5,4},{6,7},{7,6},{8,9},{9,8},{10,11... | collective-permute-start | bytes 442376 | tf_op jit(solution)/shard_map/ppermute | solution.py:284
  6.3 0.7 collective-permute-start.2
  7.0 2.2 %collective-permute-start.1 = (f32[6,48,128]{2,1,0:T(8,128)S(1)}, f32[6,48,128]{2,1,0:T(8,128)S(1)}, u32[]{:S(2)}, u32[]{:S(2)}) collective-permute-start(f32[6,48,128]{2,1,0:T(8,128)S(1)} %get-tuple-element.17), channel_id=1, source_target_pairs={{0,8},{8,0},{16,24},{24,16},{32,40},{40,32},{48,56},{56,48},{64,72... | collective-permute-start | bytes 442376 | tf_op jit(solution)/shard_map/ppermute | solution.py:282
  9.2 3.6 %collective-permute-start = (f32[6,48,128]{2,1,0:T(8,128)S(1)}, f32[6,48,128]{2,1,0:T(8,128)S(1)}, u32[]{:S(2)}, u32[]{:S(2)}) collective-permute-start(f32[6,48,128]{2,1,0:T(8,128)S(1)} %get-tuple-element.17), channel_id=1, source_target_pairs={{1,2},{2,1},{3,4},{4,3},{5,6},{6,5},{9,10},{10,9},{11,12},{12,11},... | collective-permute-start | bytes 442376 | tf_op jit(solution)/shard_map/ppermute | solution.py:283
  12.8 2.9 %load.1.cpl_ref = bf16[16,4,8,8,768]{4,3,2,1,0:T(8,128)(2,1)S(1)} custom-call(bf16[16,4,8,8,768]{4,3,2,1,0:T(8,128)(2,1)} %cpl_hbm.1), custom_call_target="tpu_custom_call" | custom-call | bytes 12582912 | tf_op jit(solution)/shard_map/load/pallas_call | solution.py:329
  15.6 0.0 collective-permute-done.3.h3
  15.7 0.0 collective-permute-done.2.h2
  15.7 0.0 collective-permute-done.1.h1
  15.7 2.3 %sweep.2 = (f32[6,128,128]{2,1,0:T(8,128)S(1)}, f32[6,48,128]{2,1,0:T(8,128)S(1)}) custom-call(s32[4,16]{1,0:T(4,128)} %bitcast.12, s32[1,8]{1,0:T(1,128)} %send_hbm.5, s32[1]{0:T(128)S(6)} %copy.13.count_ref, f32[16,8,768]{2,1,0:T(8,128)S(1)} %get-tuple-element.14.rhs_ref, bf16[16,8,8,768]{3,2,1,0:T(8,128)(2,1)S(1)} %get-tuple-element.15.inv_ref, ...), custom_call_target="tpu_custom_call" | custom-call | tf_op jit(solution)/shard_map/sweep/pallas_call | solution.py:350
  18.0 0.0 copy-start.1
  18.0 0.0 copy-start
  18.0 0.0 copy-start.2
  18.0 0.0 copy-start.3
  18.0 0.1 collective-permute-start.7
  18.1 0.8 %collective-permute-start.6 = (f32[6,48,128]{2,1,0:T(8,128)S(1)}, f32[6,48,128]{2,1,0:T(8,128)S(1)}, u32[]{:S(2)}, u32[]{:S(2)}) collective-permute-start(f32[6,48,128]{2,1,0:T(8,128)S(1)} %get-tuple-element.19), channel_id=1, source_target_pairs={{8,16},{16,8},{24,32},{32,24},{40,48},{48,40},{56,64},{64,56},{72,... | collective-permute-start | bytes 442376 | tf_op jit(solution)/shard_map/ppermute | solution.py:281
  18.9 3.6 %collective-permute-start.5 = (f32[6,48,128]{2,1,0:T(8,128)S(1)}, f32[6,48,128]{2,1,0:T(8,128)S(1)}, u32[]{:S(2)}, u32[]{:S(2)}) collective-permute-start(f32[6,48,128]{2,1,0:T(8,128)S(1)} %get-tuple-element.19), channel_id=1, source_target_pairs={{0,8},{8,0},{16,24},{24,16},{32,40},{40,32},{48,56},{56,48},{64,72... | collective-permute-start | bytes 442376 | tf_op jit(solution)/shard_map/ppermute | solution.py:282
  22.5 4.2 %collective-permute-start.4 = (f32[6,48,128]{2,1,0:T(8,128)S(1)}, f32[6,48,128]{2,1,0:T(8,128)S(1)}, u32[]{:S(2)}, u32[]{:S(2)}) collective-permute-start(f32[6,48,128]{2,1,0:T(8,128)S(1)} %get-tuple-element.19), channel_id=1, source_target_pairs={{1,2},{2,1},{3,4},{4,3},{5,6},{6,5},{9,10},{10,9},{11,12},{12,11},... | collective-permute-start | bytes 442376 | tf_op jit(solution)/shard_map/ppermute | solution.py:283
  26.7 0.0 collective-permute-done.6.h2
  26.7 2.8 %collective-permute-done.4.h0 = f32[6,48,128]{2,1,0:T(8,128)S(1)} collective-permute-done((f32[6,48,128]{2,1,0:T(8,128)S(1)}, f32[6,48,128]{2,1,0:T(8,128)S(1)}, u32[]{:S(2)}, u32[]{:S(2)}) %collective-permute-start.4) | collective-permute-done | bytes 147488 | tf_op jit(solution)/shard_map/ppermute | solution.py:283
  29.5 2.2 %sweep.3 = (f32[6,128,128]{2,1,0:T(8,128)S(1)}, f32[6,48,128]{2,1,0:T(8,128)S(1)}) custom-call(s32[4,16]{1,0:T(4,128)} %bitcast.13, s32[1,8]{1,0:T(1,128)} %send_hbm.5, s32[1]{0:T(128)S(6)} %copy.13.count_ref, f32[16,8,768]{2,1,0:T(8,128)S(1)} %get-tuple-element.14.rhs_ref, bf16[16,8,8,768]{3,2,1,0:T(8,128)(2,1)S(1)} %get-tuple-element.15.inv_ref, ...), custom_call_target="tpu_custom_call" | custom-call | tf_op jit(solution)/shard_map/sweep/pallas_call | solution.py:350
  31.8 0.1 collective-permute-start.11
  31.9 0.7 collective-permute-start.10
  32.5 3.9 %collective-permute-start.9 = (f32[6,48,128]{2,1,0:T(8,128)S(1)}, f32[6,48,128]{2,1,0:T(8,128)S(1)}, u32[]{:S(2)}, u32[]{:S(2)}) collective-permute-start(f32[6,48,128]{2,1,0:T(8,128)S(1)} %get-tuple-element.21), channel_id=1, source_target_pairs={{0,8},{8,0},{16,24},{24,16},{32,40},{40,32},{48,56},{56,48},{64,72... | collective-permute-start | bytes 442376 | tf_op jit(solution)/shard_map/ppermute | solution.py:282
  36.5 4.3 %collective-permute-start.8 = (f32[6,48,128]{2,1,0:T(8,128)S(1)}, f32[6,48,128]{2,1,0:T(8,128)S(1)}, u32[]{:S(2)}, u32[]{:S(2)}) collective-permute-start(f32[6,48,128]{2,1,0:T(8,128)S(1)} %get-tuple-element.21), channel_id=1, source_target_pairs={{1,2},{2,1},{3,4},{4,3},{5,6},{6,5},{9,10},{10,9},{11,12},{12,11},... | collective-permute-start | bytes 442376 | tf_op jit(solution)/shard_map/ppermute | solution.py:283
  40.8 0.7 %rank.1.rank_hot_ref = bf16[128,1024]{1,0:T(8,128)(2,1)S(1)} custom-call(s32[1,1024]{1,0:T(1,128)S(1)} %bitcast.8), custom_call_target="tpu_custom_call" | custom-call | tf_op jit(solution)/shard_map/rank/pallas_call | solution.py:339
  41.5 0.0 collective-permute-done.11.h3
  41.5 0.0 collective-permute-done.9.h1
  41.5 2.0 %collective-permute-done.8.h0 = f32[6,48,128]{2,1,0:T(8,128)S(1)} collective-permute-done((f32[6,48,128]{2,1,0:T(8,128)S(1)}, f32[6,48,128]{2,1,0:T(8,128)S(1)}, u32[]{:S(2)}, u32[]{:S(2)}) %collective-permute-start.8) | collective-permute-done | bytes 147488 | tf_op jit(solution)/shard_map/ppermute | solution.py:283
  43.6 4.2 %last.1 = (f32[128,768]{1,0:T(8,128)}, f32[6,16,768]{2,1,0:T(8,128)}, f32[32,8,128]{2,1,0:T(8,128)S(1)}) custom-call(s32[4,16]{1,0:T(4,128)} %bitcast.14, s32[1]{0:T(128)S(6)} %copy.13.count_ref, f32[16,8,768]{2,1,0:T(8,128)S(1)} %get-tuple-element.14.rhs_ref, bf16[16,8,8,768]{3,2,1,0:T(8,128)(2,1)S(1)} %get-tuple-element.15.inv_ref, ...), custom_call_target="tpu_custom_call" | custom-call | tf_op jit(solution)/shard_map/last/pallas_call | solution.py:360
  47.7 20.0 %all_to_all.5.parcel_ref = f32[32,8,128]{2,1,0:T(8,128)S(1)} all-to-all(f32[32,8,128]{2,1,0:T(8,128)S(1)} %get-tuple-element.24), channel_id=1, replica_groups=mesh['region'=32,'sub'=8] {'region'}, dimensions={0} | all-to-all | bytes 262144 | tf_op jit(solution)/shard_map/all_to_all | solution.py:388
  67.7 1.2 %owner.1 = f32[6,1024]{1,0:T(8,128)} custom-call(f32[32,8,128]{2,1,0:T(8,128)S(1)} %all_to_all.5.parcel_ref), custom_call_target="tpu_custom_call" | custom-call | tf_op jit(solution)/shard_map/owner/pallas_call | solution.py:389
  (8 shorter events, 0.0 us)
Async XLA Ops:
  3.0 12.6 %collective-permute-start.3 = (f32[6,48,128]{2,1,0:T(8,128)S(1)}, f32[6,48,128]{2,1,0:T(8,128)S(1)}, u32[]{:S(2)}, u32[]{:S(2)}) collective-permute-start(f32[6,48,128]{2,1,0:T(8,128)S(1)} %get-tuple-element.17), channel_id=1, source_target_pairs={{0,1},{1,0},{2,3},{3,2},{4,5},{5,4},{6,7},{7,6},{8,9},{9,8},{10,11... | collective-permute-start | bytes 442376 | tf_op jit(solution)/shard_map/ppermute | solution.py:284
  6.3 9.3 %collective-permute-start.2 = (f32[6,48,128]{2,1,0:T(8,128)S(1)}, f32[6,48,128]{2,1,0:T(8,128)S(1)}, u32[]{:S(2)}, u32[]{:S(2)}) collective-permute-start(f32[6,48,128]{2,1,0:T(8,128)S(1)} %get-tuple-element.17), channel_id=1, source_target_pairs={{8,16},{16,8},{24,32},{32,24},{40,48},{48,40},{56,64},{64,56},{72,... | collective-permute-start | bytes 442376 | tf_op jit(solution)/shard_map/ppermute | solution.py:281
  7.0 8.7 %collective-permute-start.1 = (f32[6,48,128]{2,1,0:T(8,128)S(1)}, f32[6,48,128]{2,1,0:T(8,128)S(1)}, u32[]{:S(2)}, u32[]{:S(2)}) collective-permute-start(f32[6,48,128]{2,1,0:T(8,128)S(1)} %get-tuple-element.17), channel_id=1, source_target_pairs={{0,8},{8,0},{16,24},{24,16},{32,40},{40,32},{48,56},{56,48},{64,72... | collective-permute-start | bytes 442376 | tf_op jit(solution)/shard_map/ppermute | solution.py:282
  9.2 6.5 %collective-permute-start = (f32[6,48,128]{2,1,0:T(8,128)S(1)}, f32[6,48,128]{2,1,0:T(8,128)S(1)}, u32[]{:S(2)}, u32[]{:S(2)}) collective-permute-start(f32[6,48,128]{2,1,0:T(8,128)S(1)} %get-tuple-element.17), channel_id=1, source_target_pairs={{1,2},{2,1},{3,4},{4,3},{5,6},{6,5},{9,10},{10,9},{11,12},{12,11},... | collective-permute-start | bytes 442376 | tf_op jit(solution)/shard_map/ppermute | solution.py:283
  18.0 22.8 %copy-start.1 = (s32[1024,1]{0,1:T(1,128)S(1)}, s32[1024,1]{0,1:T(1,128)}, u32[]{:S(2)}) copy-start(s32[1024,1]{0,1:T(1,128)} %param.18) | copy-start | bytes 12292
  18.0 25.6 %copy-start = (bf16[16,6,6,768]{3,0,2,1:T(8,128)(2,1)S(1)}, bf16[16,6,6,768]{3,0,2,1:T(8,128)(2,1)}, u32[]{:S(2)}) copy-start(bf16[16,6,6,768]{3,0,2,1:T(8,128)(2,1)} %param.16) | copy-start | bytes 2654212
  18.0 25.6 %copy-start.2 = (s32[1024]{0:T(1024)S(1)}, s32[1024]{0:T(1024)}, u32[]{:S(2)}) copy-start(s32[1024]{0:T(1024)} %param.17) | copy-start | bytes 12292
  18.0 25.6 %copy-start.3 = (s32[1024]{0:T(1024)S(1)}, s32[1024]{0:T(1024)}, u32[]{:S(2)}) copy-start(s32[1024]{0:T(1024)} %param.19) | copy-start | bytes 12292
  18.0 8.7 %collective-permute-start.7 = (f32[6,48,128]{2,1,0:T(8,128)S(1)}, f32[6,48,128]{2,1,0:T(8,128)S(1)}, u32[]{:S(2)}, u32[]{:S(2)}) collective-permute-start(f32[6,48,128]{2,1,0:T(8,128)S(1)} %get-tuple-element.19), channel_id=1, source_target_pairs={{0,1},{1,0},{2,3},{3,2},{4,5},{5,4},{6,7},{7,6},{8,9},{9,8},{10,11... | collective-permute-start | bytes 442376 | tf_op jit(solution)/shard_map/ppermute | solution.py:284
  18.1 8.6 %collective-permute-start.6 = (f32[6,48,128]{2,1,0:T(8,128)S(1)}, f32[6,48,128]{2,1,0:T(8,128)S(1)}, u32[]{:S(2)}, u32[]{:S(2)}) collective-permute-start(f32[6,48,128]{2,1,0:T(8,128)S(1)} %get-tuple-element.19), channel_id=1, source_target_pairs={{8,16},{16,8},{24,32},{32,24},{40,48},{48,40},{56,64},{64,56},{72,... | collective-permute-start | bytes 442376 | tf_op jit(solution)/shard_map/ppermute | solution.py:281
  18.9 7.8 %collective-permute-start.5 = (f32[6,48,128]{2,1,0:T(8,128)S(1)}, f32[6,48,128]{2,1,0:T(8,128)S(1)}, u32[]{:S(2)}, u32[]{:S(2)}) collective-permute-start(f32[6,48,128]{2,1,0:T(8,128)S(1)} %get-tuple-element.19), channel_id=1, source_target_pairs={{0,8},{8,0},{16,24},{24,16},{32,40},{40,32},{48,56},{56,48},{64,72... | collective-permute-start | bytes 442376 | tf_op jit(solution)/shard_map/ppermute | solution.py:282
  22.5 7.0 %collective-permute-start.4 = (f32[6,48,128]{2,1,0:T(8,128)S(1)}, f32[6,48,128]{2,1,0:T(8,128)S(1)}, u32[]{:S(2)}, u32[]{:S(2)}) collective-permute-start(f32[6,48,128]{2,1,0:T(8,128)S(1)} %get-tuple-element.19), channel_id=1, source_target_pairs={{1,2},{2,1},{3,4},{4,3},{5,6},{6,5},{9,10},{10,9},{11,12},{12,11},... | collective-permute-start | bytes 442376 | tf_op jit(solution)/shard_map/ppermute | solution.py:283
  31.8 9.7 %collective-permute-start.11 = (f32[6,48,128]{2,1,0:T(8,128)S(1)}, f32[6,48,128]{2,1,0:T(8,128)S(1)}, u32[]{:S(2)}, u32[]{:S(2)}) collective-permute-start(f32[6,48,128]{2,1,0:T(8,128)S(1)} %get-tuple-element.21), channel_id=1, source_target_pairs={{0,1},{1,0},{2,3},{3,2},{4,5},{5,4},{6,7},{7,6},{8,9},{9,8},{10,11... | collective-permute-start | bytes 442376 | tf_op jit(solution)/shard_map/ppermute | solution.py:284
  31.9 9.7 %collective-permute-start.10 = (f32[6,48,128]{2,1,0:T(8,128)S(1)}, f32[6,48,128]{2,1,0:T(8,128)S(1)}, u32[]{:S(2)}, u32[]{:S(2)}) collective-permute-start(f32[6,48,128]{2,1,0:T(8,128)S(1)} %get-tuple-element.21), channel_id=1, source_target_pairs={{8,16},{16,8},{24,32},{32,24},{40,48},{48,40},{56,64},{64,56},{72,... | collective-permute-start | bytes 442376 | tf_op jit(solution)/shard_map/ppermute | solution.py:281
  32.5 9.0 %collective-permute-start.9 = (f32[6,48,128]{2,1,0:T(8,128)S(1)}, f32[6,48,128]{2,1,0:T(8,128)S(1)}, u32[]{:S(2)}, u32[]{:S(2)}) collective-permute-start(f32[6,48,128]{2,1,0:T(8,128)S(1)} %get-tuple-element.21), channel_id=1, source_target_pairs={{0,8},{8,0},{16,24},{24,16},{32,40},{40,32},{48,56},{56,48},{64,72... | collective-permute-start | bytes 442376 | tf_op jit(solution)/shard_map/ppermute | solution.py:282
  36.5 7.1 %collective-permute-start.8 = (f32[6,48,128]{2,1,0:T(8,128)S(1)}, f32[6,48,128]{2,1,0:T(8,128)S(1)}, u32[]{:S(2)}, u32[]{:S(2)}) collective-permute-start(f32[6,48,128]{2,1,0:T(8,128)S(1)} %get-tuple-element.21), channel_id=1, source_target_pairs={{1,2},{2,1},{3,4},{4,3},{5,6},{6,5},{9,10},{10,9},{11,12},{12,11},... | collective-permute-start | bytes 442376 | tf_op jit(solution)/shard_map/ppermute | solution.py:283

commit v4 on v3

--- a/solution.py
+++ b/solution.py
@@ -12,6 +12,9 @@
 OWNED = 1024
 CAP = 128
 LANES = 128
+
+ORDER = ("sa", "rb", "ra", "sb")
+LAST_ORDER = ("ra", "sb", "sa", "rb")
 
 F32 = jnp.float32
 BF16 = jnp.bfloat16
@@ -53,114 +56,130 @@
     return copies
 
 
-def first_kernel(send_hbm, count_ref, rhs_hbm, inv_hbm, adj_ref, sent_ref, rhs_ref, inv_ref, send_ref, sems, table_sems):
-    (send_copy,) = fetch(((send_hbm, send_ref),), table_sems)
-    tiles = rhs_ref.shape[0]
-    parts = sems.shape[0]
-    step = tiles // parts
-    copies = []
-    for p in range(parts):
-        some = pl.ds(p * step, step)
-        copies.append(
-            (
-                pltpu.make_async_copy(rhs_hbm.at[some], rhs_ref.at[some], sems.at[p, 0]),
-                pltpu.make_async_copy(inv_hbm.at[some], inv_ref.at[some], sems.at[p, 1]),
-            )
-        )
-    for pair in copies:
-        for copy in pair:
-            copy.start()
+def put_rows(adj_ref, t, blocks):
+    for q, block in enumerate(blocks):
+        adj_ref[q, rows_of(t), :] = block
+
+
+def first_kernel(
+    send_hbm, near_hbm, count_ref, rhs_hbm, inv_hbm,
+    adj_ref, sent_ref, rhs_ref, inv_ref, send_ref, near_ref, listed_ref, sems, table_sems,
+):
+    send_copy, near_copy = fetch(((send_hbm, send_ref), (near_hbm, near_ref)), table_sems)
+    tiles, sends = rhs_ref.shape[0], send_ref.shape[1]
+    half = tiles // 2
+    pairs = [(rhs_hbm, rhs_ref)]
+    pairs += [(inv_hbm.at[pl.ds(p * half, half)], inv_ref.at[pl.ds(p * half, half)]) for p in range(2)]
+    copies = fetch(pairs, sems)
     send_copy.wait()
-    for p, pair in enumerate(copies):
-        for copy in pair:
-            copy.wait()
-
-        @pl.loop(p * step, (p + 1) * step)
-        def _(t):
-            blocks = solve_tile(t, lambda q, j: rhs_ref[t, j : j + 1, lanes_of(q)], inv_ref, t < count_ref[0])
-            for q, block in enumerate(blocks):
-                adj_ref[q, rows_of(t), :] = block
+    for t in range(tiles):
+        listed_ref[0, t] = 0
+    for s in range(sends):
+        listed_ref[0, send_ref[0, s]] = 1
+    for copy in copies:
+        copy.wait()
+
+    @pl.loop(0, sends)
+    def _(s):
+        t = send_ref[0, s]
+        row_of = lambda q, j: rhs_ref[t, j : j + 1, lanes_of(q)]
+        put_rows(adj_ref, t, solve_tile(t, row_of, inv_ref, t < count_ref[0]))
 
     pack_sent(adj_ref, send_ref, sent_ref)
-
-
-def load_kernel(cpl_hbm, cpl_ref, sems):
+    near_copy.wait()
+
+
+def first_rest_kernel(listed_ref, count_ref, rhs_ref, inv_ref, lead_ref, cpl_hbm, adj_ref, cpl_ref, sems):
     parts = sems.shape[0]
     step = cpl_ref.shape[0] // parts
     some = [pl.ds(p * step, step) for p in range(parts)]
-    for copy in fetch([(cpl_hbm.at[s], cpl_ref.at[s]) for s in some], sems):
+    copies = fetch([(cpl_hbm.at[s], cpl_ref.at[s]) for s in some], sems)
+    adj_ref[...] = lead_ref[...]
+
+    @pl.loop(0, rhs_ref.shape[0])
+    def _(t):
+        @pl.when(listed_ref[0, t] == 0)
+        def _():
+            row_of = lambda q, j: rhs_ref[t, j : j + 1, lanes_of(q)]
+            put_rows(adj_ref, t, solve_tile(t, row_of, inv_ref, t < count_ref[0]))
+
+    for copy in copies:
         copy.wait()
 
 
-def build_extended(old_ref, halo_refs, ext_ref):
+def build_extended(order, old_ref, halo_refs, ext_ref):
     own = old_ref.shape[1]
     ext_ref[:, :own, :] = old_ref[...]
     odd_region = lax.axis_index("region") % 2
     odd_sub = lax.axis_index("sub") % 2
-    places = (2 + odd_sub, 1 - odd_region, odd_region, 3 - odd_sub)
+    places = {"ra": 1 - odd_region, "rb": odd_region, "sa": 3 - odd_sub, "sb": 2 + odd_sub}
     width = halo_refs[0].shape[1]
-    for place, halo in zip(places, halo_refs):
-        ext_ref[:, pl.ds(pl.multiple_of(own + place * width, 8), width), :] = halo[...]
-
-
-def sweep_tiles(near_ref, count_ref, rhs_ref, inv_ref, cpl_ref, ext_ref, resid_ref, put):
+    for name, halo in zip(order, halo_refs):
+        ext_ref[:, pl.ds(pl.multiple_of(own + places[name] * width, 8), width), :] = halo[...]
+
+
+def sweep_tile(t, near_ref, count_ref, rhs_ref, inv_ref, cpl_ref, ext_ref, resid_ref):
     own = rhs_ref.shape[0]
-
-    @pl.loop(0, own)
+    bases = []
+    for k in range(cpl_ref.shape[1]):
+        tile = near_ref[k, t]
+        bases.append(jnp.where(tile < own, tile * 8, tile * NVAR + own * (8 - NVAR)))
+    for q in range(resid_ref.shape[0]):
+        sums = [rhs_ref[t, :, lanes_of(q)], None]
+        for k, base in enumerate(bases):
+            for m in range(NVAR):
+                term = cpl_ref[t, k, m, :, lanes_of(q)].astype(F32) * ext_ref[q, pl.ds(base + m, 1), :]
+                if k % 2:
+                    sums[1] = term if sums[1] is None else sums[1] + term
+                else:
+                    sums[0] = sums[0] - term
+        resid_ref[q] = sums[0] - sums[1]
+    return solve_tile(t, lambda q, j: resid_ref[q, j : j + 1, :], inv_ref, t < count_ref[0])
+
+
+def lead_kernel(
+    order, near_ref, send_ref, count_ref, rhs_ref, inv_ref, cpl_ref, old_ref, h0, h1, h2, h3,
+    adj_ref, sent_ref, ext_ref, resid_ref,
+):
+    build_extended(order, old_ref, (h0, h1, h2, h3), ext_ref)
+
+    @pl.loop(0, send_ref.shape[1])
+    def _(s):
+        t = send_ref[0, s]
+        put_rows(adj_ref, t, sweep_tile(t, near_ref, count_ref, rhs_ref, inv_ref, cpl_ref, ext_ref, resid_ref))
+
+    pack_sent(adj_ref, send_ref, sent_ref)
+
+
+def rest_kernel(
+    near_ref, listed_ref, count_ref, rhs_ref, inv_ref, cpl_ref, ext_ref, lead_ref, adj_ref, resid_ref
+):
+    adj_ref[...] = lead_ref[...]
+
+    @pl.loop(0, rhs_ref.shape[0])
     def _(t):
-        bases = []
-        for k in range(cpl_ref.shape[1]):
-            tile = near_ref[k, t]
-            bases.append(jnp.where(tile < own, tile * 8, tile * NVAR + own * (8 - NVAR)))
-        for q in range(resid_ref.shape[0]):
-            sums = [rhs_ref[t, :, lanes_of(q)], None]
-            for k, base in enumerate(bases):
-                for m in range(NVAR):
-                    term = cpl_ref[t, k, m, :, lanes_of(q)].astype(F32) * ext_ref[q, pl.ds(base + m, 1), :]
-                    if k % 2:
-                        sums[1] = term if sums[1] is None else sums[1] + term
-                    else:
-                        sums[0] = sums[0] - term
-            resid_ref[q] = sums[0] - sums[1]
-        put(t, solve_tile(t, lambda q, j: resid_ref[q, j : j + 1, :], inv_ref, t < count_ref[0]))
-
-
-def sweep_kernel(
-    near_hbm, send_hbm, count_ref, rhs_ref, inv_ref, cpl_ref, old_ref, h0, h1, h2, h3,
-    adj_ref, sent_ref, ext_ref, resid_ref, near_ref, send_ref, table_sems,
-):
-    copies = fetch(((near_hbm, near_ref), (send_hbm, send_ref)), table_sems)
-    build_extended(old_ref, (h0, h1, h2, h3), ext_ref)
-    for copy in copies:
-        copy.wait()
-
-    def put(t, blocks):
-        for q, block in enumerate(blocks):
-            adj_ref[q, rows_of(t), :] = block
-
-    sweep_tiles(near_ref, count_ref, rhs_ref, inv_ref, cpl_ref, ext_ref, resid_ref, put)
-    pack_sent(adj_ref, send_ref, sent_ref)
+        @pl.when(listed_ref[0, t] == 0)
+        def _():
+            put_rows(adj_ref, t, sweep_tile(t, near_ref, count_ref, rhs_ref, inv_ref, cpl_ref, ext_ref, resid_ref))
 
 
 def last_kernel(
-    near_hbm, count_ref, rhs_ref, inv_ref, cpl_ref, hess_ref, old_ref, h0, h1, h2, h3,
+    order, near_ref, count_ref, rhs_ref, inv_ref, cpl_ref, hess_ref, old_ref, h0, h1, h2, h3,
     vertex_ref, region_ref, slot_ref, rank_hot_ref,
     adj_hbm, metric_hbm, parcel_ref,
-    ext_ref, resid_ref, adj_ref, metric_ref, column_ref, gathered_ref, near_ref, table_sems, out_sems,
+    ext_ref, resid_ref, adj_ref, metric_ref, column_ref, gathered_ref, out_sems,
 ):
-    copies = fetch(((near_hbm, near_ref),), table_sems)
-    build_extended(old_ref, (h0, h1, h2, h3), ext_ref)
-    for copy in copies:
-        copy.wait()
+    build_extended(order, old_ref, (h0, h1, h2, h3), ext_ref)
     tiles, width = rhs_ref.shape[0], rhs_ref.shape[2]
     chunks = width // LANES
 
-    def put(t, blocks):
+    @pl.loop(0, tiles)
+    def _(t):
+        blocks = sweep_tile(t, near_ref, count_ref, rhs_ref, inv_ref, cpl_ref, ext_ref, resid_ref)
         for q, block in enumerate(blocks):
             adj_ref[rows_of(t), lanes_of(q)] = block
             column_ref[q, rows_of(t), :] = jnp.abs(block)
 
-    sweep_tiles(near_ref, count_ref, rhs_ref, inv_ref, cpl_ref, ext_ref, resid_ref, put)
     adj_out = pltpu.make_async_copy(adj_ref, adj_hbm, out_sems.at[0])
     adj_out.start()
 
@@ -267,22 +286,17 @@
         owned_ref[:, h * LANES : (h + 1) * LANES] = total[h * 8 : h * 8 + NVAR]
 
 
-def pairings(regions, subs):
-    def swap(length, first):
-        return [p for i in range(first, length - 1, 2) for p in ((i, i + 1), (i + 1, i))]
-
-    along_region = [("region", swap(regions, 0)), ("region", swap(regions, 1))]
-    along_sub = [("sub", swap(subs, 0)), ("sub", swap(subs, 1))]
-    return along_region + along_sub
-
-
-def exchange(sent):
-    ra, rb, sa, sb = pairings(lax.axis_size("region"), lax.axis_size("sub"))
-    got_rb = lax.ppermute(sent, *rb)
-    got_ra = lax.ppermute(sent, *ra)
-    got_sb = lax.ppermute(sent, *sb)
-    got_sa = lax.ppermute(sent, *sa)
-    return got_sb, got_ra, got_rb, got_sa
+def pairings():
+    def swap(axis, first):
+        length = lax.axis_size(axis)
+        return axis, [p for i in range(first, length - 1, 2) for p in ((i, i + 1), (i + 1, i))]
+
+    return {"ra": swap("region", 0), "rb": swap("region", 1), "sa": swap("sub", 0), "sb": swap("sub", 1)}
+
+
+def exchange(sent, order):
+    pairs = pairings()
+    return [lax.ppermute(sent, *pairs[name]) for name in order]
 
 
 def per_device(
@@ -305,37 +319,42 @@
     chunks = width // LANES
     adj_shape = jax.ShapeDtypeStruct((chunks, tiles * 8, LANES), F32)
     sent_shape = jax.ShapeDtypeStruct((chunks, sends * NVAR, LANES), F32)
-    ext = pltpu.VMEM((chunks, tiles * 8 + 4 * sends * NVAR, LANES), F32)
+    ext_shape = jax.ShapeDtypeStruct((chunks, tiles * 8 + 4 * sends * NVAR, LANES), F32)
     resid = pltpu.VMEM((chunks, 8, LANES), F32)
     hbm = pl.BlockSpec(memory_space=pltpu.HBM)
     smem = pl.BlockSpec(memory_space=pltpu.SMEM)
-    near_table = pltpu.SMEM(neighbours.shape, jnp.int32)
-    send_table = pltpu.SMEM(send_tiles.shape, jnp.int32)
-
-    adjoint, sent, rhs, diag_inv = pl.pallas_call(
+    scalars = functools.partial(pltpu.with_memory_space_constraint, memory_space=pltpu.SMEM)
+    beside = pl.CostEstimate(flops=0, bytes_accessed=4 * 2**20, transcendentals=0)
+
+    lead, sent, rhs, diag_inv, send_tiles, neighbours, listed = pl.pallas_call(
         first_kernel,
         out_shape=(
             adj_shape,
             sent_shape,
             jax.ShapeDtypeStruct(rhs.shape, rhs.dtype),
             jax.ShapeDtypeStruct(diag_inv.shape, diag_inv.dtype),
+            pltpu.SMEM(send_tiles.shape, jnp.int32),
+            pltpu.SMEM(neighbours.shape, jnp.int32),
+            pltpu.SMEM((1, tiles), jnp.int32),
         ),
-        in_specs=[hbm, smem, hbm, hbm],
-        out_specs=(VMEM,) * 4,
-        scratch_shapes=[send_table, pltpu.SemaphoreType.DMA((4, 2)), pltpu.SemaphoreType.DMA((1,))],
+        in_specs=[hbm, hbm, smem, hbm, hbm],
+        out_specs=(VMEM,) * 4 + (smem,) * 3,
+        scratch_shapes=[pltpu.SemaphoreType.DMA((3,)), pltpu.SemaphoreType.DMA((2,))],
         compiler_params=params,
         name="first",
-    )(send_tiles, tile_count, rhs, diag_inv)
-    coupling = pl.pallas_call(
-        load_kernel,
-        out_shape=jax.ShapeDtypeStruct(coupling.shape, coupling.dtype),
-        in_specs=[hbm],
-        out_specs=VMEM,
+    )(send_tiles, neighbours, tile_count, rhs, diag_inv)
+    send_tiles, neighbours, listed = scalars(send_tiles), scalars(neighbours), scalars(listed)
+    halos = exchange(sent, ORDER)
+    adjoint, coupling = pl.pallas_call(
+        first_rest_kernel,
+        out_shape=(adj_shape, jax.ShapeDtypeStruct(coupling.shape, coupling.dtype)),
+        in_specs=[smem, smem, VMEM, VMEM, VMEM, hbm],
+        out_specs=(VMEM, VMEM),
         scratch_shapes=[pltpu.SemaphoreType.DMA((4,))],
         compiler_params=params,
-        cost_estimate=pl.CostEstimate(flops=0, bytes_accessed=2 * coupling.size * 2, transcendentals=0),
-        name="load",
-    )(coupling)
+        cost_estimate=pl.CostEstimate(flops=0, bytes_accessed=4 * coupling.size, transcendentals=0),
+        name="first_rest",
+    )(listed, tile_count, rhs, diag_inv, lead, coupling)
     rank_hot = pl.pallas_call(
         rank_kernel,
         out_shape=jax.ShapeDtypeStruct((CAP, entries), BF16),
@@ -346,35 +365,43 @@
         name="rank",
     )(dest)
     for sweep in range(SWEEPS - 1):
-        halos = exchange(sent)
-        adjoint, sent = pl.pallas_call(
-            sweep_kernel,
-            out_shape=(adj_shape, sent_shape),
-            in_specs=[hbm, hbm, smem] + [VMEM] * 8,
-            out_specs=(VMEM, VMEM),
-            scratch_shapes=[ext, resid, near_table, send_table, pltpu.SemaphoreType.DMA((2,))],
+        order = LAST_ORDER if sweep == SWEEPS - 2 else ORDER
+        lead, sent, extended = pl.pallas_call(
+            functools.partial(lead_kernel, ORDER),
+            out_shape=(adj_shape, sent_shape, ext_shape),
+            in_specs=[smem] * 3 + [VMEM] * 8,
+            out_specs=(VMEM,) * 3,
+            scratch_shapes=[resid],
             compiler_params=params,
-            name="sweep",
+            name="lead",
         )(neighbours, send_tiles, tile_count, rhs, diag_inv, coupling, adjoint, *halos)
-    halos = exchange(sent)
+        halos = exchange(sent, order)
+        adjoint = pl.pallas_call(
+            rest_kernel,
+            out_shape=adj_shape,
+            in_specs=[smem] * 3 + [VMEM] * 5,
+            out_specs=VMEM,
+            scratch_shapes=[resid],
+            compiler_params=params,
+            cost_estimate=beside,
+            name="rest",
+        )(neighbours, listed, tile_count, rhs, diag_inv, coupling, extended, lead)
     out, metric, parcels = pl.pallas_call(
-        last_kernel,
+        functools.partial(last_kernel, LAST_ORDER),
         out_shape=(
             jax.ShapeDtypeStruct((tiles * 8, width), F32),
             jax.ShapeDtypeStruct((6, tiles, width), F32),
             jax.ShapeDtypeStruct((regions, 8, CAP), F32),
         ),
-        in_specs=[hbm, smem] + [VMEM] * 13,
+        in_specs=[smem, smem] + [VMEM] * 13,
         out_specs=(hbm, hbm, VMEM),
         scratch_shapes=[
-            ext,
+            pltpu.VMEM(ext_shape.shape, F32),
             resid,
             pltpu.VMEM((tiles * 8, width), F32),
             pltpu.VMEM((6, tiles, width), F32),
             pltpu.VMEM((chunks, tiles * 8, LANES), F32),
             pltpu.VMEM((8, entries), F32),
-            near_table,
-            pltpu.SemaphoreType.DMA((1,)),
             pltpu.SemaphoreType.DMA((2,)),
         ],
         compiler_params=params,

time: 69.3 us -> 66 us (0.952)
  waiting for transfers between devices: 4.84 us -> 2.91 us
  Pallas kernels: 15.1 us -> 13.8 us
    ppermute x12, waiting for transfers between devices: 4.84 us -> 2.91 us  [exchange(): return [lax.ppermute(sent, *pairs[name]) for name in order]]
    pallas_call x4 -> x6, Pallas kernels: 11.5 us -> 10.1 us  [the longest x1 3.55 us: per_device(): pl.pallas_call(functools.partial(last_kernel, LAST_ORDER), out_shape=(jax...]
  transfers between devices with their start and end apart: 12 -> 12, of which waited for: 2 -> 2; matrix products, arithmetic and copies ran while one was open for 0% -> 0% of each run, Pallas kernels for 5% -> 8%
where the time goes in v4:
time: 66 us; the launch traced here: 65.7 us
  starting transfers between devices  27.4 us (42%)
  blocking collectives  20 us (30%)
  Pallas kernels  13.8 us (21%)
  waiting for transfers between devices  2.91 us (4%)
  between operations  1.52 us (2%)
    ppermute x12, starting transfers between devices, exchange(): return [lax.ppermute(sent, *pairs[name]) for name in order]  27.4 us
    all_to_all x1, blocking collectives, per_device(): parcels = lax.all_to_all(parcels, 'region', 0, 0, tiled=True)  20 us
    pallas_call x1, Pallas kernels, per_device(): pl.pallas_call(functools.partial(last_kernel, LAST_ORDER), out_shape=(jax...  3.55 us
    ppermute x12, waiting for transfers between devices, exchange(): return [lax.ppermute(sent, *pairs[name]) for name in order]  2.91 us
    pallas_call x1, Pallas kernels, per_device(): pl.pallas_call(first_rest_kernel, out_shape=(adj_shape, jax.ShapeDtypeStr...  2.87 us
    pallas_call x2, Pallas kernels, per_device(): pl.pallas_call(rest_kernel, out_shape=adj_shape, in_specs=[smem] * 3 + [V...  1.91 us
    pallas_call x1, Pallas kernels, per_device(): pl.pallas_call(first_kernel, out_shape=(adj_shape, sent_shape, jax.ShapeD...  1.82 us
    pallas_call x2, Pallas kernels, per_device(): pl.pallas_call(functools.partial(lead_kernel, ORDER), out_shape=(adj_shap...  1.74 us
  transfers between devices with their start and end apart: 12, of which 2 were waited for; matrix products, arithmetic and copies ran while one was open for 0% of the time, Pallas kernels for 8%

profile of v4, /device:TPU:1, one launch (start us, length us, event | category | flops | bytes accessed | tf_op | source)
XLA Modules:
  0.0 65.7 jit_solution(15778961532560610763)
XLA Ops:
  1.3 1.8 %first.1 = (f32[6,128,128]{2,1,0:T(8,128)S(1)}, f32[6,48,128]{2,1,0:T(8,128)S(1)}, f32[16,8,768]{2,1,0:T(8,128)S(1)}, bf16[16,8,8,768]{3,2,1,0:T(8,128)(2,1)S(1)...) custom-call(s32[1,8]{1,0:T(1,128)} %send_hbm.1, s32[4,16]{1,0:T(4,128)} %bitcast.12, ...), custom_call_target="tpu_custom_call" | custom-call | tf_op jit(solution)/shard_map/first/pallas_call | solution.py:329
  3.1 3.3 %collective-permute-start = (f32[6,48,128]{2,1,0:T(8,128)S(1)}, f32[6,48,128]{2,1,0:T(8,128)S(1)}, u32[]{:S(2)}, u32[]{:S(2)}) collective-permute-start(f32[6,48,128]{2,1,0:T(8,128)S(1)} %get-tuple-element.29), channel_id=1, source_target_pairs={{0,1},{1,0},{2,3},{3,2},{4,5},{5,4},{6,7},{7,6},{8,9},{9,8},{10,11... | collective-permute-start | bytes 442376 | tf_op jit(solution)/shard_map/ppermute | solution.py:299
  6.4 0.7 %collective-permute-start.1 = (f32[6,48,128]{2,1,0:T(8,128)S(1)}, f32[6,48,128]{2,1,0:T(8,128)S(1)}, u32[]{:S(2)}, u32[]{:S(2)}) collective-permute-start(f32[6,48,128]{2,1,0:T(8,128)S(1)} %get-tuple-element.29), channel_id=1, source_target_pairs={{8,16},{16,8},{24,32},{32,24},{40,48},{48,40},{56,64},{64,56},{72,... | collective-permute-start | bytes 442376 | tf_op jit(solution)/shard_map/ppermute | solution.py:299
  7.1 2.2 %collective-permute-start.2 = (f32[6,48,128]{2,1,0:T(8,128)S(1)}, f32[6,48,128]{2,1,0:T(8,128)S(1)}, u32[]{:S(2)}, u32[]{:S(2)}) collective-permute-start(f32[6,48,128]{2,1,0:T(8,128)S(1)} %get-tuple-element.29), channel_id=1, source_target_pairs={{0,8},{8,0},{16,24},{24,16},{32,40},{40,32},{48,56},{56,48},{64,72... | collective-permute-start | bytes 442376 | tf_op jit(solution)/shard_map/ppermute | solution.py:299
  9.3 3.6 %collective-permute-start.3 = (f32[6,48,128]{2,1,0:T(8,128)S(1)}, f32[6,48,128]{2,1,0:T(8,128)S(1)}, u32[]{:S(2)}, u32[]{:S(2)}) collective-permute-start(f32[6,48,128]{2,1,0:T(8,128)S(1)} %get-tuple-element.29), channel_id=1, source_target_pairs={{1,2},{2,1},{3,4},{4,3},{5,6},{6,5},{9,10},{10,9},{11,12},{12,11},... | collective-permute-start | bytes 442376 | tf_op jit(solution)/shard_map/ppermute | solution.py:299
  12.9 2.9 %first_rest.1 = (f32[6,128,128]{2,1,0:T(8,128)S(1)}, bf16[16,4,8,8,768]{4,3,2,1,0:T(8,128)(2,1)S(1)}) custom-call(s32[1,16]{1,0:T(1,128)S(4)} %get-tuple-element.24.listed_ref, s32[1]{0:T(128)S(6)} %copy.13.count_ref, f32[16,8,768]{2,1,0:T(8,128)S(1)} %get-tuple-element.22.rhs_ref, bf16[16,8,8,768]{3,2,1,0:T(8,128)(2,1)S(1)} %get-tuple-element.23.inv_ref, ...), custom_call_target="tpu_custom_call" | custom-call | bytes 12582912 | tf_op jit(solution)/shard_map/first_rest/pallas_call | solution.py:348
  15.8 0.0 collective-permute-done.1.h1
  15.8 0.9 %lead.2 = (f32[6,128,128]{2,1,0:T(8,128)S(1)}, f32[6,48,128]{2,1,0:T(8,128)S(1)}, f32[6,320,128]{2,1,0:T(8,128)S(1)}) custom-call(s32[4,16]{1,0:T(4,128)S(4)} %get-tuple-element.21.near_ref, s32[1,8]{1,0:T(1,128)S(4)} %get-tuple-element.27.send_ref, s32[1]{0:T(128)S(6)} %copy.13.count_ref, f32[16,8,768]{2,1,0:T(8,128)S(1)} %get-tuple-element.22.rhs_ref, ...), custom_call_target="tpu_custom_call" | custom-call | tf_op jit(solution)/shard_map/lead/pallas_call | solution.py:369
  16.7 0.1 collective-permute-start.4
  16.8 0.7 %collective-permute-start.5 = (f32[6,48,128]{2,1,0:T(8,128)S(1)}, f32[6,48,128]{2,1,0:T(8,128)S(1)}, u32[]{:S(2)}, u32[]{:S(2)}) collective-permute-start(f32[6,48,128]{2,1,0:T(8,128)S(1)} %get-tuple-element.32), channel_id=1, source_target_pairs={{8,16},{16,8},{24,32},{32,24},{40,48},{48,40},{56,64},{64,56},{72,... | collective-permute-start | bytes 442376 | tf_op jit(solution)/shard_map/ppermute | solution.py:299
  17.4 3.6 %collective-permute-start.6 = (f32[6,48,128]{2,1,0:T(8,128)S(1)}, f32[6,48,128]{2,1,0:T(8,128)S(1)}, u32[]{:S(2)}, u32[]{:S(2)}) collective-permute-start(f32[6,48,128]{2,1,0:T(8,128)S(1)} %get-tuple-element.32), channel_id=1, source_target_pairs={{0,8},{8,0},{16,24},{24,16},{32,40},{40,32},{48,56},{56,48},{64,72... | collective-permute-start | bytes 442376 | tf_op jit(solution)/shard_map/ppermute | solution.py:299
  21.1 4.2 %collective-permute-start.7 = (f32[6,48,128]{2,1,0:T(8,128)S(1)}, f32[6,48,128]{2,1,0:T(8,128)S(1)}, u32[]{:S(2)}, u32[]{:S(2)}) collective-permute-start(f32[6,48,128]{2,1,0:T(8,128)S(1)} %get-tuple-element.32), channel_id=1, source_target_pairs={{1,2},{2,1},{3,4},{4,3},{5,6},{6,5},{9,10},{10,9},{11,12},{12,11},... | collective-permute-start | bytes 442376 | tf_op jit(solution)/shard_map/ppermute | solution.py:299
  25.3 1.0 %rest.2.old_ref = f32[6,128,128]{2,1,0:T(8,128)S(1)} custom-call(s32[4,16]{1,0:T(4,128)S(4)} %get-tuple-element.21.near_ref, s32[1,16]{1,0:T(1,128)S(4)} %get-tuple-element.24.listed_ref, s32[1]{0:T(128)S(6)} %copy.13.count_ref, f32[16,8,768]{2,1,0:T(8,128)S(1)} %get-tuple-element.22.rhs_ref, bf16[16,8,8,768]{3,2,1,0:T(8,128)(2,1)S(1)} %get-tuple-element.23.inv_ref, ...), custom_call_target="tpu_custom_call" | custom-call | bytes 4194304 | tf_op jit(solution)/shard_map/rest/pallas_call | solution.py:379
  26.2 0.0 copy-start.1
  26.2 0.0 collective-permute-done.4.h0
  26.3 0.0 collective-permute-done.6.h2
  26.3 1.8 %collective-permute-done.7.h3 = f32[6,48,128]{2,1,0:T(8,128)S(1)} collective-permute-done((f32[6,48,128]{2,1,0:T(8,128)S(1)}, f32[6,48,128]{2,1,0:T(8,128)S(1)}, u32[]{:S(2)}, u32[]{:S(2)}) %collective-permute-start.7) | collective-permute-done | bytes 147488 | tf_op jit(solution)/shard_map/ppermute | solution.py:299
  28.1 0.9 %lead.3 = (f32[6,128,128]{2,1,0:T(8,128)S(1)}, f32[6,48,128]{2,1,0:T(8,128)S(1)}, f32[6,320,128]{2,1,0:T(8,128)S(1)}) custom-call(s32[4,16]{1,0:T(4,128)S(4)} %get-tuple-element.21.near_ref, s32[1,8]{1,0:T(1,128)S(4)} %get-tuple-element.27.send_ref, s32[1]{0:T(128)S(6)} %copy.13.count_ref, f32[16,8,768]{2,1,0:T(8,128)S(1)} %get-tuple-element.22.rhs_ref, ...), custom_call_target="tpu_custom_call" | custom-call | tf_op jit(solution)/shard_map/lead/pallas_call | solution.py:369
  29.0 0.0 copy-start
  29.0 0.0 copy-start.2
  29.0 0.0 copy-start.3
  29.0 0.1 collective-permute-start.10
  29.1 0.8 %collective-permute-start.11 = (f32[6,48,128]{2,1,0:T(8,128)S(1)}, f32[6,48,128]{2,1,0:T(8,128)S(1)}, u32[]{:S(2)}, u32[]{:S(2)}) collective-permute-start(f32[6,48,128]{2,1,0:T(8,128)S(1)} %get-tuple-element.35), channel_id=1, source_target_pairs={{8,16},{16,8},{24,32},{32,24},{40,48},{48,40},{56,64},{64,56},{72,... | collective-permute-start | bytes 442376 | tf_op jit(solution)/shard_map/ppermute | solution.py:299
  29.9 3.9 %collective-permute-start.8 = (f32[6,48,128]{2,1,0:T(8,128)S(1)}, f32[6,48,128]{2,1,0:T(8,128)S(1)}, u32[]{:S(2)}, u32[]{:S(2)}) collective-permute-start(f32[6,48,128]{2,1,0:T(8,128)S(1)} %get-tuple-element.35), channel_id=1, source_target_pairs={{0,8},{8,0},{16,24},{24,16},{32,40},{40,32},{48,56},{56,48},{64,72... | collective-permute-start | bytes 442376 | tf_op jit(solution)/shard_map/ppermute | solution.py:299
  33.8 4.3 %collective-permute-start.9 = (f32[6,48,128]{2,1,0:T(8,128)S(1)}, f32[6,48,128]{2,1,0:T(8,128)S(1)}, u32[]{:S(2)}, u32[]{:S(2)}) collective-permute-start(f32[6,48,128]{2,1,0:T(8,128)S(1)} %get-tuple-element.35), channel_id=1, source_target_pairs={{1,2},{2,1},{3,4},{4,3},{5,6},{6,5},{9,10},{10,9},{11,12},{12,11},... | collective-permute-start | bytes 442376 | tf_op jit(solution)/shard_map/ppermute | solution.py:299
  38.1 0.7 %rank.1.rank_hot_ref = bf16[128,1024]{1,0:T(8,128)(2,1)S(1)} custom-call(s32[1,1024]{1,0:T(1,128)S(1)} %bitcast.8), custom_call_target="tpu_custom_call" | custom-call | tf_op jit(solution)/shard_map/rank/pallas_call | solution.py:358
  38.8 1.0 %rest.3.old_ref = f32[6,128,128]{2,1,0:T(8,128)S(1)} custom-call(s32[4,16]{1,0:T(4,128)S(4)} %get-tuple-element.21.near_ref, s32[1,16]{1,0:T(1,128)S(4)} %get-tuple-element.24.listed_ref, s32[1]{0:T(128)S(6)} %copy.13.count_ref, f32[16,8,768]{2,1,0:T(8,128)S(1)} %get-tuple-element.22.rhs_ref, bf16[16,8,8,768]{3,2,1,0:T(8,128)(2,1)S(1)} %get-tuple-element.23.inv_ref, ...), custom_call_target="tpu_custom_call" | custom-call | bytes 4194304 | tf_op jit(solution)/shard_map/rest/pallas_call | solution.py:379
  39.8 0.0 collective-permute-done.11.h3
  39.8 1.1 %collective-permute-done.9.h1 = f32[6,48,128]{2,1,0:T(8,128)S(1)} collective-permute-done((f32[6,48,128]{2,1,0:T(8,128)S(1)}, f32[6,48,128]{2,1,0:T(8,128)S(1)}, u32[]{:S(2)}, u32[]{:S(2)}) %collective-permute-start.9) | collective-permute-done | bytes 147488 | tf_op jit(solution)/shard_map/ppermute | solution.py:299
  40.9 3.5 %last.1 = (f32[128,768]{1,0:T(8,128)}, f32[6,16,768]{2,1,0:T(8,128)}, f32[32,8,128]{2,1,0:T(8,128)S(1)}) custom-call(s32[4,16]{1,0:T(4,128)S(4)} %get-tuple-element.21.near_ref, s32[1]{0:T(128)S(6)} %copy.13.count_ref, f32[16,8,768]{2,1,0:T(8,128)S(1)} %get-tuple-element.22.rhs_ref, bf16[16,8,8,768]{3,2,1,0:T(8,128)(2,1)S(1)} %get-tuple-element.23.inv_ref, ...), custom_call_target="tpu_custom_call" | custom-call | tf_op jit(solution)/shard_map/last/pallas_call | solution.py:389
  44.5 20.0 %all_to_all.5.parcel_ref = f32[32,8,128]{2,1,0:T(8,128)S(1)} all-to-all(f32[32,8,128]{2,1,0:T(8,128)S(1)} %get-tuple-element.38), channel_id=1, replica_groups=mesh['region'=32,'sub'=8] {'region'}, dimensions={0} | all-to-all | bytes 262144 | tf_op jit(solution)/shard_map/all_to_all | solution.py:415
  64.5 1.2 %owner.1 = f32[6,1024]{1,0:T(8,128)} custom-call(f32[32,8,128]{2,1,0:T(8,128)S(1)} %all_to_all.5.parcel_ref), custom_call_target="tpu_custom_call" | custom-call | tf_op jit(solution)/shard_map/owner/pallas_call | solution.py:416
  (10 shorter events, 0.0 us)
Async XLA Ops:
  3.1 12.6 %collective-permute-start = (f32[6,48,128]{2,1,0:T(8,128)S(1)}, f32[6,48,128]{2,1,0:T(8,128)S(1)}, u32[]{:S(2)}, u32[]{:S(2)}) collective-permute-start(f32[6,48,128]{2,1,0:T(8,128)S(1)} %get-tuple-element.29), channel_id=1, source_target_pairs={{0,1},{1,0},{2,3},{3,2},{4,5},{5,4},{6,7},{7,6},{8,9},{9,8},{10,11... | collective-permute-start | bytes 442376 | tf_op jit(solution)/shard_map/ppermute | solution.py:299
  6.4 9.3 %collective-permute-start.1 = (f32[6,48,128]{2,1,0:T(8,128)S(1)}, f32[6,48,128]{2,1,0:T(8,128)S(1)}, u32[]{:S(2)}, u32[]{:S(2)}) collective-permute-start(f32[6,48,128]{2,1,0:T(8,128)S(1)} %get-tuple-element.29), channel_id=1, source_target_pairs={{8,16},{16,8},{24,32},{32,24},{40,48},{48,40},{56,64},{64,56},{72,... | collective-permute-start | bytes 442376 | tf_op jit(solution)/shard_map/ppermute | solution.py:299
  7.1 8.7 %collective-permute-start.2 = (f32[6,48,128]{2,1,0:T(8,128)S(1)}, f32[6,48,128]{2,1,0:T(8,128)S(1)}, u32[]{:S(2)}, u32[]{:S(2)}) collective-permute-start(f32[6,48,128]{2,1,0:T(8,128)S(1)} %get-tuple-element.29), channel_id=1, source_target_pairs={{0,8},{8,0},{16,24},{24,16},{32,40},{40,32},{48,56},{56,48},{64,72... | collective-permute-start | bytes 442376 | tf_op jit(solution)/shard_map/ppermute | solution.py:299
  9.3 6.5 %collective-permute-start.3 = (f32[6,48,128]{2,1,0:T(8,128)S(1)}, f32[6,48,128]{2,1,0:T(8,128)S(1)}, u32[]{:S(2)}, u32[]{:S(2)}) collective-permute-start(f32[6,48,128]{2,1,0:T(8,128)S(1)} %get-tuple-element.29), channel_id=1, source_target_pairs={{1,2},{2,1},{3,4},{4,3},{5,6},{6,5},{9,10},{10,9},{11,12},{12,11},... | collective-permute-start | bytes 442376 | tf_op jit(solution)/shard_map/ppermute | solution.py:299
  16.7 9.6 %collective-permute-start.4 = (f32[6,48,128]{2,1,0:T(8,128)S(1)}, f32[6,48,128]{2,1,0:T(8,128)S(1)}, u32[]{:S(2)}, u32[]{:S(2)}) collective-permute-start(f32[6,48,128]{2,1,0:T(8,128)S(1)} %get-tuple-element.32), channel_id=1, source_target_pairs={{0,1},{1,0},{2,3},{3,2},{4,5},{5,4},{6,7},{7,6},{8,9},{9,8},{10,11... | collective-permute-start | bytes 442376 | tf_op jit(solution)/shard_map/ppermute | solution.py:299
  16.8 9.5 %collective-permute-start.5 = (f32[6,48,128]{2,1,0:T(8,128)S(1)}, f32[6,48,128]{2,1,0:T(8,128)S(1)}, u32[]{:S(2)}, u32[]{:S(2)}) collective-permute-start(f32[6,48,128]{2,1,0:T(8,128)S(1)} %get-tuple-element.32), channel_id=1, source_target_pairs={{8,16},{16,8},{24,32},{32,24},{40,48},{48,40},{56,64},{64,56},{72,... | collective-permute-start | bytes 442376 | tf_op jit(solution)/shard_map/ppermute | solution.py:299
  17.4 8.8 %collective-permute-start.6 = (f32[6,48,128]{2,1,0:T(8,128)S(1)}, f32[6,48,128]{2,1,0:T(8,128)S(1)}, u32[]{:S(2)}, u32[]{:S(2)}) collective-permute-start(f32[6,48,128]{2,1,0:T(8,128)S(1)} %get-tuple-element.32), channel_id=1, source_target_pairs={{0,8},{8,0},{16,24},{24,16},{32,40},{40,32},{48,56},{56,48},{64,72... | collective-permute-start | bytes 442376 | tf_op jit(solution)/shard_map/ppermute | solution.py:299
  21.1 7.0 %collective-permute-start.7 = (f32[6,48,128]{2,1,0:T(8,128)S(1)}, f32[6,48,128]{2,1,0:T(8,128)S(1)}, u32[]{:S(2)}, u32[]{:S(2)}) collective-permute-start(f32[6,48,128]{2,1,0:T(8,128)S(1)} %get-tuple-element.32), channel_id=1, source_target_pairs={{1,2},{2,1},{3,4},{4,3},{5,6},{6,5},{9,10},{10,9},{11,12},{12,11},... | collective-permute-start | bytes 442376 | tf_op jit(solution)/shard_map/ppermute | solution.py:299
  26.2 11.9 %copy-start.1 = (s32[1024,1]{0,1:T(1,128)S(1)}, s32[1024,1]{0,1:T(1,128)}, u32[]{:S(2)}) copy-start(s32[1024,1]{0,1:T(1,128)} %param.18) | copy-start | bytes 12292
  29.0 11.9 %copy-start = (bf16[16,6,6,768]{3,0,2,1:T(8,128)(2,1)S(1)}, bf16[16,6,6,768]{3,0,2,1:T(8,128)(2,1)}, u32[]{:S(2)}) copy-start(bf16[16,6,6,768]{3,0,2,1:T(8,128)(2,1)} %param.16) | copy-start | bytes 2654212
  29.0 11.9 %copy-start.2 = (s32[1024]{0:T(1024)S(1)}, s32[1024]{0:T(1024)}, u32[]{:S(2)}) copy-start(s32[1024]{0:T(1024)} %param.17) | copy-start | bytes 12292
  29.0 11.9 %copy-start.3 = (s32[1024]{0:T(1024)S(1)}, s32[1024]{0:T(1024)}, u32[]{:S(2)}) copy-start(s32[1024]{0:T(1024)} %param.19) | copy-start | bytes 12292
  29.0 10.8 %collective-permute-start.10 = (f32[6,48,128]{2,1,0:T(8,128)S(1)}, f32[6,48,128]{2,1,0:T(8,128)S(1)}, u32[]{:S(2)}, u32[]{:S(2)}) collective-permute-start(f32[6,48,128]{2,1,0:T(8,128)S(1)} %get-tuple-element.35), channel_id=1, source_target_pairs={{0,1},{1,0},{2,3},{3,2},{4,5},{5,4},{6,7},{7,6},{8,9},{9,8},{10,11... | collective-permute-start | bytes 442376 | tf_op jit(solution)/shard_map/ppermute | solution.py:299
  29.1 10.7 %collective-permute-start.11 = (f32[6,48,128]{2,1,0:T(8,128)S(1)}, f32[6,48,128]{2,1,0:T(8,128)S(1)}, u32[]{:S(2)}, u32[]{:S(2)}) collective-permute-start(f32[6,48,128]{2,1,0:T(8,128)S(1)} %get-tuple-element.35), channel_id=1, source_target_pairs={{8,16},{16,8},{24,32},{32,24},{40,48},{48,40},{56,64},{64,56},{72,... | collective-permute-start | bytes 442376 | tf_op jit(solution)/shard_map/ppermute | solution.py:299
  29.9 9.9 %collective-permute-start.8 = (f32[6,48,128]{2,1,0:T(8,128)S(1)}, f32[6,48,128]{2,1,0:T(8,128)S(1)}, u32[]{:S(2)}, u32[]{:S(2)}) collective-permute-start(f32[6,48,128]{2,1,0:T(8,128)S(1)} %get-tuple-element.35), channel_id=1, source_target_pairs={{0,8},{8,0},{16,24},{24,16},{32,40},{40,32},{48,56},{56,48},{64,72... | collective-permute-start | bytes 442376 | tf_op jit(solution)/shard_map/ppermute | solution.py:299
  33.8 7.1 %collective-permute-start.9 = (f32[6,48,128]{2,1,0:T(8,128)S(1)}, f32[6,48,128]{2,1,0:T(8,128)S(1)}, u32[]{:S(2)}, u32[]{:S(2)}) collective-permute-start(f32[6,48,128]{2,1,0:T(8,128)S(1)} %get-tuple-element.35), channel_id=1, source_target_pairs={{1,2},{2,1},{3,4},{4,3},{5,6},{6,5},{9,10},{10,9},{11,12},{12,11},... | collective-permute-start | bytes 442376 | tf_op jit(solution)/shard_map/ppermute | solution.py:299

commit v5 on v4

--- a/solution.py
+++ b/solution.py
@@ -198,9 +198,8 @@
     entries = vertex_ref.shape[1]
     in_tile = lax.broadcasted_iota(jnp.int32, (8, LANES), 0)
 
-    @pl.loop(0, entries // LANES)
-    def _(g):
-        here = pl.ds(pl.multiple_of(g * LANES, LANES), LANES)
+    for g in range(entries // LANES):
+        here = lanes_of(g)
         vertex = vertex_ref[:, here]
         row = jnp.broadcast_to(vertex // LANES, (8, LANES))
         lane = jnp.broadcast_to(vertex % LANES, (8, LANES))

time: 66 us -> 65.8 us (level)
  no operation moved by 1% of the time
where the time goes in v5:
time: 65.8 us; the launch traced here: 65.4 us
  starting transfers between devices  27.4 us (42%)
  blocking collectives  20 us (30%)
  Pallas kernels  13.6 us (21%)
  waiting for transfers between devices  2.9 us (4%)
  between operations  1.52 us (2%)
    ppermute x12, starting transfers between devices, exchange(): return [lax.ppermute(sent, *pairs[name]) for name in order]  27.4 us
    all_to_all x1, blocking collectives, per_device(): parcels = lax.all_to_all(parcels, 'region', 0, 0, tiled=True)  20 us
    pallas_call x1, Pallas kernels, per_device(): pl.pallas_call(functools.partial(last_kernel, LAST_ORDER), out_shape=(jax...  3.35 us
    ppermute x12, waiting for transfers between devices, exchange(): return [lax.ppermute(sent, *pairs[name]) for name in order]  2.9 us
    pallas_call x1, Pallas kernels, per_device(): pl.pallas_call(first_rest_kernel, out_shape=(adj_shape, jax.ShapeDtypeStr...  2.87 us
    pallas_call x2, Pallas kernels, per_device(): pl.pallas_call(rest_kernel, out_shape=adj_shape, in_specs=[smem] * 3 + [V...  1.91 us
    pallas_call x1, Pallas kernels, per_device(): pl.pallas_call(first_kernel, out_shape=(adj_shape, sent_shape, jax.ShapeD...  1.82 us
    pallas_call x2, Pallas kernels, per_device(): pl.pallas_call(functools.partial(lead_kernel, ORDER), out_shape=(adj_shap...  1.77 us
  transfers between devices with their start and end apart: 12, of which 2 were waited for; matrix products, arithmetic and copies ran while one was open for 0% of the time, Pallas kernels for 8%

profile of v5, /device:TPU:1, one launch (start us, length us, event | category | flops | bytes accessed | tf_op | source)
XLA Modules:
  0.0 65.4 jit_solution(10180235728319258491)
XLA Ops:
  1.3 1.8 %first.1 = (f32[6,128,128]{2,1,0:T(8,128)S(1)}, f32[6,48,128]{2,1,0:T(8,128)S(1)}, f32[16,8,768]{2,1,0:T(8,128)S(1)}, bf16[16,8,8,768]{3,2,1,0:T(8,128)(2,1)S(1)...) custom-call(s32[1,8]{1,0:T(1,128)} %send_hbm.1, s32[4,16]{1,0:T(4,128)} %bitcast.12, ...), custom_call_target="tpu_custom_call" | custom-call | tf_op jit(solution)/shard_map/first/pallas_call | solution.py:328
  3.1 3.3 %collective-permute-start = (f32[6,48,128]{2,1,0:T(8,128)S(1)}, f32[6,48,128]{2,1,0:T(8,128)S(1)}, u32[]{:S(2)}, u32[]{:S(2)}) collective-permute-start(f32[6,48,128]{2,1,0:T(8,128)S(1)} %get-tuple-element.29), channel_id=1, source_target_pairs={{0,1},{1,0},{2,3},{3,2},{4,5},{5,4},{6,7},{7,6},{8,9},{9,8},{10,11... | collective-permute-start | bytes 442376 | tf_op jit(solution)/shard_map/ppermute | solution.py:298
  6.4 0.7 %collective-permute-start.1 = (f32[6,48,128]{2,1,0:T(8,128)S(1)}, f32[6,48,128]{2,1,0:T(8,128)S(1)}, u32[]{:S(2)}, u32[]{:S(2)}) collective-permute-start(f32[6,48,128]{2,1,0:T(8,128)S(1)} %get-tuple-element.29), channel_id=1, source_target_pairs={{8,16},{16,8},{24,32},{32,24},{40,48},{48,40},{56,64},{64,56},{72,... | collective-permute-start | bytes 442376 | tf_op jit(solution)/shard_map/ppermute | solution.py:298
  7.1 2.2 %collective-permute-start.2 = (f32[6,48,128]{2,1,0:T(8,128)S(1)}, f32[6,48,128]{2,1,0:T(8,128)S(1)}, u32[]{:S(2)}, u32[]{:S(2)}) collective-permute-start(f32[6,48,128]{2,1,0:T(8,128)S(1)} %get-tuple-element.29), channel_id=1, source_target_pairs={{0,8},{8,0},{16,24},{24,16},{32,40},{40,32},{48,56},{56,48},{64,72... | collective-permute-start | bytes 442376 | tf_op jit(solution)/shard_map/ppermute | solution.py:298
  9.3 3.6 %collective-permute-start.3 = (f32[6,48,128]{2,1,0:T(8,128)S(1)}, f32[6,48,128]{2,1,0:T(8,128)S(1)}, u32[]{:S(2)}, u32[]{:S(2)}) collective-permute-start(f32[6,48,128]{2,1,0:T(8,128)S(1)} %get-tuple-element.29), channel_id=1, source_target_pairs={{1,2},{2,1},{3,4},{4,3},{5,6},{6,5},{9,10},{10,9},{11,12},{12,11},... | collective-permute-start | bytes 442376 | tf_op jit(solution)/shard_map/ppermute | solution.py:298
  12.9 2.9 %first_rest.1 = (f32[6,128,128]{2,1,0:T(8,128)S(1)}, bf16[16,4,8,8,768]{4,3,2,1,0:T(8,128)(2,1)S(1)}) custom-call(s32[1,16]{1,0:T(1,128)S(4)} %get-tuple-element.24.listed_ref, s32[1]{0:T(128)S(6)} %copy.13.count_ref, f32[16,8,768]{2,1,0:T(8,128)S(1)} %get-tuple-element.22.rhs_ref, bf16[16,8,8,768]{3,2,1,0:T(8,128)(2,1)S(1)} %get-tuple-element.23.inv_ref, ...), custom_call_target="tpu_custom_call" | custom-call | bytes 12582912 | tf_op jit(solution)/shard_map/first_rest/pallas_call | solution.py:347
  15.7 0.0 collective-permute-done.h0
  15.8 0.0 collective-permute-done.2.h2
  15.8 0.0 collective-permute-done.3.h3
  15.8 0.9 %lead.2 = (f32[6,128,128]{2,1,0:T(8,128)S(1)}, f32[6,48,128]{2,1,0:T(8,128)S(1)}, f32[6,320,128]{2,1,0:T(8,128)S(1)}) custom-call(s32[4,16]{1,0:T(4,128)S(4)} %get-tuple-element.21.near_ref, s32[1,8]{1,0:T(1,128)S(4)} %get-tuple-element.27.send_ref, s32[1]{0:T(128)S(6)} %copy.13.count_ref, f32[16,8,768]{2,1,0:T(8,128)S(1)} %get-tuple-element.22.rhs_ref, ...), custom_call_target="tpu_custom_call" | custom-call | tf_op jit(solution)/shard_map/lead/pallas_call | solution.py:368
  16.7 0.1 collective-permute-start.4
  16.8 0.7 %collective-permute-start.5 = (f32[6,48,128]{2,1,0:T(8,128)S(1)}, f32[6,48,128]{2,1,0:T(8,128)S(1)}, u32[]{:S(2)}, u32[]{:S(2)}) collective-permute-start(f32[6,48,128]{2,1,0:T(8,128)S(1)} %get-tuple-element.32), channel_id=1, source_target_pairs={{8,16},{16,8},{24,32},{32,24},{40,48},{48,40},{56,64},{64,56},{72,... | collective-permute-start | bytes 442376 | tf_op jit(solution)/shard_map/ppermute | solution.py:298
  17.5 3.6 %collective-permute-start.6 = (f32[6,48,128]{2,1,0:T(8,128)S(1)}, f32[6,48,128]{2,1,0:T(8,128)S(1)}, u32[]{:S(2)}, u32[]{:S(2)}) collective-permute-start(f32[6,48,128]{2,1,0:T(8,128)S(1)} %get-tuple-element.32), channel_id=1, source_target_pairs={{0,8},{8,0},{16,24},{24,16},{32,40},{40,32},{48,56},{56,48},{64,72... | collective-permute-start | bytes 442376 | tf_op jit(solution)/shard_map/ppermute | solution.py:298
  21.1 4.2 %collective-permute-start.7 = (f32[6,48,128]{2,1,0:T(8,128)S(1)}, f32[6,48,128]{2,1,0:T(8,128)S(1)}, u32[]{:S(2)}, u32[]{:S(2)}) collective-permute-start(f32[6,48,128]{2,1,0:T(8,128)S(1)} %get-tuple-element.32), channel_id=1, source_target_pairs={{1,2},{2,1},{3,4},{4,3},{5,6},{6,5},{9,10},{10,9},{11,12},{12,11},... | collective-permute-start | bytes 442376 | tf_op jit(solution)/shard_map/ppermute | solution.py:298
  25.3 1.0 %rest.2.old_ref = f32[6,128,128]{2,1,0:T(8,128)S(1)} custom-call(s32[4,16]{1,0:T(4,128)S(4)} %get-tuple-element.21.near_ref, s32[1,16]{1,0:T(1,128)S(4)} %get-tuple-element.24.listed_ref, s32[1]{0:T(128)S(6)} %copy.13.count_ref, f32[16,8,768]{2,1,0:T(8,128)S(1)} %get-tuple-element.22.rhs_ref, bf16[16,8,8,768]{3,2,1,0:T(8,128)(2,1)S(1)} %get-tuple-element.23.inv_ref, ...), custom_call_target="tpu_custom_call" | custom-call | bytes 4194304 | tf_op jit(solution)/shard_map/rest/pallas_call | solution.py:378
  26.2 0.0 copy-start.1
  26.3 0.0 collective-permute-done.5.h1
  26.3 1.8 %collective-permute-done.7.h3 = f32[6,48,128]{2,1,0:T(8,128)S(1)} collective-permute-done((f32[6,48,128]{2,1,0:T(8,128)S(1)}, f32[6,48,128]{2,1,0:T(8,128)S(1)}, u32[]{:S(2)}, u32[]{:S(2)}) %collective-permute-start.7) | collective-permute-done | bytes 147488 | tf_op jit(solution)/shard_map/ppermute | solution.py:298
  28.1 0.9 %lead.3 = (f32[6,128,128]{2,1,0:T(8,128)S(1)}, f32[6,48,128]{2,1,0:T(8,128)S(1)}, f32[6,320,128]{2,1,0:T(8,128)S(1)}) custom-call(s32[4,16]{1,0:T(4,128)S(4)} %get-tuple-element.21.near_ref, s32[1,8]{1,0:T(1,128)S(4)} %get-tuple-element.27.send_ref, s32[1]{0:T(128)S(6)} %copy.13.count_ref, f32[16,8,768]{2,1,0:T(8,128)S(1)} %get-tuple-element.22.rhs_ref, ...), custom_call_target="tpu_custom_call" | custom-call | tf_op jit(solution)/shard_map/lead/pallas_call | solution.py:368
  29.0 0.0 copy-start
  29.0 0.0 copy-start.2
  29.0 0.0 copy-start.3
  29.0 0.1 collective-permute-start.10
  29.1 0.8 %collective-permute-start.11 = (f32[6,48,128]{2,1,0:T(8,128)S(1)}, f32[6,48,128]{2,1,0:T(8,128)S(1)}, u32[]{:S(2)}, u32[]{:S(2)}) collective-permute-start(f32[6,48,128]{2,1,0:T(8,128)S(1)} %get-tuple-element.35), channel_id=1, source_target_pairs={{8,16},{16,8},{24,32},{32,24},{40,48},{48,40},{56,64},{64,56},{72,... | collective-permute-start | bytes 442376 | tf_op jit(solution)/shard_map/ppermute | solution.py:298
  29.9 3.9 %collective-permute-start.8 = (f32[6,48,128]{2,1,0:T(8,128)S(1)}, f32[6,48,128]{2,1,0:T(8,128)S(1)}, u32[]{:S(2)}, u32[]{:S(2)}) collective-permute-start(f32[6,48,128]{2,1,0:T(8,128)S(1)} %get-tuple-element.35), channel_id=1, source_target_pairs={{0,8},{8,0},{16,24},{24,16},{32,40},{40,32},{48,56},{56,48},{64,72... | collective-permute-start | bytes 442376 | tf_op jit(solution)/shard_map/ppermute | solution.py:298
  33.8 4.3 %collective-permute-start.9 = (f32[6,48,128]{2,1,0:T(8,128)S(1)}, f32[6,48,128]{2,1,0:T(8,128)S(1)}, u32[]{:S(2)}, u32[]{:S(2)}) collective-permute-start(f32[6,48,128]{2,1,0:T(8,128)S(1)} %get-tuple-element.35), channel_id=1, source_target_pairs={{1,2},{2,1},{3,4},{4,3},{5,6},{6,5},{9,10},{10,9},{11,12},{12,11},... | collective-permute-start | bytes 442376 | tf_op jit(solution)/shard_map/ppermute | solution.py:298
  38.1 0.7 %rank.1.rank_hot_ref = bf16[128,1024]{1,0:T(8,128)(2,1)S(1)} custom-call(s32[1,1024]{1,0:T(1,128)S(1)} %bitcast.8), custom_call_target="tpu_custom_call" | custom-call | tf_op jit(solution)/shard_map/rank/pallas_call | solution.py:357
  38.9 1.0 %rest.3.old_ref = f32[6,128,128]{2,1,0:T(8,128)S(1)} custom-call(s32[4,16]{1,0:T(4,128)S(4)} %get-tuple-element.21.near_ref, s32[1,16]{1,0:T(1,128)S(4)} %get-tuple-element.24.listed_ref, s32[1]{0:T(128)S(6)} %copy.13.count_ref, f32[16,8,768]{2,1,0:T(8,128)S(1)} %get-tuple-element.22.rhs_ref, bf16[16,8,8,768]{3,2,1,0:T(8,128)(2,1)S(1)} %get-tuple-element.23.inv_ref, ...), custom_call_target="tpu_custom_call" | custom-call | bytes 4194304 | tf_op jit(solution)/shard_map/rest/pallas_call | solution.py:378
  39.9 1.1 %collective-permute-done.9.h1 = f32[6,48,128]{2,1,0:T(8,128)S(1)} collective-permute-done((f32[6,48,128]{2,1,0:T(8,128)S(1)}, f32[6,48,128]{2,1,0:T(8,128)S(1)}, u32[]{:S(2)}, u32[]{:S(2)}) %collective-permute-start.9) | collective-permute-done | bytes 147488 | tf_op jit(solution)/shard_map/ppermute | solution.py:298
  40.9 3.3 %last.1 = (f32[128,768]{1,0:T(8,128)}, f32[6,16,768]{2,1,0:T(8,128)}, f32[32,8,128]{2,1,0:T(8,128)S(1)}) custom-call(s32[4,16]{1,0:T(4,128)S(4)} %get-tuple-element.21.near_ref, s32[1]{0:T(128)S(6)} %copy.13.count_ref, f32[16,8,768]{2,1,0:T(8,128)S(1)} %get-tuple-element.22.rhs_ref, bf16[16,8,8,768]{3,2,1,0:T(8,128)(2,1)S(1)} %get-tuple-element.23.inv_ref, ...), custom_call_target="tpu_custom_call" | custom-call | tf_op jit(solution)/shard_map/last/pallas_call | solution.py:388
  44.3 20.0 %all_to_all.5.parcel_ref = f32[32,8,128]{2,1,0:T(8,128)S(1)} all-to-all(f32[32,8,128]{2,1,0:T(8,128)S(1)} %get-tuple-element.38), channel_id=1, replica_groups=mesh['region'=32,'sub'=8] {'region'}, dimensions={0} | all-to-all | bytes 262144 | tf_op jit(solution)/shard_map/all_to_all | solution.py:414
  64.3 1.2 %owner.1 = f32[6,1024]{1,0:T(8,128)} custom-call(f32[32,8,128]{2,1,0:T(8,128)S(1)} %all_to_all.5.parcel_ref), custom_call_target="tpu_custom_call" | custom-call | tf_op jit(solution)/shard_map/owner/pallas_call | solution.py:415
  (10 shorter events, 0.0 us)
Async XLA Ops:
  3.1 12.6 %collective-permute-start = (f32[6,48,128]{2,1,0:T(8,128)S(1)}, f32[6,48,128]{2,1,0:T(8,128)S(1)}, u32[]{:S(2)}, u32[]{:S(2)}) collective-permute-start(f32[6,48,128]{2,1,0:T(8,128)S(1)} %get-tuple-element.29), channel_id=1, source_target_pairs={{0,1},{1,0},{2,3},{3,2},{4,5},{5,4},{6,7},{7,6},{8,9},{9,8},{10,11... | collective-permute-start | bytes 442376 | tf_op jit(solution)/shard_map/ppermute | solution.py:298
  6.4 9.3 %collective-permute-start.1 = (f32[6,48,128]{2,1,0:T(8,128)S(1)}, f32[6,48,128]{2,1,0:T(8,128)S(1)}, u32[]{:S(2)}, u32[]{:S(2)}) collective-permute-start(f32[6,48,128]{2,1,0:T(8,128)S(1)} %get-tuple-element.29), channel_id=1, source_target_pairs={{8,16},{16,8},{24,32},{32,24},{40,48},{48,40},{56,64},{64,56},{72,... | collective-permute-start | bytes 442376 | tf_op jit(solution)/shard_map/ppermute | solution.py:298
  7.1 8.7 %collective-permute-start.2 = (f32[6,48,128]{2,1,0:T(8,128)S(1)}, f32[6,48,128]{2,1,0:T(8,128)S(1)}, u32[]{:S(2)}, u32[]{:S(2)}) collective-permute-start(f32[6,48,128]{2,1,0:T(8,128)S(1)} %get-tuple-element.29), channel_id=1, source_target_pairs={{0,8},{8,0},{16,24},{24,16},{32,40},{40,32},{48,56},{56,48},{64,72... | collective-permute-start | bytes 442376 | tf_op jit(solution)/shard_map/ppermute | solution.py:298
  9.3 6.5 %collective-permute-start.3 = (f32[6,48,128]{2,1,0:T(8,128)S(1)}, f32[6,48,128]{2,1,0:T(8,128)S(1)}, u32[]{:S(2)}, u32[]{:S(2)}) collective-permute-start(f32[6,48,128]{2,1,0:T(8,128)S(1)} %get-tuple-element.29), channel_id=1, source_target_pairs={{1,2},{2,1},{3,4},{4,3},{5,6},{6,5},{9,10},{10,9},{11,12},{12,11},... | collective-permute-start | bytes 442376 | tf_op jit(solution)/shard_map/ppermute | solution.py:298
  16.7 9.6 %collective-permute-start.4 = (f32[6,48,128]{2,1,0:T(8,128)S(1)}, f32[6,48,128]{2,1,0:T(8,128)S(1)}, u32[]{:S(2)}, u32[]{:S(2)}) collective-permute-start(f32[6,48,128]{2,1,0:T(8,128)S(1)} %get-tuple-element.32), channel_id=1, source_target_pairs={{0,1},{1,0},{2,3},{3,2},{4,5},{5,4},{6,7},{7,6},{8,9},{9,8},{10,11... | collective-permute-start | bytes 442376 | tf_op jit(solution)/shard_map/ppermute | solution.py:298
  16.8 9.5 %collective-permute-start.5 = (f32[6,48,128]{2,1,0:T(8,128)S(1)}, f32[6,48,128]{2,1,0:T(8,128)S(1)}, u32[]{:S(2)}, u32[]{:S(2)}) collective-permute-start(f32[6,48,128]{2,1,0:T(8,128)S(1)} %get-tuple-element.32), channel_id=1, source_target_pairs={{8,16},{16,8},{24,32},{32,24},{40,48},{48,40},{56,64},{64,56},{72,... | collective-permute-start | bytes 442376 | tf_op jit(solution)/shard_map/ppermute | solution.py:298
  17.5 8.8 %collective-permute-start.6 = (f32[6,48,128]{2,1,0:T(8,128)S(1)}, f32[6,48,128]{2,1,0:T(8,128)S(1)}, u32[]{:S(2)}, u32[]{:S(2)}) collective-permute-start(f32[6,48,128]{2,1,0:T(8,128)S(1)} %get-tuple-element.32), channel_id=1, source_target_pairs={{0,8},{8,0},{16,24},{24,16},{32,40},{40,32},{48,56},{56,48},{64,72... | collective-permute-start | bytes 442376 | tf_op jit(solution)/shard_map/ppermute | solution.py:298
  21.1 7.0 %collective-permute-start.7 = (f32[6,48,128]{2,1,0:T(8,128)S(1)}, f32[6,48,128]{2,1,0:T(8,128)S(1)}, u32[]{:S(2)}, u32[]{:S(2)}) collective-permute-start(f32[6,48,128]{2,1,0:T(8,128)S(1)} %get-tuple-element.32), channel_id=1, source_target_pairs={{1,2},{2,1},{3,4},{4,3},{5,6},{6,5},{9,10},{10,9},{11,12},{12,11},... | collective-permute-start | bytes 442376 | tf_op jit(solution)/shard_map/ppermute | solution.py:298
  26.2 11.9 %copy-start.1 = (s32[1024,1]{0,1:T(1,128)S(1)}, s32[1024,1]{0,1:T(1,128)}, u32[]{:S(2)}) copy-start(s32[1024,1]{0,1:T(1,128)} %param.18) | copy-start | bytes 12292
  29.0 12.0 %copy-start = (bf16[16,6,6,768]{3,0,2,1:T(8,128)(2,1)S(1)}, bf16[16,6,6,768]{3,0,2,1:T(8,128)(2,1)}, u32[]{:S(2)}) copy-start(bf16[16,6,6,768]{3,0,2,1:T(8,128)(2,1)} %param.16) | copy-start | bytes 2654212
  29.0 12.0 %copy-start.2 = (s32[1024]{0:T(1024)S(1)}, s32[1024]{0:T(1024)}, u32[]{:S(2)}) copy-start(s32[1024]{0:T(1024)} %param.17) | copy-start | bytes 12292
  29.0 11.9 %copy-start.3 = (s32[1024]{0:T(1024)S(1)}, s32[1024]{0:T(1024)}, u32[]{:S(2)}) copy-start(s32[1024]{0:T(1024)} %param.19) | copy-start | bytes 12292
  29.0 10.8 %collective-permute-start.10 = (f32[6,48,128]{2,1,0:T(8,128)S(1)}, f32[6,48,128]{2,1,0:T(8,128)S(1)}, u32[]{:S(2)}, u32[]{:S(2)}) collective-permute-start(f32[6,48,128]{2,1,0:T(8,128)S(1)} %get-tuple-element.35), channel_id=1, source_target_pairs={{0,1},{1,0},{2,3},{3,2},{4,5},{5,4},{6,7},{7,6},{8,9},{9,8},{10,11... | collective-permute-start | bytes 442376 | tf_op jit(solution)/shard_map/ppermute | solution.py:298
  29.1 10.7 %collective-permute-start.11 = (f32[6,48,128]{2,1,0:T(8,128)S(1)}, f32[6,48,128]{2,1,0:T(8,128)S(1)}, u32[]{:S(2)}, u32[]{:S(2)}) collective-permute-start(f32[6,48,128]{2,1,0:T(8,128)S(1)} %get-tuple-element.35), channel_id=1, source_target_pairs={{8,16},{16,8},{24,32},{32,24},{40,48},{48,40},{56,64},{64,56},{72,... | collective-permute-start | bytes 442376 | tf_op jit(solution)/shard_map/ppermute | solution.py:298
  29.9 9.9 %collective-permute-start.8 = (f32[6,48,128]{2,1,0:T(8,128)S(1)}, f32[6,48,128]{2,1,0:T(8,128)S(1)}, u32[]{:S(2)}, u32[]{:S(2)}) collective-permute-start(f32[6,48,128]{2,1,0:T(8,128)S(1)} %get-tuple-element.35), channel_id=1, source_target_pairs={{0,8},{8,0},{16,24},{24,16},{32,40},{40,32},{48,56},{56,48},{64,72... | collective-permute-start | bytes 442376 | tf_op jit(solution)/shard_map/ppermute | solution.py:298
  33.8 7.1 %collective-permute-start.9 = (f32[6,48,128]{2,1,0:T(8,128)S(1)}, f32[6,48,128]{2,1,0:T(8,128)S(1)}, u32[]{:S(2)}, u32[]{:S(2)}) collective-permute-start(f32[6,48,128]{2,1,0:T(8,128)S(1)} %get-tuple-element.35), channel_id=1, source_target_pairs={{1,2},{2,1},{3,4},{4,3},{5,6},{6,5},{9,10},{10,9},{11,12},{12,11},... | collective-permute-start | bytes 442376 | tf_op jit(solution)/shard_map/ppermute | solution.py:298

commit v6 on v5

--- a/solution.py
+++ b/solution.py
@@ -13,8 +13,8 @@
 CAP = 128
 LANES = 128
 
-ORDER = ("sa", "rb", "ra", "sb")
-LAST_ORDER = ("ra", "sb", "sa", "rb")
+ORDER = ("rb", "ra", "sb", "sa")
+LAST_ORDER = ("sb", "sa", "rb", "ra")
 
 F32 = jnp.float32
 BF16 = jnp.bfloat16

time: 65.8 us -> 64.8 us (0.985)
  transfers between devices with their start and end apart: 12 -> 12, of which waited for: 2 -> 2; matrix products, arithmetic and copies ran while one was open for 0% -> 0% of each run, Pallas kernels for 8% -> 9%
where the time goes in v6:
time: 64.8 us; the launch traced here: 64.5 us
  starting transfers between devices  27.2 us (42%)
  blocking collectives  19.5 us (30%)
  Pallas kernels  13.6 us (21%)
  waiting for transfers between devices  2.73 us (4%)
  between operations  1.52 us (2%)
    ppermute x12, starting transfers between devices, exchange(): return [lax.ppermute(sent, *pairs[name]) for name in order]  27.2 us
    all_to_all x1, blocking collectives, per_device(): parcels = lax.all_to_all(parcels, 'region', 0, 0, tiled=True)  19.5 us
    pallas_call x1, Pallas kernels, per_device(): pl.pallas_call(functools.partial(last_kernel, LAST_ORDER), out_shape=(jax...  3.33 us
    pallas_call x1, Pallas kernels, per_device(): pl.pallas_call(first_rest_kernel, out_shape=(adj_shape, jax.ShapeDtypeStr...  2.87 us
    ppermute x12, waiting for transfers between devices, exchange(): return [lax.ppermute(sent, *pairs[name]) for name in order]  2.73 us
    pallas_call x2, Pallas kernels, per_device(): pl.pallas_call(rest_kernel, out_shape=adj_shape, in_specs=[smem] * 3 + [V...  1.91 us
    pallas_call x1, Pallas kernels, per_device(): pl.pallas_call(first_kernel, out_shape=(adj_shape, sent_shape, jax.ShapeD...  1.82 us
    pallas_call x2, Pallas kernels, per_device(): pl.pallas_call(functools.partial(lead_kernel, ORDER), out_shape=(adj_shap...  1.74 us
  transfers between devices with their start and end apart: 12, of which 2 were waited for; matrix products, arithmetic and copies ran while one was open for 0% of the time, Pallas kernels for 9%

profile of v6, /device:TPU:1, one launch (start us, length us, event | category | flops | bytes accessed | tf_op | source)
XLA Modules:
  0.0 64.5 jit_solution(10653667015457596377)
XLA Ops:
  1.3 1.8 %first.1 = (f32[6,128,128]{2,1,0:T(8,128)S(1)}, f32[6,48,128]{2,1,0:T(8,128)S(1)}, f32[16,8,768]{2,1,0:T(8,128)S(1)}, bf16[16,8,8,768]{3,2,1,0:T(8,128)(2,1)S(1)...) custom-call(s32[1,8]{1,0:T(1,128)} %send_hbm.1, s32[4,16]{1,0:T(4,128)} %bitcast.12, ...), custom_call_target="tpu_custom_call" | custom-call | tf_op jit(solution)/shard_map/first/pallas_call | solution.py:328
  3.1 0.7 %collective-permute-start = (f32[6,48,128]{2,1,0:T(8,128)S(1)}, f32[6,48,128]{2,1,0:T(8,128)S(1)}, u32[]{:S(2)}, u32[]{:S(2)}) collective-permute-start(f32[6,48,128]{2,1,0:T(8,128)S(1)} %get-tuple-element.29), channel_id=1, source_target_pairs={{8,16},{16,8},{24,32},{32,24},{40,48},{48,40},{56,64},{64,56},{72,... | collective-permute-start | bytes 442376 | tf_op jit(solution)/shard_map/ppermute | solution.py:298
  3.8 4.7 %collective-permute-start.1 = (f32[6,48,128]{2,1,0:T(8,128)S(1)}, f32[6,48,128]{2,1,0:T(8,128)S(1)}, u32[]{:S(2)}, u32[]{:S(2)}) collective-permute-start(f32[6,48,128]{2,1,0:T(8,128)S(1)} %get-tuple-element.29), channel_id=1, source_target_pairs={{0,8},{8,0},{16,24},{24,16},{32,40},{40,32},{48,56},{56,48},{64,72... | collective-permute-start | bytes 442376 | tf_op jit(solution)/shard_map/ppermute | solution.py:298
  8.5 4.2 %collective-permute-start.2 = (f32[6,48,128]{2,1,0:T(8,128)S(1)}, f32[6,48,128]{2,1,0:T(8,128)S(1)}, u32[]{:S(2)}, u32[]{:S(2)}) collective-permute-start(f32[6,48,128]{2,1,0:T(8,128)S(1)} %get-tuple-element.29), channel_id=1, source_target_pairs={{1,2},{2,1},{3,4},{4,3},{5,6},{6,5},{9,10},{10,9},{11,12},{12,11},... | collective-permute-start | bytes 442376 | tf_op jit(solution)/shard_map/ppermute | solution.py:298
  12.8 0.1 collective-permute-start.3
  12.9 2.9 %first_rest.1 = (f32[6,128,128]{2,1,0:T(8,128)S(1)}, bf16[16,4,8,8,768]{4,3,2,1,0:T(8,128)(2,1)S(1)}) custom-call(s32[1,16]{1,0:T(1,128)S(4)} %get-tuple-element.24.listed_ref, s32[1]{0:T(128)S(6)} %copy.13.count_ref, f32[16,8,768]{2,1,0:T(8,128)S(1)} %get-tuple-element.22.rhs_ref, bf16[16,8,8,768]{3,2,1,0:T(8,128)(2,1)S(1)} %get-tuple-element.23.inv_ref, ...), custom_call_target="tpu_custom_call" | custom-call | bytes 12582912 | tf_op jit(solution)/shard_map/first_rest/pallas_call | solution.py:347
  15.8 0.0 collective-permute-done.h0
  15.8 0.0 collective-permute-done.2.h2
  15.8 0.0 collective-permute-done.3.h3
  15.8 0.9 %lead.2 = (f32[6,128,128]{2,1,0:T(8,128)S(1)}, f32[6,48,128]{2,1,0:T(8,128)S(1)}, f32[6,320,128]{2,1,0:T(8,128)S(1)}) custom-call(s32[4,16]{1,0:T(4,128)S(4)} %get-tuple-element.21.near_ref, s32[1,8]{1,0:T(1,128)S(4)} %get-tuple-element.27.send_ref, s32[1]{0:T(128)S(6)} %copy.13.count_ref, f32[16,8,768]{2,1,0:T(8,128)S(1)} %get-tuple-element.22.rhs_ref, ...), custom_call_target="tpu_custom_call" | custom-call | tf_op jit(solution)/shard_map/lead/pallas_call | solution.py:368
  16.7 0.7 %collective-permute-start.4 = (f32[6,48,128]{2,1,0:T(8,128)S(1)}, f32[6,48,128]{2,1,0:T(8,128)S(1)}, u32[]{:S(2)}, u32[]{:S(2)}) collective-permute-start(f32[6,48,128]{2,1,0:T(8,128)S(1)} %get-tuple-element.32), channel_id=1, source_target_pairs={{8,16},{16,8},{24,32},{32,24},{40,48},{48,40},{56,64},{64,56},{72,... | collective-permute-start | bytes 442376 | tf_op jit(solution)/shard_map/ppermute | solution.py:298
  17.4 3.6 %collective-permute-start.5 = (f32[6,48,128]{2,1,0:T(8,128)S(1)}, f32[6,48,128]{2,1,0:T(8,128)S(1)}, u32[]{:S(2)}, u32[]{:S(2)}) collective-permute-start(f32[6,48,128]{2,1,0:T(8,128)S(1)} %get-tuple-element.32), channel_id=1, source_target_pairs={{0,8},{8,0},{16,24},{24,16},{32,40},{40,32},{48,56},{56,48},{64,72... | collective-permute-start | bytes 442376 | tf_op jit(solution)/shard_map/ppermute | solution.py:298
  21.0 4.1 %collective-permute-start.6 = (f32[6,48,128]{2,1,0:T(8,128)S(1)}, f32[6,48,128]{2,1,0:T(8,128)S(1)}, u32[]{:S(2)}, u32[]{:S(2)}) collective-permute-start(f32[6,48,128]{2,1,0:T(8,128)S(1)} %get-tuple-element.32), channel_id=1, source_target_pairs={{1,2},{2,1},{3,4},{4,3},{5,6},{6,5},{9,10},{10,9},{11,12},{12,11},... | collective-permute-start | bytes 442376 | tf_op jit(solution)/shard_map/ppermute | solution.py:298
  25.0 0.1 collective-permute-start.7
  25.1 1.0 %rest.2.old_ref = f32[6,128,128]{2,1,0:T(8,128)S(1)} custom-call(s32[4,16]{1,0:T(4,128)S(4)} %get-tuple-element.21.near_ref, s32[1,16]{1,0:T(1,128)S(4)} %get-tuple-element.24.listed_ref, s32[1]{0:T(128)S(6)} %copy.13.count_ref, f32[16,8,768]{2,1,0:T(8,128)S(1)} %get-tuple-element.22.rhs_ref, bf16[16,8,8,768]{3,2,1,0:T(8,128)(2,1)S(1)} %get-tuple-element.23.inv_ref, ...), custom_call_target="tpu_custom_call" | custom-call | bytes 4194304 | tf_op jit(solution)/shard_map/rest/pallas_call | solution.py:378
  26.1 0.0 copy-start.1
  26.1 0.0 collective-permute-done.4.h0
  26.1 1.7 %collective-permute-done.6.h2 = f32[6,48,128]{2,1,0:T(8,128)S(1)} collective-permute-done((f32[6,48,128]{2,1,0:T(8,128)S(1)}, f32[6,48,128]{2,1,0:T(8,128)S(1)}, u32[]{:S(2)}, u32[]{:S(2)}) %collective-permute-start.6) | collective-permute-done | bytes 147488 | tf_op jit(solution)/shard_map/ppermute | solution.py:298
  27.9 0.9 %lead.3 = (f32[6,128,128]{2,1,0:T(8,128)S(1)}, f32[6,48,128]{2,1,0:T(8,128)S(1)}, f32[6,320,128]{2,1,0:T(8,128)S(1)}) custom-call(s32[4,16]{1,0:T(4,128)S(4)} %get-tuple-element.21.near_ref, s32[1,8]{1,0:T(1,128)S(4)} %get-tuple-element.27.send_ref, s32[1]{0:T(128)S(6)} %copy.13.count_ref, f32[16,8,768]{2,1,0:T(8,128)S(1)} %get-tuple-element.22.rhs_ref, ...), custom_call_target="tpu_custom_call" | custom-call | tf_op jit(solution)/shard_map/lead/pallas_call | solution.py:368
  28.7 0.0 copy-start
  28.7 0.0 copy-start.2
  28.7 0.0 copy-start.3
  28.8 0.8 %collective-permute-start.10 = (f32[6,48,128]{2,1,0:T(8,128)S(1)}, f32[6,48,128]{2,1,0:T(8,128)S(1)}, u32[]{:S(2)}, u32[]{:S(2)}) collective-permute-start(f32[6,48,128]{2,1,0:T(8,128)S(1)} %get-tuple-element.35), channel_id=1, source_target_pairs={{8,16},{16,8},{24,32},{32,24},{40,48},{48,40},{56,64},{64,56},{72,... | collective-permute-start | bytes 442376 | tf_op jit(solution)/shard_map/ppermute | solution.py:298
  29.6 3.9 %collective-permute-start.11 = (f32[6,48,128]{2,1,0:T(8,128)S(1)}, f32[6,48,128]{2,1,0:T(8,128)S(1)}, u32[]{:S(2)}, u32[]{:S(2)}) collective-permute-start(f32[6,48,128]{2,1,0:T(8,128)S(1)} %get-tuple-element.35), channel_id=1, source_target_pairs={{0,8},{8,0},{16,24},{24,16},{32,40},{40,32},{48,56},{56,48},{64,72... | collective-permute-start | bytes 442376 | tf_op jit(solution)/shard_map/ppermute | solution.py:298
  33.5 4.2 %collective-permute-start.8 = (f32[6,48,128]{2,1,0:T(8,128)S(1)}, f32[6,48,128]{2,1,0:T(8,128)S(1)}, u32[]{:S(2)}, u32[]{:S(2)}) collective-permute-start(f32[6,48,128]{2,1,0:T(8,128)S(1)} %get-tuple-element.35), channel_id=1, source_target_pairs={{1,2},{2,1},{3,4},{4,3},{5,6},{6,5},{9,10},{10,9},{11,12},{12,11},... | collective-permute-start | bytes 442376 | tf_op jit(solution)/shard_map/ppermute | solution.py:298
  37.7 0.1 collective-permute-start.9
  37.8 0.7 %rank.1.rank_hot_ref = bf16[128,1024]{1,0:T(8,128)(2,1)S(1)} custom-call(s32[1,1024]{1,0:T(1,128)S(1)} %bitcast.8), custom_call_target="tpu_custom_call" | custom-call | tf_op jit(solution)/shard_map/rank/pallas_call | solution.py:357
  38.5 1.0 %rest.3.old_ref = f32[6,128,128]{2,1,0:T(8,128)S(1)} custom-call(s32[4,16]{1,0:T(4,128)S(4)} %get-tuple-element.21.near_ref, s32[1,16]{1,0:T(1,128)S(4)} %get-tuple-element.24.listed_ref, s32[1]{0:T(128)S(6)} %copy.13.count_ref, f32[16,8,768]{2,1,0:T(8,128)S(1)} %get-tuple-element.22.rhs_ref, bf16[16,8,8,768]{3,2,1,0:T(8,128)(2,1)S(1)} %get-tuple-element.23.inv_ref, ...), custom_call_target="tpu_custom_call" | custom-call | bytes 4194304 | tf_op jit(solution)/shard_map/rest/pallas_call | solution.py:378
  39.5 1.0 %collective-permute-done.8.h0 = f32[6,48,128]{2,1,0:T(8,128)S(1)} collective-permute-done((f32[6,48,128]{2,1,0:T(8,128)S(1)}, f32[6,48,128]{2,1,0:T(8,128)S(1)}, u32[]{:S(2)}, u32[]{:S(2)}) %collective-permute-start.8) | collective-permute-done | bytes 147488 | tf_op jit(solution)/shard_map/ppermute | solution.py:298
  40.5 3.3 %last.1 = (f32[128,768]{1,0:T(8,128)}, f32[6,16,768]{2,1,0:T(8,128)}, f32[32,8,128]{2,1,0:T(8,128)S(1)}) custom-call(s32[4,16]{1,0:T(4,128)S(4)} %get-tuple-element.21.near_ref, s32[1]{0:T(128)S(6)} %copy.13.count_ref, f32[16,8,768]{2,1,0:T(8,128)S(1)} %get-tuple-element.22.rhs_ref, bf16[16,8,8,768]{3,2,1,0:T(8,128)(2,1)S(1)} %get-tuple-element.23.inv_ref, ...), custom_call_target="tpu_custom_call" | custom-call | tf_op jit(solution)/shard_map/last/pallas_call | solution.py:388
  43.9 19.5 %all_to_all.5.parcel_ref = f32[32,8,128]{2,1,0:T(8,128)S(1)} all-to-all(f32[32,8,128]{2,1,0:T(8,128)S(1)} %get-tuple-element.38), channel_id=1, replica_groups=mesh['region'=32,'sub'=8] {'region'}, dimensions={0} | all-to-all | bytes 262144 | tf_op jit(solution)/shard_map/all_to_all | solution.py:414
  63.3 1.2 %owner.1 = f32[6,1024]{1,0:T(8,128)} custom-call(f32[32,8,128]{2,1,0:T(8,128)S(1)} %all_to_all.5.parcel_ref), custom_call_target="tpu_custom_call" | custom-call | tf_op jit(solution)/shard_map/owner/pallas_call | solution.py:415
  (10 shorter events, 0.0 us)
Async XLA Ops:
  3.1 12.6 %collective-permute-start = (f32[6,48,128]{2,1,0:T(8,128)S(1)}, f32[6,48,128]{2,1,0:T(8,128)S(1)}, u32[]{:S(2)}, u32[]{:S(2)}) collective-permute-start(f32[6,48,128]{2,1,0:T(8,128)S(1)} %get-tuple-element.29), channel_id=1, source_target_pairs={{8,16},{16,8},{24,32},{32,24},{40,48},{48,40},{56,64},{64,56},{72,... | collective-permute-start | bytes 442376 | tf_op jit(solution)/shard_map/ppermute | solution.py:298
  3.8 12.0 %collective-permute-start.1 = (f32[6,48,128]{2,1,0:T(8,128)S(1)}, f32[6,48,128]{2,1,0:T(8,128)S(1)}, u32[]{:S(2)}, u32[]{:S(2)}) collective-permute-start(f32[6,48,128]{2,1,0:T(8,128)S(1)} %get-tuple-element.29), channel_id=1, source_target_pairs={{0,8},{8,0},{16,24},{24,16},{32,40},{40,32},{48,56},{56,48},{64,72... | collective-permute-start | bytes 442376 | tf_op jit(solution)/shard_map/ppermute | solution.py:298
  8.5 7.2 %collective-permute-start.2 = (f32[6,48,128]{2,1,0:T(8,128)S(1)}, f32[6,48,128]{2,1,0:T(8,128)S(1)}, u32[]{:S(2)}, u32[]{:S(2)}) collective-permute-start(f32[6,48,128]{2,1,0:T(8,128)S(1)} %get-tuple-element.29), channel_id=1, source_target_pairs={{1,2},{2,1},{3,4},{4,3},{5,6},{6,5},{9,10},{10,9},{11,12},{12,11},... | collective-permute-start | bytes 442376 | tf_op jit(solution)/shard_map/ppermute | solution.py:298
  12.8 3.0 %collective-permute-start.3 = (f32[6,48,128]{2,1,0:T(8,128)S(1)}, f32[6,48,128]{2,1,0:T(8,128)S(1)}, u32[]{:S(2)}, u32[]{:S(2)}) collective-permute-start(f32[6,48,128]{2,1,0:T(8,128)S(1)} %get-tuple-element.29), channel_id=1, source_target_pairs={{0,1},{1,0},{2,3},{3,2},{4,5},{5,4},{6,7},{7,6},{8,9},{9,8},{10,11... | collective-permute-start | bytes 442376 | tf_op jit(solution)/shard_map/ppermute | solution.py:298
  16.7 9.4 %collective-permute-start.4 = (f32[6,48,128]{2,1,0:T(8,128)S(1)}, f32[6,48,128]{2,1,0:T(8,128)S(1)}, u32[]{:S(2)}, u32[]{:S(2)}) collective-permute-start(f32[6,48,128]{2,1,0:T(8,128)S(1)} %get-tuple-element.32), channel_id=1, source_target_pairs={{8,16},{16,8},{24,32},{32,24},{40,48},{48,40},{56,64},{64,56},{72,... | collective-permute-start | bytes 442376 | tf_op jit(solution)/shard_map/ppermute | solution.py:298
  17.4 8.8 %collective-permute-start.5 = (f32[6,48,128]{2,1,0:T(8,128)S(1)}, f32[6,48,128]{2,1,0:T(8,128)S(1)}, u32[]{:S(2)}, u32[]{:S(2)}) collective-permute-start(f32[6,48,128]{2,1,0:T(8,128)S(1)} %get-tuple-element.32), channel_id=1, source_target_pairs={{0,8},{8,0},{16,24},{24,16},{32,40},{40,32},{48,56},{56,48},{64,72... | collective-permute-start | bytes 442376 | tf_op jit(solution)/shard_map/ppermute | solution.py:298
  21.0 6.9 %collective-permute-start.6 = (f32[6,48,128]{2,1,0:T(8,128)S(1)}, f32[6,48,128]{2,1,0:T(8,128)S(1)}, u32[]{:S(2)}, u32[]{:S(2)}) collective-permute-start(f32[6,48,128]{2,1,0:T(8,128)S(1)} %get-tuple-element.32), channel_id=1, source_target_pairs={{1,2},{2,1},{3,4},{4,3},{5,6},{6,5},{9,10},{10,9},{11,12},{12,11},... | collective-permute-start | bytes 442376 | tf_op jit(solution)/shard_map/ppermute | solution.py:298
  25.0 2.8 %collective-permute-start.7 = (f32[6,48,128]{2,1,0:T(8,128)S(1)}, f32[6,48,128]{2,1,0:T(8,128)S(1)}, u32[]{:S(2)}, u32[]{:S(2)}) collective-permute-start(f32[6,48,128]{2,1,0:T(8,128)S(1)} %get-tuple-element.32), channel_id=1, source_target_pairs={{0,1},{1,0},{2,3},{3,2},{4,5},{5,4},{6,7},{7,6},{8,9},{9,8},{10,11... | collective-permute-start | bytes 442376 | tf_op jit(solution)/shard_map/ppermute | solution.py:298
  26.1 11.7 %copy-start.1 = (s32[1024,1]{0,1:T(1,128)S(1)}, s32[1024,1]{0,1:T(1,128)}, u32[]{:S(2)}) copy-start(s32[1024,1]{0,1:T(1,128)} %param.18) | copy-start | bytes 12292
  28.7 11.8 %copy-start = (bf16[16,6,6,768]{3,0,2,1:T(8,128)(2,1)S(1)}, bf16[16,6,6,768]{3,0,2,1:T(8,128)(2,1)}, u32[]{:S(2)}) copy-start(bf16[16,6,6,768]{3,0,2,1:T(8,128)(2,1)} %param.16) | copy-start | bytes 2654212
  28.7 11.8 %copy-start.2 = (s32[1024]{0:T(1024)S(1)}, s32[1024]{0:T(1024)}, u32[]{:S(2)}) copy-start(s32[1024]{0:T(1024)} %param.17) | copy-start | bytes 12292
  28.7 11.8 %copy-start.3 = (s32[1024]{0:T(1024)S(1)}, s32[1024]{0:T(1024)}, u32[]{:S(2)}) copy-start(s32[1024]{0:T(1024)} %param.19) | copy-start | bytes 12292
  28.8 10.7 %collective-permute-start.10 = (f32[6,48,128]{2,1,0:T(8,128)S(1)}, f32[6,48,128]{2,1,0:T(8,128)S(1)}, u32[]{:S(2)}, u32[]{:S(2)}) collective-permute-start(f32[6,48,128]{2,1,0:T(8,128)S(1)} %get-tuple-element.35), channel_id=1, source_target_pairs={{8,16},{16,8},{24,32},{32,24},{40,48},{48,40},{56,64},{64,56},{72,... | collective-permute-start | bytes 442376 | tf_op jit(solution)/shard_map/ppermute | solution.py:298
  29.6 9.9 %collective-permute-start.11 = (f32[6,48,128]{2,1,0:T(8,128)S(1)}, f32[6,48,128]{2,1,0:T(8,128)S(1)}, u32[]{:S(2)}, u32[]{:S(2)}) collective-permute-start(f32[6,48,128]{2,1,0:T(8,128)S(1)} %get-tuple-element.35), channel_id=1, source_target_pairs={{0,8},{8,0},{16,24},{24,16},{32,40},{40,32},{48,56},{56,48},{64,72... | collective-permute-start | bytes 442376 | tf_op jit(solution)/shard_map/ppermute | solution.py:298
  33.5 7.0 %collective-permute-start.8 = (f32[6,48,128]{2,1,0:T(8,128)S(1)}, f32[6,48,128]{2,1,0:T(8,128)S(1)}, u32[]{:S(2)}, u32[]{:S(2)}) collective-permute-start(f32[6,48,128]{2,1,0:T(8,128)S(1)} %get-tuple-element.35), channel_id=1, source_target_pairs={{1,2},{2,1},{3,4},{4,3},{5,6},{6,5},{9,10},{10,9},{11,12},{12,11},... | collective-permute-start | bytes 442376 | tf_op jit(solution)/shard_map/ppermute | solution.py:298
  37.7 2.8 %collective-permute-start.9 = (f32[6,48,128]{2,1,0:T(8,128)S(1)}, f32[6,48,128]{2,1,0:T(8,128)S(1)}, u32[]{:S(2)}, u32[]{:S(2)}) collective-permute-start(f32[6,48,128]{2,1,0:T(8,128)S(1)} %get-tuple-element.35), channel_id=1, source_target_pairs={{0,1},{1,0},{2,3},{3,2},{4,5},{5,4},{6,7},{7,6},{8,9},{9,8},{10,11... | collective-permute-start | bytes 442376 | tf_op jit(solution)/shard_map/ppermute | solution.py:298

commit v7 on v6

--- a/solution.py
+++ b/solution.py
@@ -349,7 +349,7 @@
         out_shape=(adj_shape, jax.ShapeDtypeStruct(coupling.shape, coupling.dtype)),
         in_specs=[smem, smem, VMEM, VMEM, VMEM, hbm],
         out_specs=(VMEM, VMEM),
-        scratch_shapes=[pltpu.SemaphoreType.DMA((4,))],
+        scratch_shapes=[pltpu.SemaphoreType.DMA((tiles,))],
         compiler_params=params,
         cost_estimate=pl.CostEstimate(flops=0, bytes_accessed=4 * coupling.size, transcendentals=0),
         name="first_rest",

time: 64.8 us -> 64.8 us (level)
  no operation moved by 1% of the time
where the time goes in v7:
time: 64.8 us; the launch traced here: 64.5 us
  starting transfers between devices  27.2 us (42%)
  blocking collectives  19.5 us (30%)
  Pallas kernels  13.6 us (21%)
  waiting for transfers between devices  2.71 us (4%)
  between operations  1.52 us (2%)
    ppermute x12, starting transfers between devices, exchange(): return [lax.ppermute(sent, *pairs[name]) for name in order]  27.2 us
    all_to_all x1, blocking collectives, per_device(): parcels = lax.all_to_all(parcels, 'region', 0, 0, tiled=True)  19.5 us
    pallas_call x1, Pallas kernels, per_device(): pl.pallas_call(functools.partial(last_kernel, LAST_ORDER), out_shape=(jax...  3.34 us
    pallas_call x1, Pallas kernels, per_device(): pl.pallas_call(first_rest_kernel, out_shape=(adj_shape, jax.ShapeDtypeStr...  2.91 us
    ppermute x12, waiting for transfers between devices, exchange(): return [lax.ppermute(sent, *pairs[name]) for name in order]  2.71 us
    pallas_call x2, Pallas kernels, per_device(): pl.pallas_call(rest_kernel, out_shape=adj_shape, in_specs=[smem] * 3 + [V...  1.92 us
    pallas_call x1, Pallas kernels, per_device(): pl.pallas_call(first_kernel, out_shape=(adj_shape, sent_shape, jax.ShapeD...  1.82 us
    pallas_call x2, Pallas kernels, per_device(): pl.pallas_call(functools.partial(lead_kernel, ORDER), out_shape=(adj_shap...  1.73 us
  transfers between devices with their start and end apart: 12, of which 2 were waited for; matrix products, arithmetic and copies ran while one was open for 0% of the time, Pallas kernels for 9%

profile of v7, /device:TPU:1, one launch (start us, length us, event | category | flops | bytes accessed | tf_op | source)
XLA Modules:
  0.0 64.5 jit_solution(14311568478165810985)
XLA Ops:
  1.3 1.8 %first.1 = (f32[6,128,128]{2,1,0:T(8,128)S(1)}, f32[6,48,128]{2,1,0:T(8,128)S(1)}, f32[16,8,768]{2,1,0:T(8,128)S(1)}, bf16[16,8,8,768]{3,2,1,0:T(8,128)(2,1)S(1)...) custom-call(s32[1,8]{1,0:T(1,128)} %send_hbm.1, s32[4,16]{1,0:T(4,128)} %bitcast.12, ...), custom_call_target="tpu_custom_call" | custom-call | tf_op jit(solution)/shard_map/first/pallas_call | solution.py:328
  3.1 0.7 %collective-permute-start = (f32[6,48,128]{2,1,0:T(8,128)S(1)}, f32[6,48,128]{2,1,0:T(8,128)S(1)}, u32[]{:S(2)}, u32[]{:S(2)}) collective-permute-start(f32[6,48,128]{2,1,0:T(8,128)S(1)} %get-tuple-element.29), channel_id=1, source_target_pairs={{8,16},{16,8},{24,32},{32,24},{40,48},{48,40},{56,64},{64,56},{72,... | collective-permute-start | bytes 442376 | tf_op jit(solution)/shard_map/ppermute | solution.py:298
  3.8 4.7 %collective-permute-start.1 = (f32[6,48,128]{2,1,0:T(8,128)S(1)}, f32[6,48,128]{2,1,0:T(8,128)S(1)}, u32[]{:S(2)}, u32[]{:S(2)}) collective-permute-start(f32[6,48,128]{2,1,0:T(8,128)S(1)} %get-tuple-element.29), channel_id=1, source_target_pairs={{0,8},{8,0},{16,24},{24,16},{32,40},{40,32},{48,56},{56,48},{64,72... | collective-permute-start | bytes 442376 | tf_op jit(solution)/shard_map/ppermute | solution.py:298
  8.5 4.2 %collective-permute-start.2 = (f32[6,48,128]{2,1,0:T(8,128)S(1)}, f32[6,48,128]{2,1,0:T(8,128)S(1)}, u32[]{:S(2)}, u32[]{:S(2)}) collective-permute-start(f32[6,48,128]{2,1,0:T(8,128)S(1)} %get-tuple-element.29), channel_id=1, source_target_pairs={{1,2},{2,1},{3,4},{4,3},{5,6},{6,5},{9,10},{10,9},{11,12},{12,11},... | collective-permute-start | bytes 442376 | tf_op jit(solution)/shard_map/ppermute | solution.py:298
  12.8 0.1 collective-permute-start.3
  12.9 2.9 %first_rest.1 = (f32[6,128,128]{2,1,0:T(8,128)S(1)}, bf16[16,4,8,8,768]{4,3,2,1,0:T(8,128)(2,1)S(1)}) custom-call(s32[1,16]{1,0:T(1,128)S(4)} %get-tuple-element.24.listed_ref, s32[1]{0:T(128)S(6)} %copy.13.count_ref, f32[16,8,768]{2,1,0:T(8,128)S(1)} %get-tuple-element.22.rhs_ref, bf16[16,8,8,768]{3,2,1,0:T(8,128)(2,1)S(1)} %get-tuple-element.23.inv_ref, ...), custom_call_target="tpu_custom_call" | custom-call | bytes 12582912 | tf_op jit(solution)/shard_map/first_rest/pallas_call | solution.py:347
  15.8 0.0 collective-permute-done.1.h1
  15.8 0.0 collective-permute-done.2.h2
  15.8 0.9 %lead.2 = (f32[6,128,128]{2,1,0:T(8,128)S(1)}, f32[6,48,128]{2,1,0:T(8,128)S(1)}, f32[6,320,128]{2,1,0:T(8,128)S(1)}) custom-call(s32[4,16]{1,0:T(4,128)S(4)} %get-tuple-element.21.near_ref, s32[1,8]{1,0:T(1,128)S(4)} %get-tuple-element.27.send_ref, s32[1]{0:T(128)S(6)} %copy.13.count_ref, f32[16,8,768]{2,1,0:T(8,128)S(1)} %get-tuple-element.22.rhs_ref, ...), custom_call_target="tpu_custom_call" | custom-call | tf_op jit(solution)/shard_map/lead/pallas_call | solution.py:368
  16.7 0.7 %collective-permute-start.4 = (f32[6,48,128]{2,1,0:T(8,128)S(1)}, f32[6,48,128]{2,1,0:T(8,128)S(1)}, u32[]{:S(2)}, u32[]{:S(2)}) collective-permute-start(f32[6,48,128]{2,1,0:T(8,128)S(1)} %get-tuple-element.32), channel_id=1, source_target_pairs={{8,16},{16,8},{24,32},{32,24},{40,48},{48,40},{56,64},{64,56},{72,... | collective-permute-start | bytes 442376 | tf_op jit(solution)/shard_map/ppermute | solution.py:298
  17.4 3.6 %collective-permute-start.5 = (f32[6,48,128]{2,1,0:T(8,128)S(1)}, f32[6,48,128]{2,1,0:T(8,128)S(1)}, u32[]{:S(2)}, u32[]{:S(2)}) collective-permute-start(f32[6,48,128]{2,1,0:T(8,128)S(1)} %get-tuple-element.32), channel_id=1, source_target_pairs={{0,8},{8,0},{16,24},{24,16},{32,40},{40,32},{48,56},{56,48},{64,72... | collective-permute-start | bytes 442376 | tf_op jit(solution)/shard_map/ppermute | solution.py:298
  21.0 4.0 %collective-permute-start.6 = (f32[6,48,128]{2,1,0:T(8,128)S(1)}, f32[6,48,128]{2,1,0:T(8,128)S(1)}, u32[]{:S(2)}, u32[]{:S(2)}) collective-permute-start(f32[6,48,128]{2,1,0:T(8,128)S(1)} %get-tuple-element.32), channel_id=1, source_target_pairs={{1,2},{2,1},{3,4},{4,3},{5,6},{6,5},{9,10},{10,9},{11,12},{12,11},... | collective-permute-start | bytes 442376 | tf_op jit(solution)/shard_map/ppermute | solution.py:298
  25.1 0.1 collective-permute-start.7
  25.2 1.0 %rest.2.old_ref = f32[6,128,128]{2,1,0:T(8,128)S(1)} custom-call(s32[4,16]{1,0:T(4,128)S(4)} %get-tuple-element.21.near_ref, s32[1,16]{1,0:T(1,128)S(4)} %get-tuple-element.24.listed_ref, s32[1]{0:T(128)S(6)} %copy.13.count_ref, f32[16,8,768]{2,1,0:T(8,128)S(1)} %get-tuple-element.22.rhs_ref, bf16[16,8,8,768]{3,2,1,0:T(8,128)(2,1)S(1)} %get-tuple-element.23.inv_ref, ...), custom_call_target="tpu_custom_call" | custom-call | bytes 4194304 | tf_op jit(solution)/shard_map/rest/pallas_call | solution.py:378
  26.1 0.0 copy-start.1
  26.1 0.0 collective-permute-done.4.h0
  26.2 1.7 %collective-permute-done.6.h2 = f32[6,48,128]{2,1,0:T(8,128)S(1)} collective-permute-done((f32[6,48,128]{2,1,0:T(8,128)S(1)}, f32[6,48,128]{2,1,0:T(8,128)S(1)}, u32[]{:S(2)}, u32[]{:S(2)}) %collective-permute-start.6) | collective-permute-done | bytes 147488 | tf_op jit(solution)/shard_map/ppermute | solution.py:298
  27.9 0.0 collective-permute-done.7.h3
  27.9 0.9 %lead.3 = (f32[6,128,128]{2,1,0:T(8,128)S(1)}, f32[6,48,128]{2,1,0:T(8,128)S(1)}, f32[6,320,128]{2,1,0:T(8,128)S(1)}) custom-call(s32[4,16]{1,0:T(4,128)S(4)} %get-tuple-element.21.near_ref, s32[1,8]{1,0:T(1,128)S(4)} %get-tuple-element.27.send_ref, s32[1]{0:T(128)S(6)} %copy.13.count_ref, f32[16,8,768]{2,1,0:T(8,128)S(1)} %get-tuple-element.22.rhs_ref, ...), custom_call_target="tpu_custom_call" | custom-call | tf_op jit(solution)/shard_map/lead/pallas_call | solution.py:368
  28.8 0.0 copy-start
  28.8 0.0 copy-start.2
  28.8 0.0 copy-start.3
  28.8 0.8 %collective-permute-start.10 = (f32[6,48,128]{2,1,0:T(8,128)S(1)}, f32[6,48,128]{2,1,0:T(8,128)S(1)}, u32[]{:S(2)}, u32[]{:S(2)}) collective-permute-start(f32[6,48,128]{2,1,0:T(8,128)S(1)} %get-tuple-element.35), channel_id=1, source_target_pairs={{8,16},{16,8},{24,32},{32,24},{40,48},{48,40},{56,64},{64,56},{72,... | collective-permute-start | bytes 442376 | tf_op jit(solution)/shard_map/ppermute | solution.py:298
  29.6 3.9 %collective-permute-start.11 = (f32[6,48,128]{2,1,0:T(8,128)S(1)}, f32[6,48,128]{2,1,0:T(8,128)S(1)}, u32[]{:S(2)}, u32[]{:S(2)}) collective-permute-start(f32[6,48,128]{2,1,0:T(8,128)S(1)} %get-tuple-element.35), channel_id=1, source_target_pairs={{0,8},{8,0},{16,24},{24,16},{32,40},{40,32},{48,56},{56,48},{64,72... | collective-permute-start | bytes 442376 | tf_op jit(solution)/shard_map/ppermute | solution.py:298
  33.5 4.2 %collective-permute-start.8 = (f32[6,48,128]{2,1,0:T(8,128)S(1)}, f32[6,48,128]{2,1,0:T(8,128)S(1)}, u32[]{:S(2)}, u32[]{:S(2)}) collective-permute-start(f32[6,48,128]{2,1,0:T(8,128)S(1)} %get-tuple-element.35), channel_id=1, source_target_pairs={{1,2},{2,1},{3,4},{4,3},{5,6},{6,5},{9,10},{10,9},{11,12},{12,11},... | collective-permute-start | bytes 442376 | tf_op jit(solution)/shard_map/ppermute | solution.py:298
  37.7 0.1 collective-permute-start.9
  37.8 0.7 %rank.1.rank_hot_ref = bf16[128,1024]{1,0:T(8,128)(2,1)S(1)} custom-call(s32[1,1024]{1,0:T(1,128)S(1)} %bitcast.8), custom_call_target="tpu_custom_call" | custom-call | tf_op jit(solution)/shard_map/rank/pallas_call | solution.py:357
  38.6 1.0 %rest.3.old_ref = f32[6,128,128]{2,1,0:T(8,128)S(1)} custom-call(s32[4,16]{1,0:T(4,128)S(4)} %get-tuple-element.21.near_ref, s32[1,16]{1,0:T(1,128)S(4)} %get-tuple-element.24.listed_ref, s32[1]{0:T(128)S(6)} %copy.13.count_ref, f32[16,8,768]{2,1,0:T(8,128)S(1)} %get-tuple-element.22.rhs_ref, bf16[16,8,8,768]{3,2,1,0:T(8,128)(2,1)S(1)} %get-tuple-element.23.inv_ref, ...), custom_call_target="tpu_custom_call" | custom-call | bytes 4194304 | tf_op jit(solution)/shard_map/rest/pallas_call | solution.py:378
  39.6 1.0 %collective-permute-done.8.h0 = f32[6,48,128]{2,1,0:T(8,128)S(1)} collective-permute-done((f32[6,48,128]{2,1,0:T(8,128)S(1)}, f32[6,48,128]{2,1,0:T(8,128)S(1)}, u32[]{:S(2)}, u32[]{:S(2)}) %collective-permute-start.8) | collective-permute-done | bytes 147488 | tf_op jit(solution)/shard_map/ppermute | solution.py:298
  40.5 3.3 %last.1 = (f32[128,768]{1,0:T(8,128)}, f32[6,16,768]{2,1,0:T(8,128)}, f32[32,8,128]{2,1,0:T(8,128)S(1)}) custom-call(s32[4,16]{1,0:T(4,128)S(4)} %get-tuple-element.21.near_ref, s32[1]{0:T(128)S(6)} %copy.13.count_ref, f32[16,8,768]{2,1,0:T(8,128)S(1)} %get-tuple-element.22.rhs_ref, bf16[16,8,8,768]{3,2,1,0:T(8,128)(2,1)S(1)} %get-tuple-element.23.inv_ref, ...), custom_call_target="tpu_custom_call" | custom-call | tf_op jit(solution)/shard_map/last/pallas_call | solution.py:388
  43.9 19.5 %all_to_all.5.parcel_ref = f32[32,8,128]{2,1,0:T(8,128)S(1)} all-to-all(f32[32,8,128]{2,1,0:T(8,128)S(1)} %get-tuple-element.38), channel_id=1, replica_groups=mesh['region'=32,'sub'=8] {'region'}, dimensions={0} | all-to-all | bytes 262144 | tf_op jit(solution)/shard_map/all_to_all | solution.py:414
  63.3 1.2 %owner.1 = f32[6,1024]{1,0:T(8,128)} custom-call(f32[32,8,128]{2,1,0:T(8,128)S(1)} %all_to_all.5.parcel_ref), custom_call_target="tpu_custom_call" | custom-call | tf_op jit(solution)/shard_map/owner/pallas_call | solution.py:415
  (10 shorter events, 0.0 us)
Async XLA Ops:
  3.1 12.7 %collective-permute-start = (f32[6,48,128]{2,1,0:T(8,128)S(1)}, f32[6,48,128]{2,1,0:T(8,128)S(1)}, u32[]{:S(2)}, u32[]{:S(2)}) collective-permute-start(f32[6,48,128]{2,1,0:T(8,128)S(1)} %get-tuple-element.29), channel_id=1, source_target_pairs={{8,16},{16,8},{24,32},{32,24},{40,48},{48,40},{56,64},{64,56},{72,... | collective-permute-start | bytes 442376 | tf_op jit(solution)/shard_map/ppermute | solution.py:298
  3.8 12.0 %collective-permute-start.1 = (f32[6,48,128]{2,1,0:T(8,128)S(1)}, f32[6,48,128]{2,1,0:T(8,128)S(1)}, u32[]{:S(2)}, u32[]{:S(2)}) collective-permute-start(f32[6,48,128]{2,1,0:T(8,128)S(1)} %get-tuple-element.29), channel_id=1, source_target_pairs={{0,8},{8,0},{16,24},{24,16},{32,40},{40,32},{48,56},{56,48},{64,72... | collective-permute-start | bytes 442376 | tf_op jit(solution)/shard_map/ppermute | solution.py:298
  8.5 7.3 %collective-permute-start.2 = (f32[6,48,128]{2,1,0:T(8,128)S(1)}, f32[6,48,128]{2,1,0:T(8,128)S(1)}, u32[]{:S(2)}, u32[]{:S(2)}) collective-permute-start(f32[6,48,128]{2,1,0:T(8,128)S(1)} %get-tuple-element.29), channel_id=1, source_target_pairs={{1,2},{2,1},{3,4},{4,3},{5,6},{6,5},{9,10},{10,9},{11,12},{12,11},... | collective-permute-start | bytes 442376 | tf_op jit(solution)/shard_map/ppermute | solution.py:298
  12.8 3.1 %collective-permute-start.3 = (f32[6,48,128]{2,1,0:T(8,128)S(1)}, f32[6,48,128]{2,1,0:T(8,128)S(1)}, u32[]{:S(2)}, u32[]{:S(2)}) collective-permute-start(f32[6,48,128]{2,1,0:T(8,128)S(1)} %get-tuple-element.29), channel_id=1, source_target_pairs={{0,1},{1,0},{2,3},{3,2},{4,5},{5,4},{6,7},{7,6},{8,9},{9,8},{10,11... | collective-permute-start | bytes 442376 | tf_op jit(solution)/shard_map/ppermute | solution.py:298
  16.7 9.4 %collective-permute-start.4 = (f32[6,48,128]{2,1,0:T(8,128)S(1)}, f32[6,48,128]{2,1,0:T(8,128)S(1)}, u32[]{:S(2)}, u32[]{:S(2)}) collective-permute-start(f32[6,48,128]{2,1,0:T(8,128)S(1)} %get-tuple-element.32), channel_id=1, source_target_pairs={{8,16},{16,8},{24,32},{32,24},{40,48},{48,40},{56,64},{64,56},{72,... | collective-permute-start | bytes 442376 | tf_op jit(solution)/shard_map/ppermute | solution.py:298
  17.4 8.8 %collective-permute-start.5 = (f32[6,48,128]{2,1,0:T(8,128)S(1)}, f32[6,48,128]{2,1,0:T(8,128)S(1)}, u32[]{:S(2)}, u32[]{:S(2)}) collective-permute-start(f32[6,48,128]{2,1,0:T(8,128)S(1)} %get-tuple-element.32), channel_id=1, source_target_pairs={{0,8},{8,0},{16,24},{24,16},{32,40},{40,32},{48,56},{56,48},{64,72... | collective-permute-start | bytes 442376 | tf_op jit(solution)/shard_map/ppermute | solution.py:298
  21.0 6.9 %collective-permute-start.6 = (f32[6,48,128]{2,1,0:T(8,128)S(1)}, f32[6,48,128]{2,1,0:T(8,128)S(1)}, u32[]{:S(2)}, u32[]{:S(2)}) collective-permute-start(f32[6,48,128]{2,1,0:T(8,128)S(1)} %get-tuple-element.32), channel_id=1, source_target_pairs={{1,2},{2,1},{3,4},{4,3},{5,6},{6,5},{9,10},{10,9},{11,12},{12,11},... | collective-permute-start | bytes 442376 | tf_op jit(solution)/shard_map/ppermute | solution.py:298
  25.1 2.8 %collective-permute-start.7 = (f32[6,48,128]{2,1,0:T(8,128)S(1)}, f32[6,48,128]{2,1,0:T(8,128)S(1)}, u32[]{:S(2)}, u32[]{:S(2)}) collective-permute-start(f32[6,48,128]{2,1,0:T(8,128)S(1)} %get-tuple-element.32), channel_id=1, source_target_pairs={{0,1},{1,0},{2,3},{3,2},{4,5},{5,4},{6,7},{7,6},{8,9},{9,8},{10,11... | collective-permute-start | bytes 442376 | tf_op jit(solution)/shard_map/ppermute | solution.py:298
  26.1 11.7 %copy-start.1 = (s32[1024,1]{0,1:T(1,128)S(1)}, s32[1024,1]{0,1:T(1,128)}, u32[]{:S(2)}) copy-start(s32[1024,1]{0,1:T(1,128)} %param.18) | copy-start | bytes 12292
  28.8 11.8 %copy-start = (bf16[16,6,6,768]{3,0,2,1:T(8,128)(2,1)S(1)}, bf16[16,6,6,768]{3,0,2,1:T(8,128)(2,1)}, u32[]{:S(2)}) copy-start(bf16[16,6,6,768]{3,0,2,1:T(8,128)(2,1)} %param.16) | copy-start | bytes 2654212
  28.8 11.8 %copy-start.2 = (s32[1024]{0:T(1024)S(1)}, s32[1024]{0:T(1024)}, u32[]{:S(2)}) copy-start(s32[1024]{0:T(1024)} %param.17) | copy-start | bytes 12292
  28.8 11.8 %copy-start.3 = (s32[1024]{0:T(1024)S(1)}, s32[1024]{0:T(1024)}, u32[]{:S(2)}) copy-start(s32[1024]{0:T(1024)} %param.19) | copy-start | bytes 12292
  28.8 10.7 %collective-permute-start.10 = (f32[6,48,128]{2,1,0:T(8,128)S(1)}, f32[6,48,128]{2,1,0:T(8,128)S(1)}, u32[]{:S(2)}, u32[]{:S(2)}) collective-permute-start(f32[6,48,128]{2,1,0:T(8,128)S(1)} %get-tuple-element.35), channel_id=1, source_target_pairs={{8,16},{16,8},{24,32},{32,24},{40,48},{48,40},{56,64},{64,56},{72,... | collective-permute-start | bytes 442376 | tf_op jit(solution)/shard_map/ppermute | solution.py:298
  29.6 9.9 %collective-permute-start.11 = (f32[6,48,128]{2,1,0:T(8,128)S(1)}, f32[6,48,128]{2,1,0:T(8,128)S(1)}, u32[]{:S(2)}, u32[]{:S(2)}) collective-permute-start(f32[6,48,128]{2,1,0:T(8,128)S(1)} %get-tuple-element.35), channel_id=1, source_target_pairs={{0,8},{8,0},{16,24},{24,16},{32,40},{40,32},{48,56},{56,48},{64,72... | collective-permute-start | bytes 442376 | tf_op jit(solution)/shard_map/ppermute | solution.py:298
  33.5 7.0 %collective-permute-start.8 = (f32[6,48,128]{2,1,0:T(8,128)S(1)}, f32[6,48,128]{2,1,0:T(8,128)S(1)}, u32[]{:S(2)}, u32[]{:S(2)}) collective-permute-start(f32[6,48,128]{2,1,0:T(8,128)S(1)} %get-tuple-element.35), channel_id=1, source_target_pairs={{1,2},{2,1},{3,4},{4,3},{5,6},{6,5},{9,10},{10,9},{11,12},{12,11},... | collective-permute-start | bytes 442376 | tf_op jit(solution)/shard_map/ppermute | solution.py:298
  37.7 2.8 %collective-permute-start.9 = (f32[6,48,128]{2,1,0:T(8,128)S(1)}, f32[6,48,128]{2,1,0:T(8,128)S(1)}, u32[]{:S(2)}, u32[]{:S(2)}) collective-permute-start(f32[6,48,128]{2,1,0:T(8,128)S(1)} %get-tuple-element.35), channel_id=1, source_target_pairs={{0,1},{1,0},{2,3},{3,2},{4,5},{5,4},{6,7},{7,6},{8,9},{9,8},{10,11... | collective-permute-start | bytes 442376 | tf_op jit(solution)/shard_map/ppermute | solution.py:298

commit v8 on v7

--- a/solution.py
+++ b/solution.py
@@ -14,7 +14,7 @@
 LANES = 128
 
 ORDER = ("rb", "ra", "sb", "sa")
-LAST_ORDER = ("sb", "sa", "rb", "ra")
+LAST_ORDER = ("sb", "ra", "sa", "rb")
 
 F32 = jnp.float32
 BF16 = jnp.bfloat16
@@ -107,15 +107,18 @@
         copy.wait()
 
 
+def halo_place(name):
+    odd_region = lax.axis_index("region") % 2
+    odd_sub = lax.axis_index("sub") % 2
+    return {"ra": 1 - odd_region, "rb": odd_region, "sa": 3 - odd_sub, "sb": 2 + odd_sub}[name]
+
+
 def build_extended(order, old_ref, halo_refs, ext_ref):
     own = old_ref.shape[1]
     ext_ref[:, :own, :] = old_ref[...]
-    odd_region = lax.axis_index("region") % 2
-    odd_sub = lax.axis_index("sub") % 2
-    places = {"ra": 1 - odd_region, "rb": odd_region, "sa": 3 - odd_sub, "sb": 2 + odd_sub}
-    width = halo_refs[0].shape[1]
     for name, halo in zip(order, halo_refs):
-        ext_ref[:, pl.ds(pl.multiple_of(own + places[name] * width, 8), width), :] = halo[...]
+        width = halo.shape[1]
+        ext_ref[:, pl.ds(pl.multiple_of(own + halo_place(name) * width, 8), width), :] = halo[...]
 
 
 def sweep_tile(t, near_ref, count_ref, rhs_ref, inv_ref, cpl_ref, ext_ref, resid_ref):
@@ -163,22 +166,52 @@
             put_rows(adj_ref, t, sweep_tile(t, near_ref, count_ref, rhs_ref, inv_ref, cpl_ref, ext_ref, resid_ref))
 
 
+def early_kernel(
+    order, near_ref, count_ref, rhs_ref, inv_ref, cpl_ref, old_ref, h0, h1, h2, adj_ref, ext_ref, late_ref, resid_ref
+):
+    build_extended(order, old_ref, (h0, h1, h2), ext_ref)
+    tiles, group = rhs_ref.shape[0], h0.shape[1] // NVAR
+    first = tiles + halo_place("sb") * group
+
+    @pl.loop(0, tiles)
+    def _(t):
+        late = jnp.int32(0)
+        for k in range(cpl_ref.shape[1]):
+            tile = near_ref[k, t]
+            late = late + jnp.where((tile >= first) & (tile < first + group), 1, 0)
+        late_ref[0, t] = late
+
+        @pl.when(late == 0)
+        def _():
+            put_rows(adj_ref, t, sweep_tile(t, near_ref, count_ref, rhs_ref, inv_ref, cpl_ref, ext_ref, resid_ref))
+
+
 def last_kernel(
-    order, near_ref, count_ref, rhs_ref, inv_ref, cpl_ref, hess_ref, old_ref, h0, h1, h2, h3,
+    near_ref, count_ref, late_ref, rhs_ref, inv_ref, cpl_ref, hess_ref, early_ref, old_ext_ref, halo_ref,
     vertex_ref, region_ref, slot_ref, rank_hot_ref,
     adj_hbm, metric_hbm, parcel_ref,
     ext_ref, resid_ref, adj_ref, metric_ref, column_ref, gathered_ref, out_sems,
 ):
-    build_extended(order, old_ref, (h0, h1, h2, h3), ext_ref)
+    ext_ref[...] = old_ext_ref[...]
+    own, group = rhs_ref.shape[0] * 8, halo_ref.shape[1]
+    ext_ref[:, pl.ds(pl.multiple_of(own + halo_place("sb") * group, 8), group), :] = halo_ref[...]
     tiles, width = rhs_ref.shape[0], rhs_ref.shape[2]
     chunks = width // LANES
 
-    @pl.loop(0, tiles)
-    def _(t):
-        blocks = sweep_tile(t, near_ref, count_ref, rhs_ref, inv_ref, cpl_ref, ext_ref, resid_ref)
+    def put(t, blocks):
         for q, block in enumerate(blocks):
             adj_ref[rows_of(t), lanes_of(q)] = block
             column_ref[q, rows_of(t), :] = jnp.abs(block)
+
+    @pl.loop(0, tiles)
+    def _(t):
+        @pl.when(late_ref[0, t] == 0)
+        def _():
+            put(t, [early_ref[q, rows_of(t), :] for q in range(chunks)])
+
+        @pl.when(late_ref[0, t] != 0)
+        def _():
+            put(t, sweep_tile(t, near_ref, count_ref, rhs_ref, inv_ref, cpl_ref, ext_ref, resid_ref))
 
     adj_out = pltpu.make_async_copy(adj_ref, adj_hbm, out_sems.at[0])
     adj_out.start()
@@ -385,14 +418,26 @@
             cost_estimate=beside,
             name="rest",
         )(neighbours, listed, tile_count, rhs, diag_inv, coupling, extended, lead)
+    by_name = dict(zip(LAST_ORDER, halos))
+    here = tuple(name for name in LAST_ORDER if name != "sb")
+    early, extended, late = pl.pallas_call(
+        functools.partial(early_kernel, here),
+        out_shape=(adj_shape, ext_shape, pltpu.SMEM((1, tiles), jnp.int32)),
+        in_specs=[smem] * 2 + [VMEM] * 7,
+        out_specs=(VMEM, VMEM, smem),
+        scratch_shapes=[resid],
+        compiler_params=params,
+        cost_estimate=beside,
+        name="early",
+    )(neighbours, tile_count, rhs, diag_inv, coupling, adjoint, *(by_name[name] for name in here))
     out, metric, parcels = pl.pallas_call(
-        functools.partial(last_kernel, LAST_ORDER),
+        last_kernel,
         out_shape=(
             jax.ShapeDtypeStruct((tiles * 8, width), F32),
             jax.ShapeDtypeStruct((6, tiles, width), F32),
             jax.ShapeDtypeStruct((regions, 8, CAP), F32),
         ),
-        in_specs=[smem, smem] + [VMEM] * 13,
+        in_specs=[smem] * 3 + [VMEM] * 11,
         out_specs=(hbm, hbm, VMEM),
         scratch_shapes=[
             pltpu.VMEM(ext_shape.shape, F32),
@@ -406,7 +451,8 @@
         compiler_params=params,
         name="last",
     )(
-        neighbours, tile_count, rhs, diag_inv, coupling, hessian.transpose(1, 2, 0, 3), adjoint, *halos,
+        neighbours, tile_count, scalars(late), rhs, diag_inv, coupling, hessian.transpose(1, 2, 0, 3), early, extended,
+        by_name["sb"],
         vertex, dest, slot, rank_hot,
     )
     out = out.reshape(tiles, block, width)

time: 64.8 us -> 64.8 us (level)
  Pallas kernels: 13.6 us -> 14.4 us
  waiting for transfers between devices: 2.71 us -> 1.92 us
    ppermute x12, waiting for transfers between devices: 2.71 us -> 1.92 us  [exchange(): return [lax.ppermute(sent, *pairs[name]) for name in order]]
    pallas_call x1 -> x2, Pallas kernels: 3.34 us -> 4.09 us  [the longest x1 3.25 us: per_device(): pl.pallas_call(last_kernel, out_shape=(jax.ShapeDtypeStruct((tiles * 8, w...]
  transfers between devices with their start and end apart: 12 -> 12, of which waited for: 2 -> 2; matrix products, arithmetic and copies ran while one was open for 0% -> 0% of each run, Pallas kernels for 9% -> 10%
where the time goes in v8:
time: 64.8 us; the launch traced here: 64.2 us
  starting transfers between devices  27 us (42%)
  blocking collectives  19.3 us (30%)
  Pallas kernels  14.4 us (22%)
  waiting for transfers between devices  1.92 us (3%)
  between operations  1.52 us (2%)
    ppermute x12, starting transfers between devices, exchange(): return [lax.ppermute(sent, *pairs[name]) for name in order]  27 us
    all_to_all x1, blocking collectives, per_device(): parcels = lax.all_to_all(parcels, 'region', 0, 0, tiled=True)  19.3 us
    pallas_call x1, Pallas kernels, per_device(): pl.pallas_call(last_kernel, out_shape=(jax.ShapeDtypeStruct((tiles * 8, w...  3.25 us
    pallas_call x1, Pallas kernels, per_device(): pl.pallas_call(first_rest_kernel, out_shape=(adj_shape, jax.ShapeDtypeStr...  2.91 us
    ppermute x12, waiting for transfers between devices, exchange(): return [lax.ppermute(sent, *pairs[name]) for name in order]  1.92 us
    pallas_call x2, Pallas kernels, per_device(): pl.pallas_call(rest_kernel, out_shape=adj_shape, in_specs=[smem] * 3 + [V...  1.91 us
    pallas_call x1, Pallas kernels, per_device(): pl.pallas_call(first_kernel, out_shape=(adj_shape, sent_shape, jax.ShapeD...  1.82 us
    pallas_call x2, Pallas kernels, per_device(): pl.pallas_call(functools.partial(lead_kernel, ORDER), out_shape=(adj_shap...  1.75 us
  transfers between devices with their start and end apart: 12, of which 2 were waited for; matrix products, arithmetic and copies ran while one was open for 0% of the time, Pallas kernels for 10%

profile of v8, /device:TPU:1, one launch (start us, length us, event | category | flops | bytes accessed | tf_op | source)
XLA Modules:
  0.0 64.2 jit_solution(17580205043730416723)
XLA Ops:
  1.3 1.8 %first.1 = (f32[6,128,128]{2,1,0:T(8,128)S(1)}, f32[6,48,128]{2,1,0:T(8,128)S(1)}, f32[16,8,768]{2,1,0:T(8,128)S(1)}, bf16[16,8,8,768]{3,2,1,0:T(8,128)(2,1)S(1)...) custom-call(s32[1,8]{1,0:T(1,128)} %send_hbm.1, s32[4,16]{1,0:T(4,128)} %bitcast.12, ...), custom_call_target="tpu_custom_call" | custom-call | tf_op jit(solution)/shard_map/first/pallas_call | solution.py:361
  3.1 0.7 %collective-permute-start = (f32[6,48,128]{2,1,0:T(8,128)S(1)}, f32[6,48,128]{2,1,0:T(8,128)S(1)}, u32[]{:S(2)}, u32[]{:S(2)}) collective-permute-start(f32[6,48,128]{2,1,0:T(8,128)S(1)} %get-tuple-element.32), channel_id=1, source_target_pairs={{8,16},{16,8},{24,32},{32,24},{40,48},{48,40},{56,64},{64,56},{72,... | collective-permute-start | bytes 442376 | tf_op jit(solution)/shard_map/ppermute | solution.py:331
  3.8 4.7 %collective-permute-start.1 = (f32[6,48,128]{2,1,0:T(8,128)S(1)}, f32[6,48,128]{2,1,0:T(8,128)S(1)}, u32[]{:S(2)}, u32[]{:S(2)}) collective-permute-start(f32[6,48,128]{2,1,0:T(8,128)S(1)} %get-tuple-element.32), channel_id=1, source_target_pairs={{0,8},{8,0},{16,24},{24,16},{32,40},{40,32},{48,56},{56,48},{64,72... | collective-permute-start | bytes 442376 | tf_op jit(solution)/shard_map/ppermute | solution.py:331
  8.5 4.2 %collective-permute-start.2 = (f32[6,48,128]{2,1,0:T(8,128)S(1)}, f32[6,48,128]{2,1,0:T(8,128)S(1)}, u32[]{:S(2)}, u32[]{:S(2)}) collective-permute-start(f32[6,48,128]{2,1,0:T(8,128)S(1)} %get-tuple-element.32), channel_id=1, source_target_pairs={{1,2},{2,1},{3,4},{4,3},{5,6},{6,5},{9,10},{10,9},{11,12},{12,11},... | collective-permute-start | bytes 442376 | tf_op jit(solution)/shard_map/ppermute | solution.py:331
  12.8 0.1 collective-permute-start.3
  12.9 2.9 %first_rest.1 = (f32[6,128,128]{2,1,0:T(8,128)S(1)}, bf16[16,4,8,8,768]{4,3,2,1,0:T(8,128)(2,1)S(1)}) custom-call(s32[1,16]{1,0:T(1,128)S(4)} %get-tuple-element.27.listed_ref, s32[1]{0:T(128)S(6)} %copy.13.count_ref, f32[16,8,768]{2,1,0:T(8,128)S(1)} %get-tuple-element.25.rhs_ref, bf16[16,8,8,768]{3,2,1,0:T(8,128)(2,1)S(1)} %get-tuple-element.26.inv_ref, ...), custom_call_target="tpu_custom_call" | custom-call | bytes 12582912 | tf_op jit(solution)/shard_map/first_rest/pallas_call | solution.py:380
  15.8 0.0 collective-permute-done.h0
  15.8 0.0 collective-permute-done.1.h1
  15.8 0.9 %lead.2 = (f32[6,128,128]{2,1,0:T(8,128)S(1)}, f32[6,48,128]{2,1,0:T(8,128)S(1)}, f32[6,320,128]{2,1,0:T(8,128)S(1)}) custom-call(s32[4,16]{1,0:T(4,128)S(4)} %get-tuple-element.24.near_ref, s32[1,8]{1,0:T(1,128)S(4)} %get-tuple-element.30.send_ref, s32[1]{0:T(128)S(6)} %copy.13.count_ref, f32[16,8,768]{2,1,0:T(8,128)S(1)} %get-tuple-element.25.rhs_ref, ...), custom_call_target="tpu_custom_call" | custom-call | tf_op jit(solution)/shard_map/lead/pallas_call | solution.py:401
  16.7 0.7 %collective-permute-start.4 = (f32[6,48,128]{2,1,0:T(8,128)S(1)}, f32[6,48,128]{2,1,0:T(8,128)S(1)}, u32[]{:S(2)}, u32[]{:S(2)}) collective-permute-start(f32[6,48,128]{2,1,0:T(8,128)S(1)} %get-tuple-element.35), channel_id=1, source_target_pairs={{8,16},{16,8},{24,32},{32,24},{40,48},{48,40},{56,64},{64,56},{72,... | collective-permute-start | bytes 442376 | tf_op jit(solution)/shard_map/ppermute | solution.py:331
  17.4 3.6 %collective-permute-start.5 = (f32[6,48,128]{2,1,0:T(8,128)S(1)}, f32[6,48,128]{2,1,0:T(8,128)S(1)}, u32[]{:S(2)}, u32[]{:S(2)}) collective-permute-start(f32[6,48,128]{2,1,0:T(8,128)S(1)} %get-tuple-element.35), channel_id=1, source_target_pairs={{0,8},{8,0},{16,24},{24,16},{32,40},{40,32},{48,56},{56,48},{64,72... | collective-permute-start | bytes 442376 | tf_op jit(solution)/shard_map/ppermute | solution.py:331
  21.0 4.1 %collective-permute-start.6 = (f32[6,48,128]{2,1,0:T(8,128)S(1)}, f32[6,48,128]{2,1,0:T(8,128)S(1)}, u32[]{:S(2)}, u32[]{:S(2)}) collective-permute-start(f32[6,48,128]{2,1,0:T(8,128)S(1)} %get-tuple-element.35), channel_id=1, source_target_pairs={{1,2},{2,1},{3,4},{4,3},{5,6},{6,5},{9,10},{10,9},{11,12},{12,11},... | collective-permute-start | bytes 442376 | tf_op jit(solution)/shard_map/ppermute | solution.py:331
  25.1 0.1 collective-permute-start.7
  25.2 1.0 %rest.2.old_ref = f32[6,128,128]{2,1,0:T(8,128)S(1)} custom-call(s32[4,16]{1,0:T(4,128)S(4)} %get-tuple-element.24.near_ref, s32[1,16]{1,0:T(1,128)S(4)} %get-tuple-element.27.listed_ref, s32[1]{0:T(128)S(6)} %copy.13.count_ref, f32[16,8,768]{2,1,0:T(8,128)S(1)} %get-tuple-element.25.rhs_ref, bf16[16,8,8,768]{3,2,1,0:T(8,128)(2,1)S(1)} %get-tuple-element.26.inv_ref, ...), custom_call_target="tpu_custom_call" | custom-call | bytes 4194304 | tf_op jit(solution)/shard_map/rest/pallas_call | solution.py:411
  26.1 0.0 copy-start.1
  26.1 0.0 collective-permute-done.4.h0
  26.2 1.7 %collective-permute-done.6.h2 = f32[6,48,128]{2,1,0:T(8,128)S(1)} collective-permute-done((f32[6,48,128]{2,1,0:T(8,128)S(1)}, f32[6,48,128]{2,1,0:T(8,128)S(1)}, u32[]{:S(2)}, u32[]{:S(2)}) %collective-permute-start.6) | collective-permute-done | bytes 147488 | tf_op jit(solution)/shard_map/ppermute | solution.py:331
  27.9 0.9 %lead.3 = (f32[6,128,128]{2,1,0:T(8,128)S(1)}, f32[6,48,128]{2,1,0:T(8,128)S(1)}, f32[6,320,128]{2,1,0:T(8,128)S(1)}) custom-call(s32[4,16]{1,0:T(4,128)S(4)} %get-tuple-element.24.near_ref, s32[1,8]{1,0:T(1,128)S(4)} %get-tuple-element.30.send_ref, s32[1]{0:T(128)S(6)} %copy.13.count_ref, f32[16,8,768]{2,1,0:T(8,128)S(1)} %get-tuple-element.25.rhs_ref, ...), custom_call_target="tpu_custom_call" | custom-call | tf_op jit(solution)/shard_map/lead/pallas_call | solution.py:401
  28.8 0.7 %collective-permute-start.10 = (f32[6,48,128]{2,1,0:T(8,128)S(1)}, f32[6,48,128]{2,1,0:T(8,128)S(1)}, u32[]{:S(2)}, u32[]{:S(2)}) collective-permute-start(f32[6,48,128]{2,1,0:T(8,128)S(1)} %get-tuple-element.38), channel_id=1, source_target_pairs={{8,16},{16,8},{24,32},{32,24},{40,48},{48,40},{56,64},{64,56},{72,... | collective-permute-start | bytes 442376 | tf_op jit(solution)/shard_map/ppermute | solution.py:331
  29.4 3.9 %collective-permute-start.8 = (f32[6,48,128]{2,1,0:T(8,128)S(1)}, f32[6,48,128]{2,1,0:T(8,128)S(1)}, u32[]{:S(2)}, u32[]{:S(2)}) collective-permute-start(f32[6,48,128]{2,1,0:T(8,128)S(1)} %get-tuple-element.38), channel_id=1, source_target_pairs={{0,8},{8,0},{16,24},{24,16},{32,40},{40,32},{48,56},{56,48},{64,72... | collective-permute-start | bytes 442376 | tf_op jit(solution)/shard_map/ppermute | solution.py:331
  33.4 4.2 %collective-permute-start.11 = (f32[6,48,128]{2,1,0:T(8,128)S(1)}, f32[6,48,128]{2,1,0:T(8,128)S(1)}, u32[]{:S(2)}, u32[]{:S(2)}) collective-permute-start(f32[6,48,128]{2,1,0:T(8,128)S(1)} %get-tuple-element.38), channel_id=1, source_target_pairs={{1,2},{2,1},{3,4},{4,3},{5,6},{6,5},{9,10},{10,9},{11,12},{12,11},... | collective-permute-start | bytes 442376 | tf_op jit(solution)/shard_map/ppermute | solution.py:331
  37.6 0.7 %rank.1.rank_hot_ref = bf16[128,1024]{1,0:T(8,128)(2,1)S(1)} custom-call(s32[1,1024]{1,0:T(1,128)S(1)} %bitcast.8), custom_call_target="tpu_custom_call" | custom-call | tf_op jit(solution)/shard_map/rank/pallas_call | solution.py:390
  38.3 1.0 %rest.3.old_ref = f32[6,128,128]{2,1,0:T(8,128)S(1)} custom-call(s32[4,16]{1,0:T(4,128)S(4)} %get-tuple-element.24.near_ref, s32[1,16]{1,0:T(1,128)S(4)} %get-tuple-element.27.listed_ref, s32[1]{0:T(128)S(6)} %copy.13.count_ref, f32[16,8,768]{2,1,0:T(8,128)S(1)} %get-tuple-element.25.rhs_ref, bf16[16,8,8,768]{3,2,1,0:T(8,128)(2,1)S(1)} %get-tuple-element.26.inv_ref, ...), custom_call_target="tpu_custom_call" | custom-call | bytes 4194304 | tf_op jit(solution)/shard_map/rest/pallas_call | solution.py:411
  39.3 0.0 copy-start
  39.3 0.0 copy-start.2
  39.3 0.0 copy-start.3
  39.3 0.8 %early.1 = (f32[6,128,128]{2,1,0:T(8,128)S(1)}, f32[6,320,128]{2,1,0:T(8,128)S(1)}, s32[1,16]{1,0:T(1,128)S(4)}) custom-call(s32[4,16]{1,0:T(4,128)S(4)} %get-tuple-element.24.near_ref, s32[1]{0:T(128)S(6)} %copy.13.count_ref, f32[16,8,768]{2,1,0:T(8,128)S(1)} %get-tuple-element.25.rhs_ref, bf16[16,8,8,768]{3,2,1,0:T(8,128)(2,1)S(1)} %get-tuple-element.26.inv_ref, ...), custom_call_target="tpu_custom_call" | custom-call | bytes 4194304 | tf_op jit(solution)/shard_map/early/pallas_call | solution.py:423
  40.2 0.2 collective-permute-done.11.halo_ref
  40.4 0.1 copy-done
  40.4 3.2 %last.1 = (f32[128,768]{1,0:T(8,128)}, f32[6,16,768]{2,1,0:T(8,128)}, f32[32,8,128]{2,1,0:T(8,128)S(1)}) custom-call(s32[4,16]{1,0:T(4,128)S(4)} %get-tuple-element.24.near_ref, s32[1]{0:T(128)S(6)} %copy.13.count_ref, s32[1,16]{1,0:T(1,128)S(4)} %get-tuple-element.39.late_ref, f32[16,8,768]{2,1,0:T(8,128)S(1)} %get-tuple-element.25.rhs_ref, ...), custom_call_target="tpu_custom_call" | custom-call | tf_op jit(solution)/shard_map/last/pallas_call | solution.py:433
  43.7 19.3 %all_to_all.5.parcel_ref = f32[32,8,128]{2,1,0:T(8,128)S(1)} all-to-all(f32[32,8,128]{2,1,0:T(8,128)S(1)} %get-tuple-element.44), channel_id=1, replica_groups=mesh['region'=32,'sub'=8] {'region'}, dimensions={0} | all-to-all | bytes 262144 | tf_op jit(solution)/shard_map/all_to_all | solution.py:460
  63.0 1.2 %owner.1 = f32[6,1024]{1,0:T(8,128)} custom-call(f32[32,8,128]{2,1,0:T(8,128)S(1)} %all_to_all.5.parcel_ref), custom_call_target="tpu_custom_call" | custom-call | tf_op jit(solution)/shard_map/owner/pallas_call | solution.py:461
  (11 shorter events, 0.0 us)
Async XLA Ops:
  3.1 12.7 %collective-permute-start = (f32[6,48,128]{2,1,0:T(8,128)S(1)}, f32[6,48,128]{2,1,0:T(8,128)S(1)}, u32[]{:S(2)}, u32[]{:S(2)}) collective-permute-start(f32[6,48,128]{2,1,0:T(8,128)S(1)} %get-tuple-element.32), channel_id=1, source_target_pairs={{8,16},{16,8},{24,32},{32,24},{40,48},{48,40},{56,64},{64,56},{72,... | collective-permute-start | bytes 442376 | tf_op jit(solution)/shard_map/ppermute | solution.py:331
  3.8 12.0 %collective-permute-start.1 = (f32[6,48,128]{2,1,0:T(8,128)S(1)}, f32[6,48,128]{2,1,0:T(8,128)S(1)}, u32[]{:S(2)}, u32[]{:S(2)}) collective-permute-start(f32[6,48,128]{2,1,0:T(8,128)S(1)} %get-tuple-element.32), channel_id=1, source_target_pairs={{0,8},{8,0},{16,24},{24,16},{32,40},{40,32},{48,56},{56,48},{64,72... | collective-permute-start | bytes 442376 | tf_op jit(solution)/shard_map/ppermute | solution.py:331
  8.5 7.3 %collective-permute-start.2 = (f32[6,48,128]{2,1,0:T(8,128)S(1)}, f32[6,48,128]{2,1,0:T(8,128)S(1)}, u32[]{:S(2)}, u32[]{:S(2)}) collective-permute-start(f32[6,48,128]{2,1,0:T(8,128)S(1)} %get-tuple-element.32), channel_id=1, source_target_pairs={{1,2},{2,1},{3,4},{4,3},{5,6},{6,5},{9,10},{10,9},{11,12},{12,11},... | collective-permute-start | bytes 442376 | tf_op jit(solution)/shard_map/ppermute | solution.py:331
  12.8 3.1 %collective-permute-start.3 = (f32[6,48,128]{2,1,0:T(8,128)S(1)}, f32[6,48,128]{2,1,0:T(8,128)S(1)}, u32[]{:S(2)}, u32[]{:S(2)}) collective-permute-start(f32[6,48,128]{2,1,0:T(8,128)S(1)} %get-tuple-element.32), channel_id=1, source_target_pairs={{0,1},{1,0},{2,3},{3,2},{4,5},{5,4},{6,7},{7,6},{8,9},{9,8},{10,11... | collective-permute-start | bytes 442376 | tf_op jit(solution)/shard_map/ppermute | solution.py:331
  16.7 9.4 %collective-permute-start.4 = (f32[6,48,128]{2,1,0:T(8,128)S(1)}, f32[6,48,128]{2,1,0:T(8,128)S(1)}, u32[]{:S(2)}, u32[]{:S(2)}) collective-permute-start(f32[6,48,128]{2,1,0:T(8,128)S(1)} %get-tuple-element.35), channel_id=1, source_target_pairs={{8,16},{16,8},{24,32},{32,24},{40,48},{48,40},{56,64},{64,56},{72,... | collective-permute-start | bytes 442376 | tf_op jit(solution)/shard_map/ppermute | solution.py:331
  17.4 8.8 %collective-permute-start.5 = (f32[6,48,128]{2,1,0:T(8,128)S(1)}, f32[6,48,128]{2,1,0:T(8,128)S(1)}, u32[]{:S(2)}, u32[]{:S(2)}) collective-permute-start(f32[6,48,128]{2,1,0:T(8,128)S(1)} %get-tuple-element.35), channel_id=1, source_target_pairs={{0,8},{8,0},{16,24},{24,16},{32,40},{40,32},{48,56},{56,48},{64,72... | collective-permute-start | bytes 442376 | tf_op jit(solution)/shard_map/ppermute | solution.py:331
  21.0 6.9 %collective-permute-start.6 = (f32[6,48,128]{2,1,0:T(8,128)S(1)}, f32[6,48,128]{2,1,0:T(8,128)S(1)}, u32[]{:S(2)}, u32[]{:S(2)}) collective-permute-start(f32[6,48,128]{2,1,0:T(8,128)S(1)} %get-tuple-element.35), channel_id=1, source_target_pairs={{1,2},{2,1},{3,4},{4,3},{5,6},{6,5},{9,10},{10,9},{11,12},{12,11},... | collective-permute-start | bytes 442376 | tf_op jit(solution)/shard_map/ppermute | solution.py:331
  25.1 2.8 %collective-permute-start.7 = (f32[6,48,128]{2,1,0:T(8,128)S(1)}, f32[6,48,128]{2,1,0:T(8,128)S(1)}, u32[]{:S(2)}, u32[]{:S(2)}) collective-permute-start(f32[6,48,128]{2,1,0:T(8,128)S(1)} %get-tuple-element.35), channel_id=1, source_target_pairs={{0,1},{1,0},{2,3},{3,2},{4,5},{5,4},{6,7},{7,6},{8,9},{9,8},{10,11... | collective-permute-start | bytes 442376 | tf_op jit(solution)/shard_map/ppermute | solution.py:331
  26.1 11.4 %copy-start.1 = (s32[1024,1]{0,1:T(1,128)S(1)}, s32[1024,1]{0,1:T(1,128)}, u32[]{:S(2)}) copy-start(s32[1024,1]{0,1:T(1,128)} %param.18) | copy-start | bytes 12292
  28.8 10.5 %collective-permute-start.10 = (f32[6,48,128]{2,1,0:T(8,128)S(1)}, f32[6,48,128]{2,1,0:T(8,128)S(1)}, u32[]{:S(2)}, u32[]{:S(2)}) collective-permute-start(f32[6,48,128]{2,1,0:T(8,128)S(1)} %get-tuple-element.38), channel_id=1, source_target_pairs={{8,16},{16,8},{24,32},{32,24},{40,48},{48,40},{56,64},{64,56},{72,... | collective-permute-start | bytes 442376 | tf_op jit(solution)/shard_map/ppermute | solution.py:331
  29.4 9.9 %collective-permute-start.8 = (f32[6,48,128]{2,1,0:T(8,128)S(1)}, f32[6,48,128]{2,1,0:T(8,128)S(1)}, u32[]{:S(2)}, u32[]{:S(2)}) collective-permute-start(f32[6,48,128]{2,1,0:T(8,128)S(1)} %get-tuple-element.38), channel_id=1, source_target_pairs={{0,8},{8,0},{16,24},{24,16},{32,40},{40,32},{48,56},{56,48},{64,72... | collective-permute-start | bytes 442376 | tf_op jit(solution)/shard_map/ppermute | solution.py:331
  33.3 6.0 %collective-permute-start.9 = (f32[6,48,128]{2,1,0:T(8,128)S(1)}, f32[6,48,128]{2,1,0:T(8,128)S(1)}, u32[]{:S(2)}, u32[]{:S(2)}) collective-permute-start(f32[6,48,128]{2,1,0:T(8,128)S(1)} %get-tuple-element.38), channel_id=1, source_target_pairs={{0,1},{1,0},{2,3},{3,2},{4,5},{5,4},{6,7},{7,6},{8,9},{9,8},{10,11... | collective-permute-start | bytes 442376 | tf_op jit(solution)/shard_map/ppermute | solution.py:331
  33.4 7.0 %collective-permute-start.11 = (f32[6,48,128]{2,1,0:T(8,128)S(1)}, f32[6,48,128]{2,1,0:T(8,128)S(1)}, u32[]{:S(2)}, u32[]{:S(2)}) collective-permute-start(f32[6,48,128]{2,1,0:T(8,128)S(1)} %get-tuple-element.38), channel_id=1, source_target_pairs={{1,2},{2,1},{3,4},{4,3},{5,6},{6,5},{9,10},{10,9},{11,12},{12,11},... | collective-permute-start | bytes 442376 | tf_op jit(solution)/shard_map/ppermute | solution.py:331
  39.3 1.2 %copy-start = (bf16[16,6,6,768]{3,0,2,1:T(8,128)(2,1)S(1)}, bf16[16,6,6,768]{3,0,2,1:T(8,128)(2,1)}, u32[]{:S(2)}) copy-start(bf16[16,6,6,768]{3,0,2,1:T(8,128)(2,1)} %param.16) | copy-start | bytes 2654212
  39.3 1.2 %copy-start.2 = (s32[1024]{0:T(1024)S(1)}, s32[1024]{0:T(1024)}, u32[]{:S(2)}) copy-start(s32[1024]{0:T(1024)} %param.17) | copy-start | bytes 12292
  39.3 1.2 %copy-start.3 = (s32[1024]{0:T(1024)S(1)}, s32[1024]{0:T(1024)}, u32[]{:S(2)}) copy-start(s32[1024]{0:T(1024)} %param.19) | copy-start | bytes 12292
